TPU v7x, 32 devices: a whole 2x2x4 slice. The times are simulated.
32 devices in a mesh: seq: 8 (over y, x, core), fsdp: 4 (over z).
Axes of the slice: x: 2, y: 2, z: 4, core: 2. Of those that a mesh axis runs over, the one named last changes fastest.
Arguments:
- normed_block_input: bfloat16 [4, 1024, 8192], P('fsdp', 'seq'), may hold values from -6 to 6
- stored_rotated_queries: bfloat16 [4, 1024, 4096], P('fsdp', 'seq'), may hold values from -640 to 640
- stored_rotated_keys: bfloat16 [4, 1024, 512], P('fsdp', 'seq'), may hold values from -4 to 4
- attention_output_gradient: bfloat16 [4, 1024, 4096], P('fsdp', 'seq'), may hold values from -6 to 6
- frozen_value_weight: bfloat16 [8192, 512], P('fsdp'), may hold values from -0.0625 to 0.0625
- adapter_down_weight: bfloat16 [16, 8192], replicated, may hold values from -0.0625 to 0.0625
- adapter_up_weight: bfloat16 [16, 512], replicated, may hold values from -1.5 to 1.5
- packed_document_lengths: int32 [4, 8], P('fsdp'), may hold values from 1 to 256, 1024 in all within a row
Outputs:
- input_gradient: bfloat16 [4, 1024, 8192], P('fsdp', 'seq')
- rotated_query_gradient: bfloat16 [4, 1024, 4096], P('fsdp', 'seq')
- rotated_key_gradient: bfloat16 [4, 1024, 512], P('fsdp', 'seq')
- adapter_down_gradient: float32 [16, 8192], replicated
- adapter_up_gradient: float32 [16, 512], replicated
Inputs may be any that keep to these rules, and one draw needn't show every extreme that they name: `packed_document_lengths`: row g holds, in order, the lengths of the 8 documents packed into sequence g; they sum to 1024, and in every row the longest has exactly 256 tokens.
All inputs are finite; a program needn't handle non-finite values.
Results may differ from a plain program's by a relative error of at most 0.0065.
Values may be sent and summed in bfloat16 or wider, within the bound.
No kernel may reach another device: no remote copies, remote signals or barrier semaphores. Data moves between devices by JAX's collectives and lax.ppermute only.
A program may use at most 128 MiB of HBM per device.

v0:
```python
import jax
import jax.numpy as jnp
from jax import lax
from jax.sharding import PartitionSpec as P

HEAD_FEATURES = 128
QUERY_HEADS = 32
KEY_VALUE_HEADS = 4


ADAPTER_SCALE = 2.0
NEG_FILL = -1e30


def contract_trailing(left_rows, right_rows):
    return lax.dot_general(
        left_rows, right_rows, (((1,), (1,)), ((), ())), preferred_element_type=jnp.float32
    )


def body(
    normed_block_input,
    stored_rotated_queries,
    stored_rotated_keys,
    attention_output_gradient,
    frozen_value_weight,
    adapter_down_weight,
    adapter_up_weight,
    packed_document_lengths,
):
    token_rows = normed_block_input.shape[1]
    model_features = normed_block_input.shape[2]
    hidden_activations = normed_block_input.reshape(token_rows, model_features)
    seq_count = lax.axis_size("seq")
    fsdp_count = lax.axis_size("fsdp")
    queries_per_group = QUERY_HEADS // KEY_VALUE_HEADS
    key_value_features = KEY_VALUE_HEADS * HEAD_FEATURES
    inverse = HEAD_FEATURES ** (-0.5)
    adapter_projection = contract_trailing(hidden_activations, adapter_down_weight)
    up_widened = adapter_up_weight.astype(jnp.float32)
    adapter_maps = ADAPTER_SCALE * jnp.dot(
        adapter_projection, up_widened, precision=lax.Precision.HIGHEST
    )
    base_value = jnp.dot(
        hidden_activations,
        lax.all_gather(frozen_value_weight, "fsdp", axis=0, tiled=True),
        preferred_element_type=jnp.float32,
    )
    adapter_values = (base_value + adapter_maps).astype(jnp.bfloat16)
    shaped = (token_rows, QUERY_HEADS, HEAD_FEATURES)
    key_broadcast = jnp.repeat(
        stored_rotated_keys.reshape(token_rows, KEY_VALUE_HEADS, HEAD_FEATURES),
        queries_per_group,
        axis=1,
    )
    value_broadcast = jnp.repeat(
        adapter_values.reshape(token_rows, KEY_VALUE_HEADS, HEAD_FEATURES),
        queries_per_group,
        axis=1,
    )
    head_query, head_key, head_value, head_grad = (
        lax.all_to_all(
            stored_rotated_queries.reshape(shaped), "seq", split_axis=1, concat_axis=0, tiled=True
        ),
        lax.all_to_all(key_broadcast, "seq", split_axis=1, concat_axis=0, tiled=True),
        lax.all_to_all(value_broadcast, "seq", split_axis=1, concat_axis=0, tiled=True),
        lax.all_to_all(
            attention_output_gradient.reshape(shaped),
            "seq",
            split_axis=1,
            concat_axis=0,
            tiled=True,
        ),
    )
    seq_len = head_query.shape[0]
    local_heads = head_query.shape[1]
    block_rows = min(512, seq_len)
    key_reach = block_rows + seq_len // 4
    bounds = jnp.cumsum(packed_document_lengths[0])
    places = jnp.arange(seq_len, dtype=jnp.int32)
    segments = jnp.sum((places[:, None] >= bounds[None, :]).astype(jnp.int32), axis=1)
    grad_keys = jnp.zeros((seq_len, local_heads, HEAD_FEATURES), jnp.float32)
    grad_values = jnp.zeros((seq_len, local_heads, HEAD_FEATURES), jnp.float32)
    query_parts = []
    for block_index in range(seq_len // block_rows):
        first_row = block_index * block_rows
        finish = first_row + block_rows
        opening = max(0, finish - key_reach)
        query_block = head_query[first_row:finish]
        grad_block = head_grad[first_row:finish]
        key_block = head_key[opening:finish]
        value_block = head_value[opening:finish]
        scores = (
            jnp.einsum("qhd,khd->hqk", query_block, key_block, preferred_element_type=jnp.float32)
            * inverse
        )
        allowed = (places[opening:finish][None, :] <= places[first_row:finish][:, None]) & (
            segments[opening:finish][None, :] == segments[first_row:finish][:, None]
        )
        scores = jnp.where(allowed[None], scores, NEG_FILL)
        row_peak = jnp.max(scores, axis=2, keepdims=True)
        weights = jnp.exp(scores - row_peak)
        probs_full = weights / jnp.sum(weights, axis=2, keepdims=True)
        probs_low = probs_full.astype(jnp.bfloat16)
        grad_probs = jnp.einsum(
            "qhd,khd->hqk", grad_block, value_block, preferred_element_type=jnp.float32
        )
        row_delta = jnp.sum(probs_full * grad_probs, axis=2, keepdims=True)
        grad_scores = (probs_full * (grad_probs - row_delta)).astype(jnp.bfloat16)
        query_parts.append(
            jnp.einsum("hqk,khd->qhd", grad_scores, key_block, preferred_element_type=jnp.float32)
            * inverse
        )
        key_part = (
            jnp.einsum("hqk,qhd->khd", grad_scores, query_block, preferred_element_type=jnp.float32)
            * inverse
        )
        value_part = jnp.einsum(
            "hqk,qhd->khd", probs_low, grad_block, preferred_element_type=jnp.float32
        )
        grad_keys = lax.dynamic_update_slice_in_dim(
            grad_keys, grad_keys[opening:finish] + key_part, opening, 0
        )
        grad_values = lax.dynamic_update_slice_in_dim(
            grad_values, grad_values[opening:finish] + value_part, opening, 0
        )
    grad_queries = jnp.concatenate(query_parts, axis=0).astype(jnp.bfloat16)
    token_query = lax.all_to_all(grad_queries, "seq", split_axis=0, concat_axis=1, tiled=True)
    rotated_query_gradient = token_query.reshape(1, token_rows, QUERY_HEADS * HEAD_FEATURES)
    token_key_matrix, token_value_matrix = (
        lax.all_to_all(grad_keys, "seq", split_axis=0, concat_axis=1, tiled=True),
        lax.all_to_all(grad_values, "seq", split_axis=0, concat_axis=1, tiled=True),
    )
    per_key_value_head = token_key_matrix.shape[1] // KEY_VALUE_HEADS
    rotated_key_gradient = (
        token_key_matrix.reshape(token_rows, KEY_VALUE_HEADS, per_key_value_head, HEAD_FEATURES)
        .sum(axis=2)
        .reshape(1, token_rows, key_value_features)
        .astype(jnp.bfloat16)
    )
    value_gradient_matrix = (
        token_value_matrix.reshape(token_rows, KEY_VALUE_HEADS, per_key_value_head, HEAD_FEATURES)
        .sum(axis=2)
        .reshape(token_rows, key_value_features)
    )
    value_grad_low = value_gradient_matrix.astype(jnp.bfloat16)
    adapter_rank_gradient = ADAPTER_SCALE * lax.dot_general(
        value_gradient_matrix, up_widened, (((1,), (1,)), ((), ())), precision=lax.Precision.HIGHEST
    )
    reduced_rank_gradient = adapter_rank_gradient.astype(jnp.bfloat16)
    frozen_path_gradient = contract_trailing(
        value_grad_low, lax.all_gather(frozen_value_weight, "fsdp", axis=0, tiled=True)
    )
    input_gradient = (
        frozen_path_gradient
        + jnp.dot(reduced_rank_gradient, adapter_down_weight, preferred_element_type=jnp.float32)
    ).astype(jnp.bfloat16)
    overall_token_count = token_rows * seq_count * fsdp_count
    down_shard = (
        lax.dot_general(
            reduced_rank_gradient,
            hidden_activations,
            (((0,), (0,)), ((), ())),
            preferred_element_type=jnp.float32,
        )
        / overall_token_count
    )
    up_shard = (
        ADAPTER_SCALE
        * jnp.dot(adapter_projection.T, value_gradient_matrix, precision=lax.Precision.HIGHEST)
        / overall_token_count
    )
    adapter_down_gradient, adapter_up_gradient = lax.psum((down_shard, up_shard), ("seq", "fsdp"))
    return (
        input_gradient.reshape(1, token_rows, model_features),
        rotated_query_gradient,
        rotated_key_gradient,
        adapter_down_gradient,
        adapter_up_gradient,
    )


def solution(mesh):
    placed = (
        P("fsdp", "seq", None),
        P("fsdp", "seq", None),
        P("fsdp", "seq", None),
        P("fsdp", "seq", None),
        P("fsdp", None),
        P(),
        P(),
        P("fsdp", None),
    )
    return jax.shard_map(
        body,
        mesh=mesh,
        in_specs=placed,
        out_specs=(
            P("fsdp", "seq", None),
            P("fsdp", "seq", None),
            P("fsdp", "seq", None),
            P(),
            P(),
        ),
        check_vma=False,
    )
```

profile of v0, /device:TPU:0, one launch (start us, length us, event | category | flops | bytes accessed | tf_op | source)
XLA Modules:
  0.0 388.2 jit_solution(11490689839362450961)
XLA Ops:
  10.9 5.2 %all-to-all-start.1 = ((bf16[128,32,128]{2,0,1:T(8,128)(2,1)}), bf16[128,32,128]{2,0,1:T(8,128)(2,1)S(1)}, u32[]{:S(2)}, u32[]{:S(2)}) async-start(bf16[128,32,128]{2,0,1:T(8,128)(2,1)} %bitcast.136), calls=%async_computation.1 | async-start | bytes 2097152 | tf_op jit(solution)/shard_map/all_to_all | solution.py:65
  18.4 13.1 %all-to-all-done.1 = bf16[128,32,128]{2,0,1:T(8,128)(2,1)S(1)} async-done(((bf16[128,32,128]{2,0,1:T(8,128)(2,1)}), bf16[128,32,128]{2,0,1:T(8,128)(2,1)S(1)}, u32[]{:S(2)}, u32[]{:S(2)}) %all-to-all-start.1) | async-done | bytes 1048608 | tf_op jit(solution)/shard_map/all_to_all | solution.py:65
  31.5 4.3 %all-to-all-start = ((bf16[128,32,128]{0,2,1:T(8,128)(2,1)}), bf16[128,32,128]{0,2,1:T(8,128)(2,1)}, u32[]{:S(2)}, u32[]{:S(2)}) async-start(bf16[128,32,128]{0,2,1:T(8,128)(2,1)} %bitcast.134), calls=%async_computation | async-start | bytes 2097152 | tf_op jit(solution)/shard_map/all_to_all | solution.py:62
  38.4 12.8 %all-to-all-done = bf16[128,32,128]{0,2,1:T(8,128)(2,1)} async-done(((bf16[128,32,128]{0,2,1:T(8,128)(2,1)}), bf16[128,32,128]{0,2,1:T(8,128)(2,1)}, u32[]{:S(2)}, u32[]{:S(2)}) %all-to-all-start) | async-done | bytes 1048608 | tf_op jit(solution)/shard_map/all_to_all | solution.py:62
  51.2 4.2 %all-to-all-start.2 = ((bf16[128,32,128]{0,2,1:T(8,128)(2,1)}), bf16[128,32,128]{0,2,1:T(8,128)(2,1)}, u32[]{:S(2)}, u32[]{:S(2)}) async-start(bf16[128,32,128]{0,2,1:T(8,128)(2,1)} %bitcast.133), calls=%async_computation.2 | async-start | bytes 2097152 | tf_op jit(solution)/shard_map/all_to_all | solution.py:67
  63.6 7.3 %all-to-all-done.2 = bf16[128,32,128]{0,2,1:T(8,128)(2,1)} async-done(((bf16[128,32,128]{0,2,1:T(8,128)(2,1)}), bf16[128,32,128]{0,2,1:T(8,128)(2,1)}, u32[]{:S(2)}, u32[]{:S(2)}) %all-to-all-start.2) | async-done | bytes 1048608 | tf_op jit(solution)/shard_map/all_to_all | solution.py:67
  74.3 4.8 %fusion.56 = (f32[4,512]{1,0:T(4,128)S(1)}, f32[4,512,512]{1,2,0:T(8,128)}) fusion(pred[512,512]{0,1:T(8,128)(4,1)S(1)} %copy-done.14, bf16[512,4,128]{2,0,1:T(8,128)(2,1)} %bitcast.139, bf16[512,4,128]{2,0,1:T(8,128)(2,1)} %bitcast.141), kind=kOutput, calls=%fused_computation.76 | convolution fusion | flops 272630272 | bytes 5513216 | tf_op jit(solution)/shard_map/sub | solution.py:102
  79.2 3.1 fusion.31
  83.8 6.1 %fusion.57 = (f32[4,512]{1,0:T(4,128)S(1)}, f32[4,512,768]{2,1,0:T(8,128)}) fusion(pred[512,768]{1,0:T(8,128)(4,1)} %compare_and_fusion, bf16[512,4,128]{2,0,1:T(8,128)(2,1)S(1)} %bitcast.145, bf16[768,4,128]{2,0,1:T(8,128)(2,1)S(1)} %bitcast.147), kind=kOutput, calls=%fused_computation.77 | convolution fusion | flops 408945408 | bytes 8003584 | tf_op jit(solution)/shard_map/sub | solution.py:102
  89.9 72.9 %all-gather.2.cloned.1.call-done = bf16[8192,512]{1,0:T(8,128)(2,1)} async-done(((bf16[2048,512]{1,0:T(8,128)(2,1)}), bf16[8192,512]{1,0:T(8,128)(2,1)}) %all-gather.2.cloned.1.call-update) | async-done | bytes 8388624 | tf_op jit(solution)/shard_map/all_gather | solution.py:152
  162.8 4.6 %fusion.20 = f32[128,512]{1,0:T(8,128)S(1)} fusion(bf16[8192,512]{1,0:T(8,128)(2,1)} %all-gather.2.cloned.1.call-done, bf16[1,128,8192]{2,1,0:T(8,128)(2,1)S(1)} %copy-done), kind=kOutput, calls=%fused_computation.31 | convolution fusion | flops 1073741824 | bytes 10747904 | tf_op jit(solution)/shard_map/dot_general | solution.py:44
  169.0 3.7 all-to-all-start.4
  172.7 6.0 %fusion.28 = f32[1024,4,128]{2,0,1:T(8,128)} fusion(f32[1024,4,128]{2,0,1:T(8,128)} %dynamic_update_slice.12, bf16[512,4,128]{2,0,1:T(8,128)(2,1)} %bitcast.151, f32[4,512,768]{2,1,0:T(8,128)} %get-tuple-element.19, f32[4,512]{1,0:T(4,128)S(1)} %get-tuple-element.18), kind=kOutput, calls=%fused_computation.42 | convolution fusion | flops 406192128 | bytes 9969664 | tf_op jit(solution)/shard_map/hqk,qhd->khd/dot_general | solution.py:118
  178.7 4.3 %copy.108 = f32[1024,4,128]{2,1,0:T(4,128)} copy(f32[1024,4,128]{2,0,1:T(8,128)} %fusion.28) | data formatting | bytes 4194304 | tf_op jit(solution)/shard_map/dynamic_update_slice | solution.py:124
  183.0 5.1 %all-to-all-done.4 = bf16[128,32,128]{2,0,1:T(8,128)(2,1)S(1)} async-done(((bf16[128,32,128]{2,0,1:T(8,128)(2,1)}), bf16[128,32,128]{2,0,1:T(8,128)(2,1)S(1)}, u32[]{:S(2)}, u32[]{:S(2)}) %all-to-all-start.4) | async-done | bytes 1048608 | tf_op jit(solution)/shard_map/all_to_all | solution.py:66
  188.1 4.3 %all-to-all-start.3 = ((f32[1024,4,128]{2,1,0:T(4,128)}), f32[1024,4,128]{2,1,0:T(4,128)}, u32[]{:S(2)}, u32[]{:S(2)}) async-start(f32[1024,4,128]{2,1,0:T(4,128)} %copy.108), calls=%async_computation.3 | async-start | bytes 4194304 | tf_op jit(solution)/shard_map/all_to_all | solution.py:132
  205.2 13.9 %all-to-all-done.3 = f32[1024,4,128]{2,1,0:T(4,128)} async-done(((f32[1024,4,128]{2,1,0:T(4,128)}), f32[1024,4,128]{2,1,0:T(4,128)}, u32[]{:S(2)}, u32[]{:S(2)}) %all-to-all-start.3) | async-done | bytes 2097184 | tf_op jit(solution)/shard_map/all_to_all | solution.py:132
  219.1 3.8 all-to-all-start.5
  230.1 7.9 %all-to-all-done.5 = bf16[1024,4,128]{2,1,0:T(4,128)(2,1)S(1)} async-done(((bf16[1024,4,128]{2,1,0:T(4,128)(2,1)}), bf16[1024,4,128]{2,1,0:T(4,128)(2,1)S(1)}, u32[]{:S(2)}, u32[]{:S(2)}) %all-to-all-start.5) | async-done | bytes 1048608 | tf_op jit(solution)/shard_map/all_to_all | solution.py:128
  238.0 4.4 %all-to-all-start.6 = ((f32[1024,4,128]{2,1,0:T(4,128)}), f32[1024,4,128]{2,1,0:T(4,128)}, u32[]{:S(2)}, u32[]{:S(2)}) async-start(f32[1024,4,128]{2,1,0:T(4,128)} %copy.118), calls=%async_computation.6 | async-start | bytes 4194304 | tf_op jit(solution)/shard_map/all_to_all | solution.py:131
  242.4 3.6 reduce_sum.88
  250.7 51.1 %psum.15 = f32[16,512]{1,0:T(8,128)} all-reduce(f32[16,512]{1,0:T(8,128)S(1)} %convolution_multiply_fusion.5), channel_id=1, replica_groups=mesh['seq'=8,'fsdp'=4] {'seq','fsdp'}, use_global_device_ids=true, to_apply=%region_13.14 | all-reduce | flops 8192 | bytes 65536 | tf_op jit(solution)/shard_map/psum | solution.py:173
  301.7 6.3 %fusion.47 = f32[128,8192]{1,0:T(8,128)S(1)} fusion(bf16[8192,512]{1,0:T(8,128)(2,1)} %all-gather.2.cloned.1.call-done, f32[128,512]{0,1:T(8,128)S(1)} %bitcast.131), kind=kOutput, calls=%fused_computation.65 | convolution fusion | flops 1073807360 | bytes 12845056 | tf_op jit(solution)/shard_map/dot_general | solution.py:16
  317.8 61.1 %all-reduce.4.cloned.1.call-done = f32[16,8192]{1,0:T(8,128)} async-done(((f32[16,8192]{1,0:T(8,128)}), f32[16,8192]{1,0:T(8,128)}) %all-reduce.4.cloned.1.call-update) | async-done | bytes 524304 | tf_op jit(solution)/shard_map/psum | solution.py:173
  (106 shorter events, 58.4 us)
Async XLA Ops:
  8.0 49.6 %copy-start = (bf16[1,128,8192]{2,1,0:T(8,128)(2,1)S(1)}, bf16[1,128,8192]{2,1,0:T(8,128)(2,1)}, u32[]{:S(2)}) copy-start(bf16[1,128,8192]{2,1,0:T(8,128)(2,1)} %param.8) | copy-start | bytes 6291460
  8.0 154.8 %all-gather.2.cloned.1.call-start = ((), (), s32[]{:S(2)}) async-start(), calls=%async_computation.7 | async-start | bytes 10485760 | tf_op jit(solution)/shard_map/all_gather | solution.py:152
  8.7 27.1 %copy-start.16 = (s32[1,8]{1,0:T(1,128)S(1)}, s32[1,8]{1,0:T(1,128)}, u32[]{:S(2)}) copy-start(s32[1,8]{1,0:T(1,128)} %param.15) | copy-start | bytes 100
  10.9 20.6 %all-to-all-start.1 = ((bf16[128,32,128]{2,0,1:T(8,128)(2,1)}), bf16[128,32,128]{2,0,1:T(8,128)(2,1)S(1)}, u32[]{:S(2)}, u32[]{:S(2)}) async-start(bf16[128,32,128]{2,0,1:T(8,128)(2,1)} %bitcast.136), calls=%async_computation.1 | async-start | bytes 2097152 | tf_op jit(solution)/shard_map/all_to_all | solution.py:65
  16.1 41.5 %copy-start.8 = (bf16[16,8192]{1,0:T(8,128)(2,1)S(1)}, bf16[16,8192]{1,0:T(8,128)(2,1)}, u32[]{:S(2)}) copy-start(bf16[16,8192]{1,0:T(8,128)(2,1)} %param.13) | copy-start | bytes 786436
  31.5 19.7 %all-to-all-start = ((bf16[128,32,128]{0,2,1:T(8,128)(2,1)}), bf16[128,32,128]{0,2,1:T(8,128)(2,1)}, u32[]{:S(2)}, u32[]{:S(2)}) async-start(bf16[128,32,128]{0,2,1:T(8,128)(2,1)} %bitcast.134), calls=%async_computation | async-start | bytes 2097152 | tf_op jit(solution)/shard_map/all_to_all | solution.py:62
  51.2 19.7 %all-to-all-start.2 = ((bf16[128,32,128]{0,2,1:T(8,128)(2,1)}), bf16[128,32,128]{0,2,1:T(8,128)(2,1)}, u32[]{:S(2)}, u32[]{:S(2)}) async-start(bf16[128,32,128]{0,2,1:T(8,128)(2,1)} %bitcast.133), calls=%async_computation.2 | async-start | bytes 2097152 | tf_op jit(solution)/shard_map/all_to_all | solution.py:67
  61.9 12.4 %copy-start.14 = (pred[512,512]{0,1:T(8,128)(4,1)S(1)}, pred[512,512]{0,1:T(8,128)(4,1)}, u32[]{:S(2)}) copy-start(pred[512,512]{0,1:T(8,128)(4,1)} %compare_and_fusion.1) | copy-start | bytes 786436
  79.2 4.6 %copy-start.6 = (bf16[4,128,4,128]{3,1,0,2:T(8,128)(2,1)S(1)}, bf16[4,128,4,128]{3,1,0,2:T(8,128)(2,1)}, u32[]{:S(2)}) copy-start(bf16[4,128,4,128]{3,1,0,2:T(8,128)(2,1)} %copy.104) | copy-start | bytes 1572868
  79.2 4.6 %copy-start.10 = (bf16[6,128,4,128]{3,1,0,2:T(8,128)(2,1)S(1)}, bf16[6,128,4,128]{3,1,0,2:T(8,128)(2,1)}, u32[]{:S(2)}) copy-start(bf16[6,128,4,128]{3,1,0,2:T(8,128)(2,1)} %copy.105) | copy-start | bytes 2359300
  89.9 77.5 %copy-start.15 = (bf16[16,512]{1,0:T(8,128)(2,1)S(1)}, bf16[16,512]{1,0:T(8,128)(2,1)}, u32[]{:S(2)}) copy-start(bf16[16,512]{1,0:T(8,128)(2,1)} %param.14) | copy-start | bytes 49156
  169.0 19.1 %all-to-all-start.4 = ((bf16[128,32,128]{2,0,1:T(8,128)(2,1)}), bf16[128,32,128]{2,0,1:T(8,128)(2,1)S(1)}, u32[]{:S(2)}, u32[]{:S(2)}) async-start(bf16[128,32,128]{2,0,1:T(8,128)(2,1)} %bitcast.135), calls=%async_computation.4 | async-start | bytes 2097152 | tf_op jit(solution)/shard_map/all_to_all | solution.py:66
  188.1 31.0 %all-to-all-start.3 = ((f32[1024,4,128]{2,1,0:T(4,128)}), f32[1024,4,128]{2,1,0:T(4,128)}, u32[]{:S(2)}, u32[]{:S(2)}) async-start(f32[1024,4,128]{2,1,0:T(4,128)} %copy.108), calls=%async_computation.3 | async-start | bytes 4194304 | tf_op jit(solution)/shard_map/all_to_all | solution.py:132
  192.4 2.2 copy-start.4
  192.4 2.3 copy-start.13
  192.6 3.5 slice-start
  194.7 2.1 slice-start.1
  194.7 2.1 copy-start.12
  219.1 18.9 %all-to-all-start.5 = ((bf16[1024,4,128]{2,1,0:T(4,128)(2,1)}), bf16[1024,4,128]{2,1,0:T(4,128)(2,1)S(1)}, u32[]{:S(2)}, u32[]{:S(2)}) async-start(bf16[1024,4,128]{2,1,0:T(4,128)(2,1)} %copy.115), calls=%async_computation.5 | async-start | bytes 2097152 | tf_op jit(solution)/shard_map/all_to_all | solution.py:128
  222.9 2.7 copy-start.3
  222.9 2.8 copy-start.7
  238.0 76.1 %all-to-all-start.6 = ((f32[1024,4,128]{2,1,0:T(4,128)}), f32[1024,4,128]{2,1,0:T(4,128)}, u32[]{:S(2)}, u32[]{:S(2)}) async-start(f32[1024,4,128]{2,1,0:T(4,128)} %copy.118), calls=%async_computation.6 | async-start | bytes 4194304 | tf_op jit(solution)/shard_map/all_to_all | solution.py:131
  242.4 136.5 %all-reduce.4.cloned.1.call-start = ((), (), s32[]{:S(2)}) async-start(), calls=%async_computation.8 | async-start | bytes 1048576 | tf_op jit(solution)/shard_map/psum | solution.py:173
  301.7 6.3 %copy-start.9 = (bf16[16,8192]{1,0:T(8,128)(2,1)S(1)}, bf16[16,8192]{1,0:T(8,128)(2,1)}, u32[]{:S(2)}) copy-start(bf16[16,8192]{1,0:T(8,128)(2,1)} %param.13) | copy-start | bytes 786436
  (4 other events, 6.2 us)
Sparse Core Ops, SparseCore 0:
  10.4 152.3 all-gather.1
Sparse Core Ops, SparseCore 1:
  250.4 128.4 all-reduce.3
where the time goes:
time: 389 us; the launch traced here: 388 us
  waiting for transfers between devices  195 us (50%)
  blocking collectives  51.1 us (13%)
  matrix products  44 us (11%)
  local copies, waits for them, and re-layouts  39.4 us (10%)
  starting transfers between devices  30 us (8%)
  between operations  16 us (4%)
  other arithmetic  13 us (3%)
    all_gather x1, waiting for transfers between devices, body(): lax.all_gather(frozen_value_weight, 'fsdp', axis=0, tiled=True)  72.9 us
    psum x1, waiting for transfers between devices, body(): lax.psum((down_shard, up_shard), ('seq', 'fsdp'))  61.1 us
    psum x1, blocking collectives, body(): lax.psum((down_shard, up_shard), ('seq', 'fsdp'))  51.1 us
    all_to_all x1, waiting for transfers between devices, body(): lax.all_to_all(grad_values, 'seq', split_axis=0, concat_axis=1, tiled=True)  13.9 us
    all_to_all x1, waiting for transfers between devices, body(): lax.all_to_all(key_broadcast, 'seq', split_axis=1, concat_axis=0, tiled=T...  13.1 us
    all_to_all x1, waiting for transfers between devices, body(): lax.all_to_all(stored_rotated_queries.reshape(shaped), 'seq', split_axis=...  12.8 us
    unnamed x42, local copies, waits for them, and re-layouts  11.6 us
    sub x2, matrix products, body(): weights = jnp.exp(scores - row_peak)  11 us
  transfers between devices with their start and end apart: 9, of which 8 were waited for; matrix products, arithmetic and copies ran while one was open for 22% of the time, Pallas kernels for 0%

commit v1 on v0

v1 whole, which is shorter than its diff:
```python
import math

import jax
import jax.numpy as jnp
import numpy as np
from jax import lax
from jax.experimental import pallas as pl
from jax.experimental.pallas import tpu as pltpu
from jax.sharding import PartitionSpec as P

HEAD_FEATURES = 128
QUERY_HEADS = 32
KEY_VALUE_HEADS = 4
GROUP = QUERY_HEADS // KEY_VALUE_HEADS
ADAPTER_SCALE = 2.0
NEG_FILL = -1e30
INVERSE = HEAD_FEATURES ** (-0.5)
LOG2E = math.log2(math.e)
VMEM_LIMIT = 48 * 1024 * 1024
F32 = jnp.float32
BF16 = jnp.bfloat16


def params():
    return pltpu.CompilerParams(vmem_limit_bytes=VMEM_LIMIT)


def cost(flops, nbytes):
    return pl.CostEstimate(flops=int(flops), bytes_accessed=int(nbytes), transcendentals=0)


def contract_trailing(left, right):
    return lax.dot_general(left, right, (((1,), (1,)), ((), ())), preferred_element_type=F32)


def contract_leading(left, right, precision=None):
    return lax.dot_general(
        left, right, (((0,), (0,)), ((), ())), preferred_element_type=F32, precision=precision
    )


def flip(value, axis, mask):
    size = lax.axis_size(axis)
    choose = mask if callable(mask) else (lambda index: mask)
    return lax.ppermute(value, axis, [(i, i ^ choose(i)) for i in range(size)])


def shift(value, axis, by):
    size = lax.axis_size(axis)
    return lax.ppermute(value, axis, [(i, i + by) for i in range(size) if 0 <= i + by < size])


def turn(value, axis, by):
    size = lax.axis_size(axis)
    return lax.ppermute(value, axis, [(i, (i + by) % size) for i in range(size)])


def pair_rows(ref, index):
    first = ref[:, (2 * index) * HEAD_FEATURES : (2 * index + 1) * HEAD_FEATURES]
    second = ref[:, (2 * index + 1) * HEAD_FEATURES : (2 * index + 2) * HEAD_FEATURES]
    return jnp.concatenate([first, second], axis=0)


def probs_kernel(back, docs, tokens):
    def kernel(info, q_ref, o_ref, *refs):
        key_refs = refs[: back + 1]
        p_ref = refs[back + 1]
        dv_refs = refs[back + 2 : 2 * back + 3]
        bias_ref = refs[2 * back + 3]
        keys = (back + 1) * tokens

        @pl.when(pl.program_id(0) == 0)
        def _():
            here = info[0]
            query_place = here * tokens + lax.broadcasted_iota(jnp.int32, (keys, tokens), 1)
            key_place = (here - back) * tokens + lax.broadcasted_iota(jnp.int32, (keys, tokens), 0)
            opening = jnp.zeros((keys, tokens), jnp.int32)
            bound = jnp.int32(0)
            for doc in range(docs):
                bound = bound + info[1 + doc]
                opening = jnp.where(query_place >= bound, bound, opening)
            allowed = (key_place <= query_place) & (key_place >= opening)
            bias_ref[...] = jnp.where(allowed, 0.0, NEG_FILL)

        key_rows = jnp.concatenate([r[...] for r in key_refs], axis=0)
        total = jnp.zeros((keys, HEAD_FEATURES), F32)
        for pair in range(GROUP // 2):
            scores = contract_trailing(key_rows, pair_rows(q_ref, pair))
            bias = bias_ref[...]
            scores = scores + jnp.concatenate([bias, bias], axis=1)
            peak = jnp.max(scores, axis=0, keepdims=True)
            weights = jnp.exp2((scores - peak) * (INVERSE * LOG2E))
            probs = weights * (1.0 / jnp.sum(weights, axis=0, keepdims=True))
            probs_low = probs.astype(BF16)
            p_ref[0, :, 2 * pair * tokens : 2 * (pair + 1) * tokens] = probs_low
            total = total + jnp.dot(probs_low, pair_rows(o_ref, pair), preferred_element_type=F32)
        for block in range(back + 1):
            rows = total[block * tokens : (block + 1) * tokens]
            dv_refs[block][...] = rows.astype(dv_refs[block].dtype)

    return kernel


def head_blocks(tokens, width):
    return pl.BlockSpec((tokens, width), lambda head, *_: (0, head))


def probs_call(info, q, o, key_blocks):
    back = len(key_blocks) - 1
    tokens = q.shape[0]
    keys = (back + 1) * tokens
    kv = key_blocks[0].shape[1]
    wide = head_blocks(tokens, GROUP * HEAD_FEATURES)
    thin = head_blocks(tokens, HEAD_FEATURES)
    out = pl.pallas_call(
        probs_kernel(back, info.shape[0] - 1, tokens),
        grid_spec=pltpu.PrefetchScalarGridSpec(
            num_scalar_prefetch=1,
            grid=(KEY_VALUE_HEADS,),
            in_specs=[wide, wide] + [thin] * (back + 1),
            out_specs=[pl.BlockSpec((1, keys, GROUP * tokens), lambda head, *_: (head, 0, 0))]
            + [thin] * (back + 1),
            scratch_shapes=[pltpu.VMEM((keys, tokens), F32)],
        ),
        out_shape=[jax.ShapeDtypeStruct((KEY_VALUE_HEADS, keys, GROUP * tokens), BF16)]
        + [jax.ShapeDtypeStruct((tokens, kv), BF16)] * back
        + [jax.ShapeDtypeStruct((tokens, kv), F32)],
        compiler_params=params(),
        cost_estimate=cost(8 * QUERY_HEADS * keys * tokens * HEAD_FEATURES, 8 << 20),
        name="probs",
    )(info, q, o, *key_blocks)
    return out[0], out[1:]


def scores_grad_kernel(back, tokens):
    def kernel(p_ref, q_ref, o_ref, *refs):
        key_refs = refs[: back + 1]
        value_refs = refs[back + 1 : 2 * back + 2]
        dq_ref = refs[2 * back + 2]
        dk_refs = refs[2 * back + 3 :]
        keys = (back + 1) * tokens
        key_rows = jnp.concatenate([r[...] for r in key_refs], axis=0)
        value_rows = jnp.concatenate([r[...] for r in value_refs], axis=0)
        key_columns = key_rows.T
        total = jnp.zeros((keys, HEAD_FEATURES), F32)
        for pair in range(GROUP // 2):
            grad_probs = contract_trailing(value_rows, pair_rows(o_ref, pair))
            probs = p_ref[0, :, 2 * pair * tokens : 2 * (pair + 1) * tokens].astype(F32)
            mass = jnp.sum(probs, axis=0, keepdims=True)
            delta = jnp.sum(probs * grad_probs, axis=0, keepdims=True) / mass
            grad_scores = (probs * (grad_probs - delta)).astype(BF16)
            total = total + jnp.dot(
                grad_scores, pair_rows(q_ref, pair), preferred_element_type=F32
            )
            dq = jnp.dot(key_columns, grad_scores, preferred_element_type=F32) * INVERSE
            dq_ref[:, 2 * pair * HEAD_FEATURES : (2 * pair + 1) * HEAD_FEATURES] = (
                dq[:, :tokens].T.astype(BF16)
            )
            dq_ref[:, (2 * pair + 1) * HEAD_FEATURES : (2 * pair + 2) * HEAD_FEATURES] = (
                dq[:, tokens:].T.astype(BF16)
            )
        for block in range(back + 1):
            rows = total[block * tokens : (block + 1) * tokens] * INVERSE
            dk_refs[block][...] = rows.astype(dk_refs[block].dtype)

    return kernel


def scores_grad_call(probs, q, o, key_blocks, value_blocks):
    back = len(key_blocks) - 1
    tokens = q.shape[0]
    keys = (back + 1) * tokens
    kv = key_blocks[0].shape[1]
    wide = head_blocks(tokens, GROUP * HEAD_FEATURES)
    thin = head_blocks(tokens, HEAD_FEATURES)
    out = pl.pallas_call(
        scores_grad_kernel(back, tokens),
        grid=(KEY_VALUE_HEADS,),
        in_specs=[pl.BlockSpec((1, keys, GROUP * tokens), lambda head: (head, 0, 0)), wide, wide]
        + [thin] * (2 * back + 2),
        out_specs=[wide] + [thin] * (back + 1),
        out_shape=[jax.ShapeDtypeStruct(q.shape, BF16)]
        + [jax.ShapeDtypeStruct((tokens, kv), BF16)] * back
        + [jax.ShapeDtypeStruct((tokens, kv), F32)],
        compiler_params=params(),
        cost_estimate=cost(12 * QUERY_HEADS * keys * tokens * HEAD_FEATURES, 8 << 20),
        name="scores_grad",
    )(probs, q, o, *key_blocks, *value_blocks)
    return out[0], out[1:]


def own_values_kernel(x_ref, own_ref, down_ref, up_ref, w_ref, acc_ref, rank_ref):
    low_rank = contract_trailing(x_ref[...], down_ref[...])
    rank_ref[...] = low_rank
    adapter = jnp.dot(
        low_rank,
        up_ref[...].astype(F32),
        precision=lax.Precision.HIGHEST,
        preferred_element_type=F32,
    )
    acc_ref[...] = ADAPTER_SCALE * adapter + jnp.dot(
        own_ref[...], w_ref[...], preferred_element_type=F32
    )


def own_values_call(place, x, down, up, w):
    tokens, model = x.shape
    rows, kv = w.shape
    rank = down.shape[0]

    def kernel(place_ref, *refs):
        own_values_kernel(*refs)

    def whole(shape):
        return pl.BlockSpec(shape, lambda i, *_: (0, 0))

    return pl.pallas_call(
        kernel,
        grid_spec=pltpu.PrefetchScalarGridSpec(
            num_scalar_prefetch=1,
            grid=(1,),
            in_specs=[
                whole(x.shape),
                pl.BlockSpec((tokens, rows), lambda i, place: (0, place[0])),
                whole(down.shape),
                whole(up.shape),
                whole(w.shape),
            ],
            out_specs=[whole((tokens, kv)), whole((tokens, rank))],
        ),
        out_shape=[
            jax.ShapeDtypeStruct((tokens, kv), F32),
            jax.ShapeDtypeStruct((tokens, rank), F32),
        ],
        compiler_params=params(),
        cost_estimate=cost(2 * tokens * rows * kv * 2, 5 << 20),
        name="own_values",
    )(place, x, x, down, up, w)


def pieces_of(piece_refs, step):
    number = 0
    for ref in piece_refs:
        for j in range(ref.shape[0] // step):
            yield number, ref, j * step
            number += 1


def more_values_call(place, x, acc, pieces, step, last):
    tokens, model = x.shape
    kv = acc.shape[1]
    rows = sum(piece.shape[0] for piece in pieces)

    def kernel(place_ref, x_ref, acc_ref, *refs):
        total = acc_ref[...]
        for number, ref, first in pieces_of(refs[:-1], step):
            column = pl.multiple_of(place_ref[1 + number] * step, step)
            total = total + jnp.dot(
                x_ref[:, pl.ds(column, step)],
                ref[first : first + step, :],
                preferred_element_type=F32,
            )
        refs[-1][...] = total.astype(refs[-1].dtype)

    def whole(shape):
        return pl.BlockSpec(shape, lambda i, *_: (0, 0))

    return pl.pallas_call(
        kernel,
        grid_spec=pltpu.PrefetchScalarGridSpec(
            num_scalar_prefetch=1,
            grid=(1,),
            in_specs=[
                pl.BlockSpec((tokens, rows), lambda i, place: (0, place[0])),
                whole(acc.shape),
            ]
            + [whole(piece.shape) for piece in pieces],
            out_specs=whole(acc.shape),
        ),
        out_shape=jax.ShapeDtypeStruct(acc.shape, BF16 if last else F32),
        compiler_params=params(),
        cost_estimate=cost(2 * tokens * rows * kv, 3 << 20),
        name="more_values",
    )(place, x, acc, *pieces)


def input_grad_call(place, dv_low, rank_grad, down, pieces, step, model, so_far):
    tokens, kv = dv_low.shape
    rows = sum(piece.shape[0] for piece in pieces)
    rank = down.shape[0]
    first_call = so_far is None

    def kernel(place_ref, dv_ref, rank_ref, down_ref, *refs):
        out_ref = refs[-1]
        piece_refs = refs[: len(pieces)]
        for number, ref, first in pieces_of(piece_refs, step):
            column = pl.multiple_of(place_ref[1 + number] * step, step)
            grad = contract_trailing(dv_ref[...], ref[first : first + step, :])
            grad = grad + jnp.dot(
                rank_ref[...], down_ref[:, pl.ds(column, step)], preferred_element_type=F32
            )
            out_ref[:, pl.ds(column, step)] = grad.astype(BF16)

    def whole(shape):
        return pl.BlockSpec(shape, lambda i, *_: (0, 0))

    def shard(height):
        return pl.BlockSpec((height, rows), lambda i, place: (0, place[0]))

    operands = [place, dv_low, rank_grad, down, *pieces]
    in_specs = [whole(dv_low.shape), whole(rank_grad.shape), shard(rank)] + [
        whole(piece.shape) for piece in pieces
    ]
    aliases = {}
    if not first_call:
        aliases = {len(operands): 0}
        operands.append(so_far)
        in_specs.append(pl.BlockSpec(memory_space=pl.ANY))
    return pl.pallas_call(
        kernel,
        grid_spec=pltpu.PrefetchScalarGridSpec(
            num_scalar_prefetch=1, grid=(1,), in_specs=in_specs, out_specs=shard(tokens)
        ),
        out_shape=jax.ShapeDtypeStruct((tokens, model), BF16),
        input_output_aliases=aliases,
        compiler_params=params(),
        cost_estimate=cost(2 * tokens * rows * kv, 3 << 20),
        name="input_grad",
    )(*operands)


def adapter_grad_call(dv_own, dv_back, up, low_rank, x, parts, scale):
    tokens, model = x.shape
    rank, kv = up.shape
    width = (model + kv) // parts
    cut = 512 if model % 512 == 0 else model

    def kernel(own_ref, up_ref, low_ref, x_ref, *refs):
        back_refs = refs[: len(dv_back)]
        dv_ref, rank_ref, out_ref = refs[len(dv_back) :]
        value_grad = own_ref[...]
        for ref in back_refs:
            value_grad = value_grad + ref[...].astype(F32)
        dv_ref[...] = value_grad.astype(BF16)
        rank_grad = ADAPTER_SCALE * lax.dot_general(
            value_grad,
            up_ref[...].astype(F32),
            (((1,), (1,)), ((), ())),
            precision=lax.Precision.HIGHEST,
            preferred_element_type=F32,
        )
        rank_low = rank_grad.astype(BF16)
        rank_ref[...] = rank_low
        down = contract_leading(rank_low, x_ref[...]) * scale
        raised = contract_leading(low_ref[...], value_grad, lax.Precision.HIGHEST)
        both = jnp.concatenate([down, raised * (ADAPTER_SCALE * scale)], axis=1)
        for part in range(parts):
            out_ref[part] = both[:, part * width : (part + 1) * width]

    return pl.pallas_call(
        kernel,
        out_shape=[
            jax.ShapeDtypeStruct((tokens, kv), BF16),
            jax.ShapeDtypeStruct((tokens, rank), BF16),
            jax.ShapeDtypeStruct((parts, rank, width), F32),
        ],
        compiler_params=params(),
        cost_estimate=cost(2 * tokens * rank * model * 16, 4 << 20),
        name="adapter_grad",
    )(dv_own, up, low_rank, x, *dv_back)


def sum_everywhere(grads, here):
    seq_count = lax.axis_size("seq")
    low, high = here & 1, (here >> 1) & 1
    kept = lax.dynamic_slice_in_dim(grads, 2 * low, 2, 0)
    sent = lax.dynamic_slice_in_dim(grads, 2 - 2 * low, 2, 0)
    half = kept + flip(sent, "seq", 1)
    kept = lax.dynamic_slice_in_dim(half, high, 1, 0)
    sent = lax.dynamic_slice_in_dim(half, 1 - high, 1, 0)
    part = kept + flip(sent, "seq", 2)
    bit = 4
    while bit < seq_count:
        part = part + flip(part, "seq", bit)
        bit *= 2
    bit = 1
    while bit < lax.axis_size("fsdp"):
        part = part + flip(part, "fsdp", bit)
        bit *= 2
    other = flip(part, "seq", 2)
    half = jnp.where(
        high == 0, jnp.concatenate([part, other], 0), jnp.concatenate([other, part], 0)
    )
    other = flip(half, "seq", 1)
    return jnp.where(
        low == 0, jnp.concatenate([half, other], 0), jnp.concatenate([other, half], 0)
    )


def gather_order(seq_count):
    held = [[i] for i in range(seq_count)]
    bits = chip_bits(seq_count)
    for step in range(len(bits)):
        held = [held[i] + held[i ^ chip_mask(seq_count, step)(i)] for i in range(seq_count)]
    return np.array([held[i] + held[i ^ 1] for i in range(seq_count)], np.int32)


def chip_bits(seq_count):
    return [1 << b for b in range(1, seq_count.bit_length() - 1)]


def chip_mask(seq_count, step):
    bits = chip_bits(seq_count)
    return lambda index: bits[step] if index % 2 == 0 else bits[len(bits) - 1 - step]


def spread(part):
    seq_count = lax.axis_size("seq")
    held = [part]
    for step in range(len(chip_bits(seq_count))):
        joined = held[0] if len(held) == 1 else jnp.concatenate(held, axis=0)
        held = [joined, flip(joined, "seq", chip_mask(seq_count, step))]
    return held + [flip(block, "seq", 1) for block in held]


def body(
    normed_block_input,
    stored_rotated_queries,
    stored_rotated_keys,
    attention_output_gradient,
    frozen_value_weight,
    adapter_down_weight,
    adapter_up_weight,
    packed_document_lengths,
):
    x = normed_block_input[0]
    q = stored_rotated_queries[0]
    k = stored_rotated_keys[0]
    o = attention_output_gradient[0]
    w = frozen_value_weight
    tokens, model = x.shape
    seq_count = lax.axis_size("seq")
    fsdp_count = lax.axis_size("fsdp")
    here = lax.axis_index("seq")
    shard_number = lax.axis_index("fsdp")
    rows = w.shape[0]
    part_rows = rows // seq_count
    longest = tokens * seq_count // 4
    back = min(-(-(longest - 1) // tokens), seq_count - 1)

    own_part = lax.dynamic_slice_in_dim(w, here * part_rows, part_rows, 0)
    arrived = [turn(own_part, "fsdp", by) for by in range(1, fsdp_count)]
    key_blocks = [shift(k, "seq", by) for by in range(back, 0, -1)] + [k]

    info = jnp.concatenate([here[None], packed_document_lengths[0]]).astype(jnp.int32)
    probs, dv_blocks = probs_call(info, q, o, key_blocks)
    dv_back = [shift(dv_blocks[back - by], "seq", -by) for by in range(1, back + 1)]

    order = jnp.asarray(gather_order(seq_count))[here]
    own_place = jnp.stack([shard_number, jnp.int32(0)])
    acc, low_rank = own_values_call(own_place, x, adapter_down_weight, adapter_up_weight, w)
    dv_low, rank_grad, adapter_grads = adapter_grad_call(
        dv_blocks[back],
        dv_back,
        adapter_up_weight,
        low_rank,
        x,
        4,
        1.0 / (tokens * seq_count * fsdp_count),
    )
    input_gradient = input_grad_call(
        own_place, dv_low, rank_grad, adapter_down_weight, [w], rows, model, None
    )
    for by in range(1, fsdp_count):
        owner = (shard_number - by) % fsdp_count
        pieces = spread(arrived[by - 1])
        if part_rows % 128 == 0:
            step = part_rows
            place = jnp.concatenate([owner[None], order])
        else:
            step = rows
            joined = jnp.concatenate(pieces, axis=0).reshape(seq_count, part_rows, -1)
            pieces = [jnp.take(joined, jnp.argsort(order), axis=0).reshape(rows, -1)]
            place = jnp.stack([owner, jnp.int32(0)])
        acc = more_values_call(place, x, acc, pieces, step, by == fsdp_count - 1)
        input_gradient = input_grad_call(
            place,
            dv_low,
            rank_grad,
            adapter_down_weight,
            pieces,
            step,
            model,
            input_gradient,
        )
    value_blocks = [shift(acc, "seq", by) for by in range(back, 0, -1)] + [acc]
    rotated_query_gradient, dk_blocks = scores_grad_call(probs, q, o, key_blocks, value_blocks)
    key_gradient = dk_blocks[back]
    for by in range(1, back + 1):
        key_gradient = key_gradient + shift(dk_blocks[back - by], "seq", -by).astype(F32)

    adapter_grads = sum_everywhere(adapter_grads, here)
    adapter_grads = adapter_grads.transpose(1, 0, 2).reshape(adapter_down_weight.shape[0], -1)
    return (
        input_gradient[None],
        rotated_query_gradient[None],
        key_gradient.astype(BF16)[None],
        adapter_grads[:, :model],
        adapter_grads[:, model:],
    )


def solution(mesh):
    placed = (
        P("fsdp", "seq", None),
        P("fsdp", "seq", None),
        P("fsdp", "seq", None),
        P("fsdp", "seq", None),
        P("fsdp", None),
        P(),
        P(),
        P("fsdp", None),
    )
    return jax.shard_map(
        body,
        mesh=mesh,
        in_specs=placed,
        out_specs=(
            P("fsdp", "seq", None),
            P("fsdp", "seq", None),
            P("fsdp", "seq", None),
            P(),
            P(),
        ),
        check_vma=False,
    )
```

time: 389 us -> 137 us (0.35)
  the two profiles are of different devices: /device:TPU:0 before, /device:TPU:5 now
where the time goes in v1:
time: 137 us; the launch traced here: 136 us
  starting transfers between devices  55.4 us (40%)
  Pallas kernels  38.6 us (28%)
  local copies, waits for them, and re-layouts  18.9 us (14%)
  waiting for transfers between devices  17.9 us (13%)
  other arithmetic  3.8 us (3%)
    ppermute x19, starting transfers between devices, flip(): return lax.ppermute(value, axis, [(i, i ^ choose(i)) for i in range(size)])  27.8 us
    ppermute x8, starting transfers between devices, shift(): lax.ppermute(value, axis, [(i, i + by) for i in range(size) if 0 <= i + b...  23 us
    ppermute x19, waiting for transfers between devices, flip(): return lax.ppermute(value, axis, [(i, i ^ choose(i)) for i in range(size)])  17.5 us
    unnamed x61, local copies, waits for them, and re-layouts  15 us
    pallas_call x4, Pallas kernels, input_grad_call(): pl.pallas_call(kernel, grid_spec=pltpu.PrefetchScalarGridSpec(num_scalar_...  13.1 us
    pallas_call x1, Pallas kernels, scores_grad_call(): pl.pallas_call(scores_grad_kernel(back, tokens), grid=(KEY_VALUE_HEADS,),...  8.71 us
    pallas_call x3, Pallas kernels, more_values_call(): pl.pallas_call(kernel, grid_spec=pltpu.PrefetchScalarGridSpec(num_scalar_...  7.64 us
    pallas_call x1, Pallas kernels, probs_call(): pl.pallas_call(probs_kernel(back, info.shape[0] - 1, tokens), grid_spec=p...  5.22 us
  transfers between devices with their start and end apart: 30, of which 5 were waited for; matrix products, arithmetic and copies ran while one was open for 7% of the time, Pallas kernels for 28%

profile of v1, /device:TPU:5, one launch (start us, length us, event | category | flops | bytes accessed | tf_op | source)
XLA Modules:
  0.0 135.8 jit_solution(11812311707741715540)
XLA Ops:
  0.6 3.7 %collective-permute-start.1 = (bf16[128,512]{1,0:T(8,128)(2,1)}, bf16[128,512]{1,0:T(8,128)(2,1)S(1)}, u32[]{:S(2)}, u32[]{:S(2)}) collective-permute-start(bf16[128,512]{1,0:T(8,128)(2,1)} %bitcast.30), channel_id=1, source_target_pairs={{0,4},{4,8},{8,12},{12,16},{16,20},{20,24},{24,28},{1,5},{5,9},{9,... | collective-permute-start | bytes 393224 | tf_op jit(solution)/shard_map/ppermute | solution.py:50
  9.2 2.3 %collective-permute-start.9 = (bf16[256,512]{1,0:T(8,128)(2,1)}, bf16[256,512]{1,0:T(8,128)(2,1)}, u32[]{:S(2)}, u32[]{:S(2)}) collective-permute-start(bf16[256,512]{1,0:T(8,128)(2,1)} %constant_dynamic-slice_fusion.2), channel_id=1, source_target_pairs={{0,2},{1,3},{2,0},{3,1},{4,6},{5,7},{6,4},{7,5},{8,10},{9,11},{10,... | collective-permute-start | bytes 786440 | tf_op jit(solution)/shard_map/ppermute | solution.py:55
  16.8 5.2 %probs.1 = (bf16[4,384,1024]{2,1,0:T(8,128)(2,1)S(1)}, bf16[128,512]{1,0:T(8,128)(2,1)S(1)}, bf16[128,512]{1,0:T(8,128)(2,1)S(1)}, f32[128,512]{1,0:T(8,128)S(1)}) custom-call(s32[9]{0:T(128)S(1)} %pad_add_fusion.1.info, bf16[128,4096]{1,0:T(8,128)(2,1)S(1)} %bitcast.26, bf16[128,4096]{1,0:T(8,128)(2,1)S(1)} %bitcast.28, ...), custom_call_target="tpu_custom_call" | custom-call | flops 1610612736 | bytes 8388608 | tf_op jit(solution)/shard_map/probs/pallas_call | solution.py:115
  23.7 3.1 %collective-permute-start.2 = (bf16[128,512]{1,0:T(8,128)(2,1)S(1)}, bf16[128,512]{1,0:T(8,128)(2,1)S(1)}, u32[]{:S(2)}, u32[]{:S(2)}) collective-permute-start(bf16[128,512]{1,0:T(8,128)(2,1)S(1)} %get-tuple-element.20), channel_id=1, source_target_pairs={{4,0},{8,4},{12,8},{16,12},{20,16},{24,20},{28,24},{5,1},{9,5},{13... | collective-permute-start | bytes 393224 | tf_op jit(solution)/shard_map/ppermute | solution.py:50
  26.8 3.1 %collective-permute-start.3 = (bf16[128,512]{1,0:T(8,128)(2,1)S(1)}, bf16[128,512]{1,0:T(8,128)(2,1)S(1)}, u32[]{:S(2)}, u32[]{:S(2)}) collective-permute-start(bf16[128,512]{1,0:T(8,128)(2,1)S(1)} %get-tuple-element.21), channel_id=1, source_target_pairs={{8,0},{12,4},{16,8},{20,12},{24,16},{28,20},{9,1},{13,5},{17,9},{2... | collective-permute-start | bytes 393224 | tf_op jit(solution)/shard_map/ppermute | solution.py:50
  30.0 2.7 %own_values.1 = (f32[128,512]{1,0:T(8,128)S(1)}, f32[128,16]{1,0:T(8,128)S(1)}) custom-call(s32[2]{0:T(128)S(1)} %pad_add_fusion.2.place_ref, bf16[128,8192]{1,0:T(8,128)(2,1)S(1)} %bitcast.20, bf16[128,8192]{1,0:T(8,128)(2,1)S(1)} %bitcast.21, bf16[16,8192]{1,0:T(8,128)(2,1)S(1)} %copy-done.3, bf16[16,512]{1,0:T(8,128)(2,1)S(1)} %copy-done.15, ...), custom_call_target="tpu_custom_call" | custom-call | flops 536870912 | bytes 5242880 | tf_op jit(solution)/shard_map/own_values/pallas_call | solution.py:217
  34.0 2.5 %collective-permute-start.23 = (f32[2,16,2176]{2,1,0:T(8,128)S(1)}, f32[2,16,2176]{2,1,0:T(8,128)S(1)}, u32[]{:S(2)}, u32[]{:S(2)}) collective-permute-start(f32[2,16,2176]{2,1,0:T(8,128)S(1)} %constant_dynamic-slice_fusion.1), channel_id=1, source_target_pairs={{0,4},{4,0},{8,12},{12,8},{16,20},{20,16},{24,28},{28,24},{1,5},{5... | collective-permute-start | bytes 835592 | tf_op jit(solution)/shard_map/ppermute | solution.py:45
  44.9 4.3 %collective-permute-done.10 = bf16[256,512]{1,0:T(8,128)(2,1)S(1)} collective-permute-done((bf16[256,512]{1,0:T(8,128)(2,1)}, bf16[256,512]{1,0:T(8,128)(2,1)S(1)}, u32[]{:S(2)}, u32[]{:S(2)}) %collective-permute-start.10) | collective-permute-done | bytes 262176 | tf_op jit(solution)/shard_map/ppermute | solution.py:45
  50.9 6.2 %collective-permute-done.24 = f32[1,16,2176]{2,1,0:T(8,128)S(1)} collective-permute-done((f32[1,16,2176]{2,1,0:T(8,128)S(1)}, f32[1,16,2176]{2,1,0:T(8,128)S(1)}, u32[]{:S(2)}, u32[]{:S(2)}) %collective-permute-start.24) | collective-permute-done | bytes 139296 | tf_op jit(solution)/shard_map/ppermute | solution.py:45
  57.3 5.8 %collective-permute-done.25 = f32[1,16,2176]{2,1,0:T(8,128)S(1)} collective-permute-done((f32[1,16,2176]{2,1,0:T(8,128)S(1)}, f32[1,16,2176]{2,1,0:T(8,128)S(1)}, u32[]{:S(2)}, u32[]{:S(2)}) %collective-permute-start.25) | collective-permute-done | bytes 139296 | tf_op jit(solution)/shard_map/ppermute | solution.py:45
  63.6 6.2 %collective-permute-start.18 = (bf16[512,512]{1,0:T(8,128)(2,1)}, bf16[512,512]{1,0:T(8,128)(2,1)}, u32[]{:S(2)}, u32[]{:S(2)}) collective-permute-start(bf16[512,512]{1,0:T(8,128)(2,1)} %collective-permute-done.16.refs_1_), channel_id=1, source_target_pairs={{0,4},{4,0},{8,12},{12,8},{16,20},{20,16},{24,28},{28,24},{1,5},{5... | collective-permute-start | bytes 1572872 | tf_op jit(solution)/shard_map/ppermute | solution.py:45
  70.9 5.2 %collective-permute-start.12 = (bf16[512,512]{1,0:T(8,128)(2,1)S(1)}, bf16[512,512]{1,0:T(8,128)(2,1)}, u32[]{:S(2)}, u32[]{:S(2)}) collective-permute-start(bf16[512,512]{1,0:T(8,128)(2,1)S(1)} %constant_dynamic-update-slice_fusion.2.refs_0_), channel_id=1, source_target_pairs={{0,4},{4,0},{8,12},{12,8},{16,20},{20,16},{24,28},{28,24},{1,5},{5... | collective-permute-start | bytes 1572872 | tf_op jit(solution)/shard_map/ppermute | solution.py:45
  77.3 6.0 %collective-permute-start.8 = (bf16[512,512]{1,0:T(8,128)(2,1)}, bf16[512,512]{1,0:T(8,128)(2,1)}, u32[]{:S(2)}, u32[]{:S(2)}) collective-permute-start(bf16[512,512]{1,0:T(8,128)(2,1)} %collective-permute-done.6.refs_1_), channel_id=1, source_target_pairs={{0,4},{4,0},{8,12},{12,8},{16,20},{20,16},{24,28},{28,24},{1,5},{5... | collective-permute-start | bytes 1572872 | tf_op jit(solution)/shard_map/ppermute | solution.py:45
  88.2 2.2 %more_values.3.acc_ref = f32[128,512]{1,0:T(8,128)S(1)} custom-call(s32[9]{0:T(128)S(1)} %get-tuple-element.31.place_ref, bf16[128,8192]{1,0:T(8,128)(2,1)S(1)} %bitcast.23, f32[128,512]{1,0:T(8,128)S(1)} %copy-done.14, bf16[512,512]{1,0:T(8,128)(2,1)S(1)} %copy-done.5, bf16[512,512]{1,0:T(8,128)(2,1)} %collective-permute-done.16.refs_1_, ...), custom_call_target="tpu_custom_call" | custom-call | flops 268435456 | bytes 3145728 | tf_op jit(solution)/shard_map/more_values/pallas_call | solution.py:268
  90.5 2.4 %more_values.4.acc_ref = f32[128,512]{1,0:T(8,128)S(1)} custom-call(s32[9]{0:T(128)S(1)} %get-tuple-element.32.place_ref, bf16[128,8192]{1,0:T(8,128)(2,1)S(1)} %bitcast.24, f32[128,512]{1,0:T(8,128)S(1)} %more_values.3.acc_ref, bf16[512,512]{1,0:T(8,128)(2,1)S(1)} %constant_dynamic-update-slice_fusion.2.refs_0_, ...), custom_call_target="tpu_custom_call" | custom-call | flops 268435456 | bytes 3145728 | tf_op jit(solution)/shard_map/more_values/pallas_call | solution.py:268
  92.9 3.0 %more_values.5.refs_5_ = bf16[128,512]{1,0:T(8,128)(2,1)} custom-call(s32[9]{0:T(128)S(1)} %get-tuple-element.33.place_ref, bf16[128,8192]{1,0:T(8,128)(2,1)S(1)} %bitcast.25, f32[128,512]{1,0:T(8,128)S(1)} %more_values.4.acc_ref, bf16[512,512]{1,0:T(8,128)(2,1)S(1)} %constant_dynamic-update-slice_fusion.refs_0_, ...), custom_call_target="tpu_custom_call" | custom-call | flops 268435456 | bytes 3145728 | tf_op jit(solution)/shard_map/more_values/pallas_call | solution.py:268
  95.9 3.4 %collective-permute-start.20 = (bf16[128,512]{1,0:T(8,128)(2,1)}, bf16[128,512]{1,0:T(8,128)(2,1)S(1)}, u32[]{:S(2)}, u32[]{:S(2)}) collective-permute-start(bf16[128,512]{1,0:T(8,128)(2,1)} %more_values.5.refs_5_), channel_id=1, source_target_pairs={{0,4},{4,8},{8,12},{12,16},{16,20},{20,24},{24,28},{1,5},{5,9},{9,... | collective-permute-start | bytes 393224 | tf_op jit(solution)/shard_map/ppermute | solution.py:50
  104.4 2.3 %input_grad.4.refs_4_ = bf16[128,8192]{1,0:T(8,128)(2,1)} custom-call(s32[2]{0:T(128)S(1)} %pad_add_fusion.2.place_ref, bf16[128,512]{1,0:T(8,128)(2,1)S(1)} %get-tuple-element.22.dv_ref, bf16[128,16]{1,0:T(8,128)(2,1)S(1)} %copy-done.11, bf16[16,8192]{1,0:T(8,128)(2,1)S(1)} %copy-done.3, bf16[2048,512]{1,0:T(8,128)(2,1)S(1)} %copy-done.2), custom_call_target="tpu_custom_call" | custom-call | flops 268435456 | bytes 3145728 | tf_op jit(solution)/shard_map/input_grad/pallas_call | solution.py:319
  107.0 8.7 %scores_grad.1 = (bf16[128,4096]{1,0:T(8,128)(2,1)}, bf16[128,512]{1,0:T(8,128)(2,1)S(1)}, bf16[128,512]{1,0:T(8,128)(2,1)S(1)}, f32[128,512]{1,0:T(8,128)S(1)}) custom-call(bf16[4,384,1024]{2,1,0:T(8,128)(2,1)} %copy-done.26, bf16[128,4096]{1,0:T(8,128)(2,1)S(1)} %bitcast.27, bf16[128,4096]{1,0:T(8,128)(2,1)S(1)} %bitcast.29, ...), custom_call_target="tpu_custom_call" | custom-call | flops 2415919104 | bytes 8388608 | tf_op jit(solution)/shard_map/scores_grad/pallas_call | solution.py:176
  115.8 2.2 %collective-permute-start.21 = (bf16[128,512]{1,0:T(8,128)(2,1)S(1)}, bf16[128,512]{1,0:T(8,128)(2,1)S(1)}, u32[]{:S(2)}, u32[]{:S(2)}) collective-permute-start(bf16[128,512]{1,0:T(8,128)(2,1)S(1)} %get-tuple-element.28), channel_id=1, source_target_pairs={{4,0},{8,4},{12,8},{16,12},{20,16},{24,20},{28,24},{5,1},{9,5},{13... | collective-permute-start | bytes 393224 | tf_op jit(solution)/shard_map/ppermute | solution.py:50
  118.0 3.6 %collective-permute-start.22 = (bf16[128,512]{1,0:T(8,128)(2,1)S(1)}, bf16[128,512]{1,0:T(8,128)(2,1)S(1)}, u32[]{:S(2)}, u32[]{:S(2)}) collective-permute-start(bf16[128,512]{1,0:T(8,128)(2,1)S(1)} %get-tuple-element.29), channel_id=1, source_target_pairs={{8,0},{12,4},{16,8},{20,12},{24,16},{28,20},{9,1},{13,5},{17,9},{2... | collective-permute-start | bytes 393224 | tf_op jit(solution)/shard_map/ppermute | solution.py:50
  124.2 3.5 %input_grad.5.refs_4_ = bf16[128,8192]{1,0:T(8,128)(2,1)} custom-call(s32[9]{0:T(128)S(1)} %get-tuple-element.31.place_ref, bf16[128,512]{1,0:T(8,128)(2,1)S(1)} %get-tuple-element.22.dv_ref, bf16[128,16]{1,0:T(8,128)(2,1)S(1)} %copy-done.12, bf16[16,8192]{1,0:T(8,128)(2,1)S(1)} %copy-done.3, ...), custom_call_target="tpu_custom_call", output_to_operand_aliasing={{}: (8, {})} | custom-call | flops 268435456 | bytes 3145728 | tf_op jit(solution)/shard_map/input_grad/pallas_call | solution.py:319
  127.8 3.7 %input_grad.6.refs_4_ = bf16[128,8192]{1,0:T(8,128)(2,1)} custom-call(s32[9]{0:T(128)S(1)} %get-tuple-element.32.place_ref, bf16[128,512]{1,0:T(8,128)(2,1)S(1)} %get-tuple-element.22.dv_ref, bf16[128,16]{1,0:T(8,128)(2,1)S(1)} %copy-done.12, bf16[16,8192]{1,0:T(8,128)(2,1)S(1)} %copy-done.3, ...), custom_call_target="tpu_custom_call", output_to_operand_aliasing={{}: (8, {})} | custom-call | flops 268435456 | bytes 3145728 | tf_op jit(solution)/shard_map/input_grad/pallas_call | solution.py:319
  131.4 3.7 %input_grad.7 = bf16[128,8192]{1,0:T(8,128)(2,1)} custom-call(s32[9]{0:T(128)S(1)} %get-tuple-element.33.place_ref, bf16[128,512]{1,0:T(8,128)(2,1)S(1)} %get-tuple-element.22.dv_ref, bf16[128,16]{1,0:T(8,128)(2,1)S(1)} %copy-done.12, bf16[16,8192]{1,0:T(8,128)(2,1)S(1)} %copy-done.3, ...), custom_call_target="tpu_custom_call", output_to_operand_aliasing={{}: (8, {})} | custom-call | flops 268435456 | bytes 3145728 | tf_op jit(solution)/shard_map/input_grad/pallas_call | solution.py:319
  (129 shorter events, 39.5 us)
Async XLA Ops:
  0.6 12.7 %collective-permute-start.1 = (bf16[128,512]{1,0:T(8,128)(2,1)}, bf16[128,512]{1,0:T(8,128)(2,1)S(1)}, u32[]{:S(2)}, u32[]{:S(2)}) collective-permute-start(bf16[128,512]{1,0:T(8,128)(2,1)} %bitcast.30), channel_id=1, source_target_pairs={{0,4},{4,8},{8,12},{12,16},{16,20},{20,24},{24,28},{1,5},{5,9},{9,... | collective-permute-start | bytes 393224 | tf_op jit(solution)/shard_map/ppermute | solution.py:50
  4.3 9.0 %collective-permute-start = (bf16[128,512]{1,0:T(8,128)(2,1)}, bf16[128,512]{1,0:T(8,128)(2,1)S(1)}, u32[]{:S(2)}, u32[]{:S(2)}) collective-permute-start(bf16[128,512]{1,0:T(8,128)(2,1)} %bitcast.31), channel_id=1, source_target_pairs={{0,8},{4,12},{8,16},{12,20},{16,24},{20,28},{1,9},{5,13},{9,17},{1... | collective-permute-start | bytes 393224 | tf_op jit(solution)/shard_map/ppermute | solution.py:50
  7.9 28.6 %collective-permute-start.14 = (bf16[256,512]{1,0:T(8,128)(2,1)}, bf16[256,512]{1,0:T(8,128)(2,1)}, u32[]{:S(2)}, u32[]{:S(2)}) collective-permute-start(bf16[256,512]{1,0:T(8,128)(2,1)} %constant_dynamic-slice_fusion.2), channel_id=1, source_target_pairs={{0,1},{1,2},{2,3},{3,0},{4,5},{5,6},{6,7},{7,4},{8,9},{9,10},{10,1... | collective-permute-start | bytes 786440 | tf_op jit(solution)/shard_map/ppermute | solution.py:55
  9.2 29.8 %collective-permute-start.9 = (bf16[256,512]{1,0:T(8,128)(2,1)}, bf16[256,512]{1,0:T(8,128)(2,1)}, u32[]{:S(2)}, u32[]{:S(2)}) collective-permute-start(bf16[256,512]{1,0:T(8,128)(2,1)} %constant_dynamic-slice_fusion.2), channel_id=1, source_target_pairs={{0,2},{1,3},{2,0},{3,1},{4,6},{5,7},{6,4},{7,5},{8,10},{9,11},{10,... | collective-permute-start | bytes 786440 | tf_op jit(solution)/shard_map/ppermute | solution.py:55
  11.5 25.0 %collective-permute-start.4 = (bf16[256,512]{1,0:T(8,128)(2,1)}, bf16[256,512]{1,0:T(8,128)(2,1)}, u32[]{:S(2)}, u32[]{:S(2)}) collective-permute-start(bf16[256,512]{1,0:T(8,128)(2,1)} %constant_dynamic-slice_fusion.2), channel_id=1, source_target_pairs={{0,3},{1,0},{2,1},{3,2},{4,7},{5,4},{6,5},{7,6},{8,11},{9,8},{10,9... | collective-permute-start | bytes 786440 | tf_op jit(solution)/shard_map/ppermute | solution.py:55
  23.7 9.0 %collective-permute-start.2 = (bf16[128,512]{1,0:T(8,128)(2,1)S(1)}, bf16[128,512]{1,0:T(8,128)(2,1)S(1)}, u32[]{:S(2)}, u32[]{:S(2)}) collective-permute-start(bf16[128,512]{1,0:T(8,128)(2,1)S(1)} %get-tuple-element.20), channel_id=1, source_target_pairs={{4,0},{8,4},{12,8},{16,12},{20,16},{24,20},{28,24},{5,1},{9,5},{13... | collective-permute-start | bytes 393224 | tf_op jit(solution)/shard_map/ppermute | solution.py:50
  34.0 9.6 %collective-permute-start.23 = (f32[2,16,2176]{2,1,0:T(8,128)S(1)}, f32[2,16,2176]{2,1,0:T(8,128)S(1)}, u32[]{:S(2)}, u32[]{:S(2)}) collective-permute-start(f32[2,16,2176]{2,1,0:T(8,128)S(1)} %constant_dynamic-slice_fusion.1), channel_id=1, source_target_pairs={{0,4},{4,0},{8,12},{12,8},{16,20},{20,16},{24,28},{28,24},{1,5},{5... | collective-permute-start | bytes 835592 | tf_op jit(solution)/shard_map/ppermute | solution.py:45
  36.6 13.2 %collective-permute-start.5 = (bf16[256,512]{1,0:T(8,128)(2,1)}, bf16[256,512]{1,0:T(8,128)(2,1)S(1)}, u32[]{:S(2)}, u32[]{:S(2)}) collective-permute-start(bf16[256,512]{1,0:T(8,128)(2,1)} %collective-permute-done.4), channel_id=1, source_target_pairs={{0,8},{4,20},{8,0},{12,28},{16,24},{20,4},{24,16},{28,12},{1,9},{5... | collective-permute-start | bytes 786440 | tf_op jit(solution)/shard_map/ppermute | solution.py:45
  39.0 10.2 %collective-permute-start.10 = (bf16[256,512]{1,0:T(8,128)(2,1)}, bf16[256,512]{1,0:T(8,128)(2,1)S(1)}, u32[]{:S(2)}, u32[]{:S(2)}) collective-permute-start(bf16[256,512]{1,0:T(8,128)(2,1)} %collective-permute-done.9), channel_id=1, source_target_pairs={{0,8},{4,20},{8,0},{12,28},{16,24},{20,4},{24,16},{28,12},{1,9},{5... | collective-permute-start | bytes 786440 | tf_op jit(solution)/shard_map/ppermute | solution.py:45
  42.3 27.7 %collective-permute-start.17 = (bf16[512,512]{1,0:T(8,128)(2,1)S(1)}, bf16[512,512]{1,0:T(8,128)(2,1)S(1)}, u32[]{:S(2)}, u32[]{:S(2)}) collective-permute-start(bf16[512,512]{1,0:T(8,128)(2,1)S(1)} %constant_dynamic-update-slice_fusion.4.refs_0_), channel_id=1, source_target_pairs={{0,4},{4,0},{8,12},{12,8},{16,20},{20,16},{24,28},{28,24},{1,5},{5... | collective-permute-start | bytes 1572872 | tf_op jit(solution)/shard_map/ppermute | solution.py:45
  43.3 20.3 %collective-permute-start.16 = (bf16[512,512]{1,0:T(8,128)(2,1)S(1)}, bf16[512,512]{1,0:T(8,128)(2,1)}, u32[]{:S(2)}, u32[]{:S(2)}) collective-permute-start(bf16[512,512]{1,0:T(8,128)(2,1)S(1)} %constant_dynamic-update-slice_fusion.4.refs_0_), channel_id=1, source_target_pairs={{0,16},{4,12},{8,24},{12,4},{16,0},{20,28},{24,8},{28,20},{1,17},{... | collective-permute-start | bytes 1572872 | tf_op jit(solution)/shard_map/ppermute | solution.py:45
  43.7 13.5 %collective-permute-start.24 = (f32[1,16,2176]{2,1,0:T(8,128)S(1)}, f32[1,16,2176]{2,1,0:T(8,128)S(1)}, u32[]{:S(2)}, u32[]{:S(2)}) collective-permute-start(f32[1,16,2176]{2,1,0:T(8,128)S(1)} %constant_dynamic-slice_fusion), channel_id=1, source_target_pairs={{0,8},{4,12},{8,0},{12,4},{16,24},{20,28},{24,16},{28,20},{1,9},{5... | collective-permute-start | bytes 417800 | tf_op jit(solution)/shard_map/ppermute | solution.py:45
  49.3 26.8 %collective-permute-start.11 = (bf16[512,512]{1,0:T(8,128)(2,1)S(1)}, bf16[512,512]{1,0:T(8,128)(2,1)}, u32[]{:S(2)}, u32[]{:S(2)}) collective-permute-start(bf16[512,512]{1,0:T(8,128)(2,1)S(1)} %constant_dynamic-update-slice_fusion.2.refs_0_), channel_id=1, source_target_pairs={{0,16},{4,12},{8,24},{12,4},{16,0},{20,28},{24,8},{28,20},{1,17},{... | collective-permute-start | bytes 1572872 | tf_op jit(solution)/shard_map/ppermute | solution.py:45
  49.8 26.3 %collective-permute-start.6 = (bf16[512,512]{1,0:T(8,128)(2,1)S(1)}, bf16[512,512]{1,0:T(8,128)(2,1)}, u32[]{:S(2)}, u32[]{:S(2)}) collective-permute-start(bf16[512,512]{1,0:T(8,128)(2,1)S(1)} %constant_dynamic-update-slice_fusion.refs_0_), channel_id=1, source_target_pairs={{0,16},{4,12},{8,24},{12,4},{16,0},{20,28},{24,8},{28,20},{1,17},{... | collective-permute-start | bytes 1572872 | tf_op jit(solution)/shard_map/ppermute | solution.py:45
  63.6 21.4 %collective-permute-start.18 = (bf16[512,512]{1,0:T(8,128)(2,1)}, bf16[512,512]{1,0:T(8,128)(2,1)}, u32[]{:S(2)}, u32[]{:S(2)}) collective-permute-start(bf16[512,512]{1,0:T(8,128)(2,1)} %collective-permute-done.16.refs_1_), channel_id=1, source_target_pairs={{0,4},{4,0},{8,12},{12,8},{16,20},{20,16},{24,28},{28,24},{1,5},{5... | collective-permute-start | bytes 1572872 | tf_op jit(solution)/shard_map/ppermute | solution.py:45
  70.9 19.6 %collective-permute-start.12 = (bf16[512,512]{1,0:T(8,128)(2,1)S(1)}, bf16[512,512]{1,0:T(8,128)(2,1)}, u32[]{:S(2)}, u32[]{:S(2)}) collective-permute-start(bf16[512,512]{1,0:T(8,128)(2,1)S(1)} %constant_dynamic-update-slice_fusion.2.refs_0_), channel_id=1, source_target_pairs={{0,4},{4,0},{8,12},{12,8},{16,20},{20,16},{24,28},{28,24},{1,5},{5... | collective-permute-start | bytes 1572872 | tf_op jit(solution)/shard_map/ppermute | solution.py:45
  76.1 14.4 %collective-permute-start.13 = (bf16[512,512]{1,0:T(8,128)(2,1)}, bf16[512,512]{1,0:T(8,128)(2,1)}, u32[]{:S(2)}, u32[]{:S(2)}) collective-permute-start(bf16[512,512]{1,0:T(8,128)(2,1)} %collective-permute-done.11.refs_1_), channel_id=1, source_target_pairs={{0,4},{4,0},{8,12},{12,8},{16,20},{20,16},{24,28},{28,24},{1,5},{5... | collective-permute-start | bytes 1572872 | tf_op jit(solution)/shard_map/ppermute | solution.py:45
  76.1 16.8 %collective-permute-start.7 = (bf16[512,512]{1,0:T(8,128)(2,1)S(1)}, bf16[512,512]{1,0:T(8,128)(2,1)}, u32[]{:S(2)}, u32[]{:S(2)}) collective-permute-start(bf16[512,512]{1,0:T(8,128)(2,1)S(1)} %constant_dynamic-update-slice_fusion.refs_0_), channel_id=1, source_target_pairs={{0,4},{4,0},{8,12},{12,8},{16,20},{20,16},{24,28},{28,24},{1,5},{5... | collective-permute-start | bytes 1572872 | tf_op jit(solution)/shard_map/ppermute | solution.py:45
  77.3 15.6 %collective-permute-start.8 = (bf16[512,512]{1,0:T(8,128)(2,1)}, bf16[512,512]{1,0:T(8,128)(2,1)}, u32[]{:S(2)}, u32[]{:S(2)}) collective-permute-start(bf16[512,512]{1,0:T(8,128)(2,1)} %collective-permute-done.6.refs_1_), channel_id=1, source_target_pairs={{0,4},{4,0},{8,12},{12,8},{16,20},{20,16},{24,28},{28,24},{1,5},{5... | collective-permute-start | bytes 1572872 | tf_op jit(solution)/shard_map/ppermute | solution.py:45
  85.0 16.3 %collective-permute-start.28 = (f32[1,16,2176]{2,1,0:T(8,128)S(1)}, f32[1,16,2176]{2,1,0:T(8,128)S(1)}, u32[]{:S(2)}, u32[]{:S(2)}) collective-permute-start(f32[1,16,2176]{2,1,0:T(8,128)S(1)} %add.69), channel_id=1, source_target_pairs={{0,8},{4,12},{8,0},{12,4},{16,24},{20,28},{24,16},{28,20},{1,9},{5... | collective-permute-start | bytes 417800 | tf_op jit(solution)/shard_map/ppermute | solution.py:45
  95.9 10.8 %collective-permute-start.20 = (bf16[128,512]{1,0:T(8,128)(2,1)}, bf16[128,512]{1,0:T(8,128)(2,1)S(1)}, u32[]{:S(2)}, u32[]{:S(2)}) collective-permute-start(bf16[128,512]{1,0:T(8,128)(2,1)} %more_values.5.refs_5_), channel_id=1, source_target_pairs={{0,4},{4,8},{8,12},{12,16},{16,20},{20,24},{24,28},{1,5},{5,9},{9,... | collective-permute-start | bytes 393224 | tf_op jit(solution)/shard_map/ppermute | solution.py:50
  101.3 20.3 %collective-permute-start.29 = (f32[2,16,2176]{2,1,0:T(8,128)S(1)}, f32[2,16,2176]{2,1,0:T(8,128)}, u32[]{:S(2)}, u32[]{:S(2)}) collective-permute-start(f32[2,16,2176]{2,1,0:T(8,128)S(1)} %maximum_select_fusion.1), channel_id=1, source_target_pairs={{0,4},{4,0},{8,12},{12,8},{16,20},{20,16},{24,28},{28,24},{1,5},{5... | collective-permute-start | bytes 835592 | tf_op jit(solution)/shard_map/ppermute | solution.py:45
  115.8 19.3 %collective-permute-start.21 = (bf16[128,512]{1,0:T(8,128)(2,1)S(1)}, bf16[128,512]{1,0:T(8,128)(2,1)S(1)}, u32[]{:S(2)}, u32[]{:S(2)}) collective-permute-start(bf16[128,512]{1,0:T(8,128)(2,1)S(1)} %get-tuple-element.28), channel_id=1, source_target_pairs={{4,0},{8,4},{12,8},{16,12},{20,16},{24,20},{28,24},{5,1},{9,5},{13... | collective-permute-start | bytes 393224 | tf_op jit(solution)/shard_map/ppermute | solution.py:50
  118.0 17.1 %collective-permute-start.22 = (bf16[128,512]{1,0:T(8,128)(2,1)S(1)}, bf16[128,512]{1,0:T(8,128)(2,1)S(1)}, u32[]{:S(2)}, u32[]{:S(2)}) collective-permute-start(bf16[128,512]{1,0:T(8,128)(2,1)S(1)} %get-tuple-element.29), channel_id=1, source_target_pairs={{8,0},{12,4},{16,8},{20,12},{24,16},{28,20},{9,1},{13,5},{17,9},{2... | collective-permute-start | bytes 393224 | tf_op jit(solution)/shard_map/ppermute | solution.py:50
  (35 other events, 209.9 us)

commit v2 on v0

v2 whole, which is shorter than its diff:
```python
import math

import jax
import jax.numpy as jnp
import numpy as np
from jax import lax
from jax.experimental import pallas as pl
from jax.experimental.pallas import tpu as pltpu
from jax.sharding import PartitionSpec as P

HEAD_FEATURES = 128
QUERY_HEADS = 32
KEY_VALUE_HEADS = 4
GROUP = QUERY_HEADS // KEY_VALUE_HEADS
ADAPTER_SCALE = 2.0
NEG_FILL = -1e30
INVERSE = HEAD_FEATURES ** (-0.5)
LOG2E = math.log2(math.e)
VMEM_LIMIT = 32 * 1024 * 1024
SMALL = pl.CostEstimate(flops=1, bytes_accessed=1, transcendentals=0)
F32 = jnp.float32
BF16 = jnp.bfloat16


def params():
    return pltpu.CompilerParams(vmem_limit_bytes=VMEM_LIMIT)


def contract_trailing(left, right):
    return lax.dot_general(left, right, (((1,), (1,)), ((), ())), preferred_element_type=F32)


def contract_leading(left, right, precision=None):
    return lax.dot_general(
        left, right, (((0,), (0,)), ((), ())), preferred_element_type=F32, precision=precision
    )


def flip(value, axis, mask, name="exchange"):
    size = lax.axis_size(axis)
    choose = mask if callable(mask) else (lambda index: mask)
    with jax.named_scope(name):
        return lax.ppermute(value, axis, [(i, i ^ choose(i)) for i in range(size)])


def shift(value, axis, by, name="halo"):
    size = lax.axis_size(axis)
    with jax.named_scope(name):
        return lax.ppermute(value, axis, [(i, i + by) for i in range(size) if 0 <= i + by < size])


def turn(value, axis, by, name="weight_ring"):
    size = lax.axis_size(axis)
    with jax.named_scope(name):
        return lax.ppermute(value, axis, [(i, (i + by) % size) for i in range(size)])


def after(values):
    return lax.optimization_barrier(values)


def vmem():
    return pl.BlockSpec(memory_space=pltpu.VMEM)


def smem():
    return pl.BlockSpec(memory_space=pltpu.SMEM)


def hbm():
    return pl.BlockSpec(memory_space=pltpu.HBM)


def copies(pairs, sems):
    started = []
    for number, (source, target) in enumerate(pairs):
        copy = pltpu.make_async_copy(source, target, sems.at[number])
        copy.start()
        started.append(copy)
    return started


def dma(count):
    return pltpu.SemaphoreType.DMA((count,))


def column_blocks(ref, count):
    width = ref.shape[1] // count
    return [ref.at[:, pl.ds(i * width, width)] for i in range(count)]


def head_rows(ref, head):
    first = head * GROUP
    return jnp.concatenate(
        [
            ref[:, (first + i) * HEAD_FEATURES : (first + i + 1) * HEAD_FEATURES]
            for i in range(GROUP)
        ],
        axis=0,
    )


def own_rows(tokens):
    key = lax.broadcasted_iota(jnp.int32, (tokens, GROUP * tokens), 0)
    query = lax.broadcasted_iota(jnp.int32, (tokens, GROUP * tokens), 1) % tokens
    return key <= query


def to_slots(rows, own, tokens):
    last = rows.shape[0] - tokens
    return jnp.concatenate(
        [jnp.where(own, rows[last:], rows[:tokens]), rows[tokens:last]], axis=0
    )


def from_slots(slots, own, tokens):
    shared = slots[:tokens]
    return jnp.concatenate(
        [
            jnp.where(own, 0.0, shared).astype(BF16),
            slots[tokens:].astype(BF16),
            jnp.where(own, shared, 0.0).astype(BF16),
        ],
        axis=0,
    )


HEADS_A_STEP = 2


def head_specs(tokens, slots):
    probs = pl.BlockSpec((HEADS_A_STEP, slots, GROUP * tokens), lambda step: (step, 0, 0))
    wide = pl.BlockSpec((tokens, HEADS_A_STEP * GROUP * HEAD_FEATURES), lambda step: (0, step))
    thin = pl.BlockSpec((tokens, HEADS_A_STEP * HEAD_FEATURES), lambda step: (0, step))
    return probs, wide, thin


def probs_call(me, lengths, q, o, key_blocks):
    back = len(key_blocks) - 1
    docs = lengths.shape[1]
    tokens = q.shape[0]
    kv = key_blocks[0].shape[1]
    slots = back * tokens

    def kernel(me_ref, lengths_ref, q_ref, o_ref, *refs):
        key_refs = refs[: back + 1]
        p_ref = refs[back + 1]
        dv_refs = refs[back + 2 : 2 * back + 3]
        bias_ref = refs[2 * back + 3]

        @pl.when(pl.program_id(0) == 0)
        def _():
            here = me_ref[0]
            key = lax.broadcasted_iota(jnp.int32, (slots, tokens), 0)
            query = lax.broadcasted_iota(jnp.int32, (slots, tokens), 1)
            query_place = here * tokens + query
            shared = (key < tokens) & (key <= query)
            key_place = here * tokens + jnp.where(shared, key, key - slots)
            opening = jnp.zeros((slots, tokens), jnp.int32)
            bound = jnp.int32(0)
            for doc in range(docs):
                bound = bound + lengths_ref[0, doc]
                opening = jnp.where(query_place >= bound, bound, opening)
            bias_ref[...] = jnp.where(key_place >= opening, 0.0, NEG_FILL)

        own = own_rows(tokens)
        for head in range(HEADS_A_STEP):
            columns = slice(head * HEAD_FEATURES, (head + 1) * HEAD_FEATURES)
            key_rows = jnp.concatenate([r[:, columns] for r in key_refs], axis=0)
            scores = contract_trailing(key_rows, head_rows(q_ref, head))
            scores = to_slots(scores, own, tokens)
            scores = scores + jnp.concatenate([bias_ref[...]] * GROUP, axis=1)
            peak = jnp.max(scores, axis=0, keepdims=True)
            weights = jnp.exp2((scores - peak) * (INVERSE * LOG2E))
            probs = weights * (1.0 / jnp.sum(weights, axis=0, keepdims=True))
            p_ref[head] = probs.astype(BF16)
            dv = jnp.dot(
                from_slots(probs, own, tokens),
                head_rows(o_ref, head),
                preferred_element_type=F32,
            )
            for block in range(back + 1):
                rows = dv[block * tokens : (block + 1) * tokens]
                dv_refs[block][:, columns] = rows.astype(dv_refs[block].dtype)

    probs, wide, thin = head_specs(tokens, slots)
    out = pl.pallas_call(
        kernel,
        grid=(KEY_VALUE_HEADS // HEADS_A_STEP,),
        in_specs=[smem(), smem(), wide, wide] + [thin] * (back + 1),
        out_specs=[probs] + [thin] * (back + 1),
        out_shape=[jax.ShapeDtypeStruct((KEY_VALUE_HEADS, slots, GROUP * tokens), BF16)]
        + [jax.ShapeDtypeStruct((tokens, kv), BF16)] * back
        + [jax.ShapeDtypeStruct((tokens, kv), F32)],
        scratch_shapes=[pltpu.VMEM((slots, tokens), F32)],
        compiler_params=params(),
        cost_estimate=SMALL,
        name="probs",
    )(me, lengths, q, o, *key_blocks)
    return out[0], out[1:]


def scores_grad_call(probs, q, o, key_blocks, value_blocks):
    back = len(key_blocks) - 1
    tokens = q.shape[0]
    kv = key_blocks[0].shape[1]

    def kernel(p_ref, q_ref, o_ref, *refs):
        key_refs = refs[: back + 1]
        value_refs = refs[back + 1 : 2 * back + 2]
        dq_ref = refs[2 * back + 2]
        dk_refs = refs[2 * back + 3 :]
        own = own_rows(tokens)
        for head in range(HEADS_A_STEP):
            columns = slice(head * HEAD_FEATURES, (head + 1) * HEAD_FEATURES)
            key_rows = jnp.concatenate([r[:, columns] for r in key_refs], axis=0)
            value_rows = jnp.concatenate([r[:, columns] for r in value_refs], axis=0)
            grad_probs = contract_trailing(value_rows, head_rows(o_ref, head))
            grad_probs = to_slots(grad_probs, own, tokens)
            probs = p_ref[head].astype(F32)
            mass = jnp.sum(probs, axis=0, keepdims=True)
            delta = jnp.sum(probs * grad_probs, axis=0, keepdims=True) / mass
            grad_scores = from_slots(probs * (grad_probs - delta), own, tokens)
            dk = jnp.dot(grad_scores, head_rows(q_ref, head), preferred_element_type=F32)
            dk = dk * INVERSE
            dq = jnp.dot(key_rows.T, grad_scores, preferred_element_type=F32) * INVERSE
            for i in range(GROUP):
                first = (head * GROUP + i) * HEAD_FEATURES
                dq_ref[:, first : first + HEAD_FEATURES] = (
                    dq[:, i * tokens : (i + 1) * tokens].T.astype(BF16)
                )
            for block in range(back + 1):
                rows = dk[block * tokens : (block + 1) * tokens]
                dk_refs[block][:, columns] = rows.astype(dk_refs[block].dtype)

    block, wide, thin = head_specs(tokens, probs.shape[1])
    out = pl.pallas_call(
        kernel,
        grid=(KEY_VALUE_HEADS // HEADS_A_STEP,),
        in_specs=[block, wide, wide] + [thin] * (2 * back + 2),
        out_specs=[wide] + [thin] * (back + 1),
        out_shape=[jax.ShapeDtypeStruct(q.shape, BF16)]
        + [jax.ShapeDtypeStruct((tokens, kv), BF16)] * back
        + [jax.ShapeDtypeStruct((tokens, kv), F32)],
        compiler_params=params(),
        cost_estimate=SMALL,
        name="scores_grad",
    )(probs, q, o, *key_blocks, *value_blocks)
    return out[0], out[1:]


def swap(array, name):
    return flip(array, "seq", 1, name)


def x_halves_call(me, x, shards):
    tokens, model = x.shape
    half = model // shards // 2

    def kernel(me_ref, x_hbm, mine_ref, theirs_ref, sems):
        core = me_ref[0] % 2
        pairs = []
        for which, target in ((1 - core, theirs_ref), (core, mine_ref)):
            for shard in range(shards):
                first = pl.multiple_of(2 * shard * half + which * half, half)
                pairs.append(
                    (x_hbm.at[:, pl.ds(first, half)], target.at[:, pl.ds(shard * half, half)])
                )
        for copy in copies(pairs, sems):
            copy.wait()

    return pl.pallas_call(
        kernel,
        in_specs=[smem(), hbm()],
        out_specs=[vmem()] * 2,
        out_shape=[jax.ShapeDtypeStruct((tokens, model // 2), BF16)] * 2,
        scratch_shapes=[dma(2 * shards)],
        compiler_params=params(),
        cost_estimate=SMALL,
        name="x_halves",
    )(me, x)


def put_half_call(me, out, theirs, shards):
    tokens, model = out.shape
    half = model // shards // 2

    def kernel(me_ref, theirs_ref, out_in, out_hbm, sems):
        which = 1 - me_ref[0] % 2
        pairs = []
        for shard in range(shards):
            first = pl.multiple_of(2 * shard * half + which * half, half)
            pairs.append(
                (theirs_ref.at[:, pl.ds(shard * half, half)], out_hbm.at[:, pl.ds(first, half)])
            )
        for copy in copies(pairs, sems):
            copy.wait()

    return pl.pallas_call(
        kernel,
        in_specs=[smem(), vmem(), hbm()],
        out_specs=hbm(),
        out_shape=jax.ShapeDtypeStruct((tokens, model), BF16),
        scratch_shapes=[dma(shards)],
        input_output_aliases={2: 0},
        compiler_params=params(),
        cost_estimate=SMALL,
        name="put_half",
    )(me, theirs, out)


def join_call(me, mine, theirs, shards, model):
    rank, width = mine.shape
    kv = width - model // 2
    half = model // shards // 2

    def kernel(me_ref, mine_ref, theirs_ref, down_ref, up_ref):
        core = me_ref[0] % 2
        for which, ref in ((core, mine_ref), (1 - core, theirs_ref)):
            for shard in range(shards):
                first = pl.multiple_of(2 * shard * half + which * half, half)
                down_ref[:, pl.ds(first, half)] = ref[:, shard * half : (shard + 1) * half]
        up_ref[...] = mine_ref[:, model // 2 :] + theirs_ref[:, model // 2 :]

    return pl.pallas_call(
        kernel,
        in_specs=[smem(), vmem(), vmem()],
        out_specs=[vmem()] * 2,
        out_shape=[
            jax.ShapeDtypeStruct((rank, model), F32),
            jax.ShapeDtypeStruct((rank, kv), F32),
        ],
        compiler_params=params(),
        cost_estimate=SMALL,
        name="join_adapter",
    )(me, mine, theirs)


def own_values_call(me, x_mine, x_theirs, down, up, w):
    tokens, width = x_mine.shape
    rows, kv = w.shape
    rank, model = down.shape
    half = rows // 2
    shards = model // rows

    def kernel(me_ref, mine_hbm, theirs_hbm, down_hbm, up_ref, w_hbm, acc_ref, low_ref, *scratch):
        x_ref, down_ref, w_ref, sems = scratch
        core = me_ref[0] % 2
        pairs = []
        for shard in range(shards):
            first = pl.multiple_of(shard * rows + core * half, half)
            pairs.append(
                (down_hbm.at[:, pl.ds(first, half)], down_ref.at[:, pl.ds(shard * half, half)])
            )
        pairs.append((mine_hbm, x_ref.at[pl.ds(0, tokens)]))
        pairs.append((theirs_hbm, x_ref.at[pl.ds(tokens, tokens)]))
        pairs.append((w_hbm.at[pl.ds(pl.multiple_of(core * half, half), half)], w_ref))
        for copy in copies(pairs, sems):
            copy.wait()
        low = contract_trailing(x_ref[...], down_ref[...])
        low_ref[...] = low
        adapter = jnp.dot(
            low,
            up_ref[...].astype(F32),
            precision=lax.Precision.HIGHEST,
            preferred_element_type=F32,
        )
        first = pl.multiple_of(me_ref[1] * half, half)
        acc_ref[...] = ADAPTER_SCALE * adapter + jnp.dot(
            x_ref[:, pl.ds(first, half)], w_ref[...], preferred_element_type=F32
        )

    return pl.pallas_call(
        kernel,
        in_specs=[smem(), hbm(), hbm(), hbm(), vmem(), hbm()],
        out_specs=[vmem()] * 2,
        out_shape=[
            jax.ShapeDtypeStruct((2 * tokens, kv), F32),
            jax.ShapeDtypeStruct((2 * tokens, rank), F32),
        ],
        scratch_shapes=[
            pltpu.VMEM((2 * tokens, width), BF16),
            pltpu.VMEM((rank, width), BF16),
            pltpu.VMEM((half, kv), BF16),
            dma(shards + 3),
        ],
        compiler_params=params(),
        cost_estimate=SMALL,
        name="own_values",
    )(me, x_mine, x_theirs, down, up, w)


class Pieces:
    def __init__(self, half, seq_count, fsdp_count):
        self.fsdp_count = fsdp_count
        self.half = half
        self.by_parts = (half // (seq_count // 2)) % 128 == 0
        self.step = half // (seq_count // 2) if self.by_parts else half
        self.each = half // self.step
        self.order = gather_order(seq_count)

    def chip(self, me_ref, number):
        if not self.by_parts:
            return 0
        even, odd = (int(self.order[i][number] ^ i) // 2 for i in range(2))
        here = me_ref[0]
        return lax.bitwise_xor(here // 2, jnp.where(here % 2 == 0, even, odd))

    def owner(self, me_ref, by):
        return lax.rem(me_ref[1] + (self.fsdp_count - by), self.fsdp_count)


def heights(arrays):
    firsts, first = [], 0
    for array in arrays:
        firsts.append(first)
        first += array.shape[0]
    return firsts, first


def more_values_call(me, x_mine, x_theirs, acc, shards, pieces, last):
    tokens = x_mine.shape[0]
    half, step = pieces.half, pieces.step
    bys = list(shards)
    arrays = [array for by in bys for array in shards[by]]
    firsts, rows = heights(arrays)
    count = len(bys)
    kv = acc.shape[1]

    def kernel(me_ref, acc_ref, mine_hbm, theirs_hbm, *refs):
        outs = refs[len(arrays) : -3]
        x_ref, w_ref, sems = refs[-3:]
        pairs = []
        for i, by in enumerate(bys):
            columns = pl.ds(pl.multiple_of(pieces.owner(me_ref, by) * half, half), half)
            pairs.append((mine_hbm.at[:, columns], x_ref.at[i, pl.ds(0, tokens)]))
            pairs.append((theirs_hbm.at[:, columns], x_ref.at[i, pl.ds(tokens, tokens)]))
        for ref, first, array in zip(refs, firsts, arrays):
            pairs.append((ref, w_ref.at[pl.ds(first, array.shape[0])]))
        for copy in copies(pairs, sems):
            copy.wait()
        total = acc_ref[...]
        for row in range(0, rows, step):
            i, number = row // half, (row % half) // step
            column = pl.multiple_of(pieces.chip(me_ref, number) * step, step)
            total = total + jnp.dot(
                x_ref[i, :, pl.ds(column, step)],
                w_ref[row : row + step, :],
                preferred_element_type=F32,
            )
        if last:
            outs[0][...] = total[:tokens]
            outs[1][...] = total[tokens:]
        else:
            outs[0][...] = total

    one = jax.ShapeDtypeStruct((tokens, kv), F32)
    out = pl.pallas_call(
        kernel,
        in_specs=[smem(), vmem()] + [hbm()] * (2 + len(arrays)),
        out_specs=[vmem()] * (2 if last else 1),
        out_shape=[one, one] if last else [jax.ShapeDtypeStruct(acc.shape, F32)],
        scratch_shapes=[
            pltpu.VMEM((count, 2 * tokens, half), BF16),
            pltpu.VMEM((rows, kv), BF16),
            dma(2 * count + len(arrays)),
        ],
        compiler_params=params(),
        cost_estimate=SMALL,
        name="more_values",
    )(me, acc, x_mine, x_theirs, *arrays)
    return out if last else out[0]


def input_grad_call(me, dv_mine, dv_theirs, rank_grad, down, w, shards, pieces):
    tokens, kv = dv_mine.shape
    rank, model = down.shape
    half, step = pieces.half, pieces.step
    rows = 2 * half
    bys = list(shards)
    arrays = [array for by in bys for array in shards[by]]
    firsts, _ = heights(arrays)
    count = 1 + len(bys)
    width = model // 2

    def kernel(me_ref, mine_ref, theirs_ref, rank_ref, down_hbm, w_hbm, *refs):
        out_hbm, send_hbm, down_ref, w_ref, term, buffer, sems, out_sems = refs[len(arrays) :]
        core = me_ref[0] % 2
        starts = [pl.multiple_of(i * rows + core * half, half) for i in range(count)]
        pairs = [
            (down_hbm.at[:, pl.ds(starts[i], half)], down_ref.at[:, pl.ds(i * half, half)])
            for i in range(count)
        ]
        pairs.append(
            (w_hbm.at[pl.ds(pl.multiple_of(core * half, half), half)], w_ref.at[pl.ds(0, half)])
        )
        for ref, first, array in zip(refs, firsts, arrays):
            pairs.append((ref, w_ref.at[pl.ds(half + first, array.shape[0])]))
        loads = copies(pairs, sems)
        for load in loads[: count + 1]:
            load.wait()
        term[...] = jnp.dot(rank_ref[...], down_ref[...], preferred_element_type=F32)
        dv = jnp.concatenate([mine_ref[...], theirs_ref[...]], axis=0)
        own = pl.multiple_of(me_ref[1] * half, half)
        grad = contract_trailing(dv, w_ref[0:half, :]) + term[:, pl.ds(own, half)]
        buffer[:, pl.ds(own, half)] = grad.astype(BF16)
        for load in loads[count + 1 :]:
            load.wait()
        for i, by in enumerate(bys):
            rows_of = pl.ds(half + i * half, half)
            grad = contract_trailing(dv, w_ref[rows_of, :])
            for number in range(pieces.each):
                column = pieces.owner(me_ref, by) * half + pieces.chip(me_ref, number) * step
                column = pl.multiple_of(column, step)
                part = grad[:, number * step : (number + 1) * step]
                part = part + term[:, pl.ds(column, step)]
                buffer[:, pl.ds(column, step)] = part.astype(BF16)
        pairs = [(buffer.at[pl.ds(tokens, tokens)], send_hbm)]
        for i in range(count):
            pairs.append(
                (
                    buffer.at[pl.ds(0, tokens), pl.ds(i * half, half)],
                    out_hbm.at[:, pl.ds(starts[i], half)],
                )
            )
        for copy in copies(pairs, out_sems):
            copy.wait()

    return pl.pallas_call(
        kernel,
        in_specs=[smem(), vmem(), vmem(), vmem()] + [hbm()] * (2 + len(arrays)),
        out_specs=[hbm()] * 2,
        out_shape=[
            jax.ShapeDtypeStruct((tokens, model), BF16),
            jax.ShapeDtypeStruct((tokens, width), BF16),
        ],
        scratch_shapes=[
            pltpu.VMEM((rank, width), BF16),
            pltpu.VMEM((width, kv), BF16),
            pltpu.VMEM((2 * tokens, width), F32),
            pltpu.VMEM((2 * tokens, width), BF16),
            dma(count + 1 + len(arrays)),
            dma(1 + count),
        ],
        compiler_params=params(),
        cost_estimate=SMALL,
        name="input_grad",
    )(me, dv_mine, dv_theirs, rank_grad, down, w, *arrays)


def adapter_grad_call(dv_mine, dv_theirs, up, low, x_mine, x_theirs, scale):
    tokens, width = x_mine.shape
    rank, kv = up.shape

    def kernel(mine_ref, theirs_ref, up_ref, low_ref, x_mine_hbm, x_theirs_hbm, *refs):
        rank_ref, out_ref, x_ref, sems = refs
        loads = copies(
            [
                (x_mine_hbm, x_ref.at[pl.ds(0, tokens)]),
                (x_theirs_hbm, x_ref.at[pl.ds(tokens, tokens)]),
            ],
            sems,
        )
        dv = jnp.concatenate([mine_ref[...], theirs_ref[...]], axis=0)
        rank_low = (ADAPTER_SCALE * contract_trailing(dv, up_ref[...])).astype(BF16)
        rank_ref[...] = rank_low
        raised = contract_leading(low_ref[...], dv.astype(F32), lax.Precision.HIGHEST)
        out_ref[:, width:] = raised * (ADAPTER_SCALE * scale)
        for load in loads:
            load.wait()
        out_ref[:, :width] = contract_leading(rank_low, x_ref[...]) * scale

    return pl.pallas_call(
        kernel,
        in_specs=[vmem()] * 4 + [hbm()] * 2,
        out_specs=[vmem()] * 2,
        out_shape=[
            jax.ShapeDtypeStruct((2 * tokens, rank), BF16),
            jax.ShapeDtypeStruct((rank, width + kv), F32),
        ],
        scratch_shapes=[pltpu.VMEM((2 * tokens, width), BF16), dma(2)],
        compiler_params=params(),
        cost_estimate=SMALL,
        name="adapter_grad",
    )(dv_mine, dv_theirs, up, low, x_mine, x_theirs)


def sum_steps(seq_count, fsdp_count):
    steps, bit = [], 1
    while bit < fsdp_count:
        steps.append(("fsdp", bit))
        bit *= 2
    return steps + [("seq", bit) for bit in chip_bits(seq_count)[::-1]]


def sum_step(low, step, keep=False):
    axis, mask = step
    total = low.astype(F32) + flip(low, axis, mask, "adapter_sum").astype(F32)
    return total if keep else total.astype(BF16)


def chip_bits(seq_count):
    return [1 << b for b in range(1, seq_count.bit_length() - 1)]


def chip_mask(seq_count, stage):
    bits = chip_bits(seq_count)
    return lambda index: bits[stage] if index % 2 == 0 else bits[len(bits) - 1 - stage]


def gather_order(seq_count):
    held = [[i] for i in range(seq_count)]
    for stage in range(len(chip_bits(seq_count))):
        mask = chip_mask(seq_count, stage)
        held = [held[i] + held[i ^ mask(i)] for i in range(seq_count)]
    order = np.array(held, np.int32)
    relative = order ^ np.arange(seq_count, dtype=np.int32)[:, None]
    assert (relative == relative[np.arange(seq_count) % 2]).all()
    return order


def ring_order(fsdp_count):
    return sorted(range(1, fsdp_count), key=lambda by: (min(by, fsdp_count - by), by))


def across(array, stage):
    mask = chip_mask(lax.axis_size("seq"), stage)
    return flip(array, "seq", mask, f"weight_chip_{stage}")


def spread_step(held):
    stages = len(chip_bits(lax.axis_size("seq")))
    size = len(held)
    if size == 1 << stages:
        return None
    if size == 1 and stages >= 2:
        return held + [across(held[0], 0), across(held[0], 1)]
    if size == 3:
        return held + [across(held[1], 1)]
    stage = size.bit_length() - 1
    if size == 1:
        return held + [across(held[0], stage)]
    joined = jnp.concatenate(held, axis=0)
    other = across(joined, stage)
    height = held[0].shape[0]
    return held + [other[i * height : (i + 1) * height] for i in range(size)]


def natural_half(held, order, here):
    width = held[0].shape[1]
    chips = jnp.asarray(order)[here] // 2
    joined = jnp.concatenate(held, axis=0).reshape(len(held), -1, width)
    return [jnp.take(joined, jnp.argsort(chips), axis=0).reshape(-1, width)]


def body(
    normed_block_input,
    stored_rotated_queries,
    stored_rotated_keys,
    attention_output_gradient,
    frozen_value_weight,
    adapter_down_weight,
    adapter_up_weight,
    packed_document_lengths,
):
    x = normed_block_input[0]
    q = stored_rotated_queries[0]
    k = stored_rotated_keys[0]
    o = attention_output_gradient[0]
    w = frozen_value_weight
    down, up = adapter_down_weight, adapter_up_weight
    tokens, model = x.shape
    seq_count = lax.axis_size("seq")
    fsdp_count = lax.axis_size("fsdp")
    here = lax.axis_index("seq")
    half = w.shape[0] // 2
    part_rows = half // (seq_count // 2)
    longest = tokens * seq_count // 4
    back = -(-longest // tokens)
    me = jnp.stack([here, lax.axis_index("fsdp")]).astype(jnp.int32)
    pieces = Pieces(half, seq_count, fsdp_count)
    ring = ring_order(fsdp_count)

    first_row = (here % 2) * half + (here // 2) * part_rows
    arrived = {0: lax.dynamic_slice_in_dim(w, first_row, part_rows, 0)}
    to_come = list(ring)
    held = {}

    def ring_step(count):
        for by in to_come[:count]:
            upward = 2 * by <= fsdp_count
            source = by - 1 if upward else (by + 1) % fsdp_count
            arrived[by] = turn(arrived[source], "fsdp", 1 if upward else -1)
        del to_come[:count]

    def advance(bys=ring):
        for by in list(held):
            held[by] = spread_step(held[by]) or held[by]
        for by in ring:
            if by in bys and by in ready and by not in held:
                held[by] = spread_step([arrived[by]]) or [arrived[by]]

    ready = set()

    ring_step(2)
    arrived[0], x = after((arrived[0], x))
    key_blocks = [shift(k, "seq", by, "key_halo") for by in range(back, 0, -1)] + [k]
    x_mine, x_sent = x_halves_call(me, x, fsdp_count)
    x_theirs = swap(x_sent, "x_core")
    probs, dv_blocks = probs_call(me, packed_document_lengths, q, o, key_blocks)
    arrived, dv_blocks, x_theirs = after((arrived, dv_blocks, x_theirs))
    ready.update(by for by in arrived if by)

    dv_back = [
        shift(dv_blocks[back - by], "seq", -by, "value_grad_halo") for by in range(1, back + 1)
    ]
    advance()
    ring_step(1)
    acc, low = own_values_call(me, x_mine, x_theirs, down, up, w)
    arrived, held, dv_back, acc, low = after((arrived, held, dv_back, acc, low))
    ready.update(by for by in arrived if by)

    steps = sum_steps(seq_count, fsdp_count)
    used = {}
    chips = seq_count // 2
    sums = None

    def complete():
        return {by: held[by] for by in ring if by in held and len(held[by]) == chips}

    def arrays_of(parts):
        if pieces.by_parts:
            return parts
        return {by: natural_half(parts[by], pieces.order, here) for by in parts}

    while sums is None or len(complete()) < len(ring):
        done = {by: parts for by, parts in complete().items() if by not in used}
        advance()
        ring_step(1)
        if sums is None:
            dv = dv_blocks[back]
            for block in dv_back:
                dv = dv + block.astype(F32)
            dv_mine = dv.astype(BF16)
            dv_theirs = swap(dv_mine, "value_grad_core")
            scale = 1.0 / (tokens * seq_count * fsdp_count)
            rank_grad, sums = adapter_grad_call(
                dv_mine, dv_theirs, up, low, x_mine, x_theirs, scale
            )
        if len(steps) > 2:
            sums = sum_step(sums, steps.pop(0))
        if done and len(done) == len(ring) - 1:
            acc = more_values_call(me, x_mine, x_theirs, acc, arrays_of(done), pieces, False)
            used.update(done)
        arrived, held, acc, sums = after((arrived, held, acc, sums))
        ready.update(by for by in arrived if by)
    rest = {by: held[by] for by in ring if by not in used}
    values, values_sent = more_values_call(
        me, x_mine, x_theirs, acc, arrays_of(rest), pieces, True
    )

    values = (values + swap(values_sent, "values_core")).astype(BF16)
    values, dv_mine, sums = after((values, dv_mine, sums))
    value_blocks = [shift(values, "seq", by, "value_halo") for by in range(back, 0, -1)] + [values]
    while len(steps) > 1:
        sums = sum_step(sums, steps.pop(0))
    input_grad, input_grad_sent = input_grad_call(
        me, dv_mine, dv_theirs, rank_grad, down, w, arrays_of(complete()), pieces
    )
    value_blocks, sums, input_grad_sent = after((value_blocks, sums, input_grad_sent))

    total = sum_step(sums, steps[0], keep=True) if steps else sums.astype(F32)
    rotated_query_gradient, dk_blocks = scores_grad_call(probs, q, o, key_blocks, value_blocks)
    total, input_grad_sent, dk_blocks = after((total, input_grad_sent, dk_blocks))
    dk_back = [
        shift(dk_blocks[back - by], "seq", -by, "key_grad_halo") for by in range(1, back + 1)
    ]
    total_theirs = swap(total, "adapter_core")
    input_grad_theirs = swap(input_grad_sent, "input_grad_core")
    input_gradient = put_half_call(me, input_grad, input_grad_theirs, fsdp_count)
    down_gradient, up_gradient = join_call(me, total, total_theirs, fsdp_count, model)
    dk_back, input_gradient, down_gradient, up_gradient = after(
        (dk_back, input_gradient, down_gradient, up_gradient)
    )
    key_gradient = dk_blocks[back]
    for block in dk_back:
        key_gradient = key_gradient + block.astype(F32)
    return (
        input_gradient[None],
        rotated_query_gradient[None],
        key_gradient.astype(BF16)[None],
        down_gradient,
        up_gradient,
    )


def solution(mesh):
    placed = (
        P("fsdp", "seq", None),
        P("fsdp", "seq", None),
        P("fsdp", "seq", None),
        P("fsdp", "seq", None),
        P("fsdp", None),
        P(),
        P(),
        P("fsdp", None),
    )
    return jax.shard_map(
        body,
        mesh=mesh,
        in_specs=placed,
        out_specs=(
            P("fsdp", "seq", None),
            P("fsdp", "seq", None),
            P("fsdp", "seq", None),
            P(),
            P(),
        ),
        check_vma=False,
    )
```

time: 389 us -> 106 us (0.27)
  waiting for transfers between devices: 195 us -> 33.1 us
  blocking collectives: 51.1 us -> 0 us
  matrix products: 44 us -> 0 us
  local copies, waits for them, and re-layouts: 39.4 us -> 4.29 us
  Pallas kernels: 0 us -> 23.1 us
  between operations: 16 us -> 0.97 us
  starting transfers between devices: 30 us -> 42.9 us
  other arithmetic: 13 us -> 0.99 us
    all_gather x1 -> x0, waiting for transfers between devices: 72.9 us -> none  [body(): lax.all_gather(frozen_value_weight, 'fsdp', axis=0, tiled=True)]
    psum x1 -> x0, waiting for transfers between devices: 61.1 us -> none  [body(): lax.psum((down_shard, up_shard), ('seq', 'fsdp'))]
    all_to_all x7 -> x0, waiting for transfers between devices: 60.1 us -> none  [the longest x1 13.9 us: body(): lax.all_to_all(grad_values, 'seq', split_axis=0, concat_axis=1, tiled=True)]
    psum x1 -> x0, blocking collectives: 51.1 us -> none  [body(): lax.psum((down_shard, up_shard), ('seq', 'fsdp'))]
    ppermute x0 -> x29, starting transfers between devices: none -> 42.9 us  [the longest x18 23 us: flip(): return lax.ppermute(value, axis, [(i, i ^ choose(i)) for i in range(size)])]
    ppermute x0 -> x29, waiting for transfers between devices: none -> 33.1 us  [the longest x18 24.7 us: flip(): return lax.ppermute(value, axis, [(i, i ^ choose(i)) for i in range(size)])]
    dot_general x16 -> x0, matrix products: 33 us -> none  [the longest x2 9.07 us: body(): jnp.einsum('hqk,qhd->khd', probs_low, grad_block, preferred_element_type=...]
    all_to_all x7 -> x0, starting transfers between devices: 29.9 us -> none  [the longest x1 5.17 us: body(): lax.all_to_all(key_broadcast, 'seq', split_axis=1, concat_axis=0, tiled=T...]
  transfers between devices with their start and end apart: 9 -> 29, of which waited for: 8 -> 14; matrix products, arithmetic and copies ran while one was open for 22% -> 0% of each run, Pallas kernels for 0% -> 19%
where the time goes in v2:
time: 106 us; the launch traced here: 105 us
  starting transfers between devices  42.9 us (40%)
  waiting for transfers between devices  33.1 us (31%)
  Pallas kernels  23.1 us (22%)
  local copies, waits for them, and re-layouts  4.29 us (4%)
    ppermute x18, waiting for transfers between devices, flip(): return lax.ppermute(value, axis, [(i, i ^ choose(i)) for i in range(size)])  24.7 us
    ppermute x18, starting transfers between devices, flip(): return lax.ppermute(value, axis, [(i, i ^ choose(i)) for i in range(size)])  23 us
    ppermute x8, starting transfers between devices, shift(): lax.ppermute(value, axis, [(i, i + by) for i in range(size) if 0 <= i + b...  15.2 us
    ppermute x8, waiting for transfers between devices, shift(): lax.ppermute(value, axis, [(i, i + by) for i in range(size) if 0 <= i + b...  8.46 us
    ppermute x3, starting transfers between devices, turn(): lax.ppermute(value, axis, [(i, (i + by) % size) for i in range(size)])  4.67 us
    pallas_call x1, Pallas kernels, scores_grad_call(): pl.pallas_call(kernel, grid=(KEY_VALUE_HEADS // HEADS_A_STEP,), in_specs=...  4.32 us
    pallas_call x1, Pallas kernels, input_grad_call(): pl.pallas_call(kernel, in_specs=[smem(), vmem(), vmem(), vmem()] + [hbm()...  4.29 us
    pallas_call x1, Pallas kernels, probs_call(): pl.pallas_call(kernel, grid=(KEY_VALUE_HEADS // HEADS_A_STEP,), in_specs=...  3.55 us
  transfers between devices with their start and end apart: 29, of which 14 were waited for; matrix products, arithmetic and copies ran while one was open for 0% of the time, Pallas kernels for 19%

profile of v2, /device:TPU:0, one launch (start us, length us, event | category | flops | bytes accessed | tf_op | source)
XLA Modules:
  0.0 105.5 jit_solution(2030304935514190161)
XLA Ops:
  4.8 4.7 %collective-permute-start.1 = (bf16[256,512]{1,0:T(8,128)(2,1)S(1)}, bf16[256,512]{1,0:T(8,128)(2,1)S(1)}, u32[]{:S(2)}, u32[]{:S(2)}) collective-permute-start(bf16[256,512]{1,0:T(8,128)(2,1)S(1)} %constant_dynamic-slice_fusion), channel_id=1, source_target_pairs={{0,3},{1,0},{2,1},{3,2},{4,7},{5,4},{6,5},{7,6},{8,11},{9,8},{10,9... | collective-permute-start | bytes 786440 | tf_op jit(solution)/shard_map/weight_ring/ppermute | solution.py:55
  9.4 2.1 %collective-permute-start.3 = (bf16[128,512]{1,0:T(8,128)(2,1)}, bf16[128,512]{1,0:T(8,128)(2,1)S(1)}, u32[]{:S(2)}, u32[]{:S(2)}) collective-permute-start(bf16[128,512]{1,0:T(8,128)(2,1)} %bitcast.15), channel_id=1, source_target_pairs={{0,4},{4,8},{8,12},{12,16},{16,20},{20,24},{24,28},{1,5},{5,9},{9,... | collective-permute-start | bytes 393224 | tf_op jit(solution)/shard_map/key_halo/ppermute | solution.py:49
  11.5 3.4 %collective-permute-start.2 = (bf16[128,512]{1,0:T(8,128)(2,1)}, bf16[128,512]{1,0:T(8,128)(2,1)S(1)}, u32[]{:S(2)}, u32[]{:S(2)}) collective-permute-start(bf16[128,512]{1,0:T(8,128)(2,1)} %bitcast.16), channel_id=1, source_target_pairs={{0,8},{4,12},{8,16},{12,20},{16,24},{20,28},{1,9},{5,13},{9,17},{1... | collective-permute-start | bytes 393224 | tf_op jit(solution)/shard_map/key_halo/ppermute | solution.py:49
  14.9 3.8 %collective-permute-done.2.refs_0_ = bf16[128,512]{1,0:T(8,128)(2,1)S(1)} collective-permute-done((bf16[128,512]{1,0:T(8,128)(2,1)}, bf16[128,512]{1,0:T(8,128)(2,1)S(1)}, u32[]{:S(2)}, u32[]{:S(2)}) %collective-permute-start.2) | collective-permute-done | bytes 131104 | tf_op jit(solution)/shard_map/key_halo/ppermute | solution.py:49
  20.3 3.5 %probs.1 = (bf16[4,256,1024]{2,1,0:T(8,128)(2,1)S(1)}, bf16[128,512]{1,0:T(8,128)(2,1)S(1)}, bf16[128,512]{1,0:T(8,128)(2,1)S(1)}, f32[128,512]{1,0:T(8,128)S(1)}) custom-call(s32[2]{0:T(128)S(1)} %pad_add_fusion.me_ref, s32[1,8]{1,0:T(1,128)S(1)} %copy-done.8, bf16[128,4096]{1,0:T(8,128)(2,1)S(1)} %bitcast.10, bf16[128,4096]{1,0:T(8,128)(2,1)S(1)} %bitcast.12, ...), custom_call_target="tpu_custom_call" | custom-call | flops 1 | bytes 1 | tf_op jit(solution)/shard_map/probs/pallas_call | solution.py:187
  26.5 5.3 %collective-permute-start.9 = (bf16[256,512]{1,0:T(8,128)(2,1)S(1)}, bf16[256,512]{1,0:T(8,128)(2,1)S(1)}, u32[]{:S(2)}, u32[]{:S(2)}) collective-permute-start(bf16[256,512]{1,0:T(8,128)(2,1)S(1)} %collective-permute-done.1.refs_4_), channel_id=1, source_target_pairs={{0,16},{4,12},{8,24},{12,4},{16,0},{20,28},{24,8},{28,20},{1,17},{... | collective-permute-start | bytes 786440 | tf_op jit(solution)/shard_map/weight_chip_1/ppermute | solution.py:43
  31.7 2.0 %collective-permute-start.8 = (bf16[256,512]{1,0:T(8,128)(2,1)S(1)}, bf16[256,512]{1,0:T(8,128)(2,1)S(1)}, u32[]{:S(2)}, u32[]{:S(2)}) collective-permute-start(bf16[256,512]{1,0:T(8,128)(2,1)S(1)} %collective-permute-done.1.refs_4_), channel_id=1, source_target_pairs={{0,8},{4,20},{8,0},{12,28},{16,24},{20,4},{24,16},{28,12},{1,9},{5... | collective-permute-start | bytes 786440 | tf_op jit(solution)/shard_map/weight_chip_0/ppermute | solution.py:43
  34.5 3.4 %own_values.1 = (f32[256,512]{1,0:T(8,128)S(1)}, f32[256,16]{1,0:T(8,128)S(1)}) custom-call(s32[2]{0:T(128)S(1)} %pad_add_fusion.me_ref, bf16[128,4096]{1,0:T(8,128)(2,1)S(1)} %get-tuple-element.97.mine_hbm.x_mine_hbm, bf16[128,4096]{1,0:T(8,128)(2,1)S(1)} %collective-permute-done.4.theirs_hbm.x_theirs_hbm, bf16[16,8192]{1,0:T(8,128)(2,1)S(1)} %copy-done.4, ...), custom_call_target="tpu_custom_call" | custom-call | flops 1 | bytes 1 | tf_op jit(solution)/shard_map/own_values/pallas_call | solution.py:373
  38.3 2.7 %collective-permute-done.8.refs_5_ = bf16[256,512]{1,0:T(8,128)(2,1)S(1)} collective-permute-done((bf16[256,512]{1,0:T(8,128)(2,1)S(1)}, bf16[256,512]{1,0:T(8,128)(2,1)S(1)}, u32[]{:S(2)}, u32[]{:S(2)}) %collective-permute-start.8) | collective-permute-done | bytes 262176 | tf_op jit(solution)/shard_map/weight_chip_0/ppermute | solution.py:43
  41.0 2.9 %collective-permute-done.7.refs_2_ = bf16[256,512]{1,0:T(8,128)(2,1)S(1)} collective-permute-done((bf16[256,512]{1,0:T(8,128)(2,1)S(1)}, bf16[256,512]{1,0:T(8,128)(2,1)S(1)}, u32[]{:S(2)}, u32[]{:S(2)}) %collective-permute-start.7) | collective-permute-done | bytes 262176 | tf_op jit(solution)/shard_map/weight_chip_1/ppermute | solution.py:43
  48.1 2.8 %collective-permute-start.14 = (bf16[256,512]{1,0:T(8,128)(2,1)S(1)}, bf16[256,512]{1,0:T(8,128)(2,1)S(1)}, u32[]{:S(2)}, u32[]{:S(2)}) collective-permute-start(bf16[256,512]{1,0:T(8,128)(2,1)S(1)} %collective-permute-done.5.refs_0_.refs_8_), channel_id=1, source_target_pairs={{0,16},{4,12},{8,24},{12,4},{16,0},{20,28},{24,8},{28,20},{1,17},{... | collective-permute-start | bytes 786440 | tf_op jit(solution)/shard_map/weight_chip_1/ppermute | solution.py:43
  53.5 3.7 %collective-permute-done.17 = f32[16,4608]{1,0:T(8,128)S(1)} collective-permute-done((f32[16,4608]{1,0:T(8,128)S(1)}, f32[16,4608]{1,0:T(8,128)S(1)}, u32[]{:S(2)}, u32[]{:S(2)}) %collective-permute-start.17) | collective-permute-done | bytes 294944 | tf_op jit(solution)/shard_map/adapter_sum/ppermute | solution.py:43
  57.2 3.7 %collective-permute-done.12.refs_3_ = bf16[256,512]{1,0:T(8,128)(2,1)S(1)} collective-permute-done((bf16[256,512]{1,0:T(8,128)(2,1)S(1)}, bf16[256,512]{1,0:T(8,128)(2,1)S(1)}, u32[]{:S(2)}, u32[]{:S(2)}) %collective-permute-start.12) | collective-permute-done | bytes 262176 | tf_op jit(solution)/shard_map/weight_chip_1/ppermute | solution.py:43
  60.9 2.8 %collective-permute-done.15.refs_7_ = bf16[256,512]{1,0:T(8,128)(2,1)S(1)} collective-permute-done((bf16[256,512]{1,0:T(8,128)(2,1)S(1)}, bf16[256,512]{1,0:T(8,128)(2,1)S(1)}, u32[]{:S(2)}, u32[]{:S(2)}) %collective-permute-start.15) | collective-permute-done | bytes 262176 | tf_op jit(solution)/shard_map/weight_chip_1/ppermute | solution.py:43
  63.7 3.9 %collective-permute-start.19 = (bf16[16,4608]{1,0:T(8,128)(2,1)S(1)}, bf16[16,4608]{1,0:T(8,128)(2,1)S(1)}, u32[]{:S(2)}, u32[]{:S(2)}) collective-permute-start(bf16[16,4608]{1,0:T(8,128)(2,1)S(1)} %add_convert_fusion.2), channel_id=1, source_target_pairs={{0,2},{1,3},{2,0},{3,1},{4,6},{5,7},{6,4},{7,5},{8,10},{9,11},{10,... | collective-permute-start | bytes 442376 | tf_op jit(solution)/shard_map/adapter_sum/ppermute | solution.py:43
  69.1 1.6 %more_values.2.acc_ref = f32[256,512]{1,0:T(8,128)S(1)} custom-call(s32[2]{0:T(128)S(1)} %pad_add_fusion.me_ref, f32[256,512]{1,0:T(8,128)S(1)} %get-tuple-element.125.acc_ref, bf16[128,4096]{1,0:T(8,128)(2,1)S(1)} %get-tuple-element.97.mine_hbm.x_mine_hbm, bf16[128,4096]{1,0:T(8,128)(2,1)S(1)} %collective-permute-done.4.theirs_hbm.x_theirs_hbm, ...), custom_call_target="tpu_custom_call" | custom-call | flops 1 | bytes 1 | tf_op jit(solution)/shard_map/more_values/pallas_call | solution.py:458
  70.7 3.4 %collective-permute-done.19 = bf16[16,4608]{1,0:T(8,128)(2,1)S(1)} collective-permute-done((bf16[16,4608]{1,0:T(8,128)(2,1)S(1)}, bf16[16,4608]{1,0:T(8,128)(2,1)S(1)}, u32[]{:S(2)}, u32[]{:S(2)}) %collective-permute-start.19) | collective-permute-done | bytes 147488 | tf_op jit(solution)/shard_map/adapter_sum/ppermute | solution.py:43
  77.0 1.7 %collective-permute-start.23 = (bf16[16,4608]{1,0:T(8,128)(2,1)S(1)}, bf16[16,4608]{1,0:T(8,128)(2,1)S(1)}, u32[]{:S(2)}, u32[]{:S(2)}) collective-permute-start(bf16[16,4608]{1,0:T(8,128)(2,1)S(1)} %add_convert_fusion.1), channel_id=1, source_target_pairs={{0,16},{4,20},{8,24},{12,28},{16,0},{20,4},{24,8},{28,12},{1,17},{... | collective-permute-start | bytes 442376 | tf_op jit(solution)/shard_map/adapter_sum/ppermute | solution.py:43
  78.7 1.8 %collective-permute-start.22 = (bf16[128,512]{1,0:T(8,128)(2,1)S(1)}, bf16[128,512]{1,0:T(8,128)(2,1)S(1)}, u32[]{:S(2)}, u32[]{:S(2)}) collective-permute-start(bf16[128,512]{1,0:T(8,128)(2,1)S(1)} %add_convert_fusion.4.refs_5_), channel_id=1, source_target_pairs={{0,4},{4,8},{8,12},{12,16},{16,20},{20,24},{24,28},{1,5},{5,9},{9,... | collective-permute-start | bytes 393224 | tf_op jit(solution)/shard_map/value_halo/ppermute | solution.py:49
  80.5 2.9 %collective-permute-start.21 = (bf16[128,512]{1,0:T(8,128)(2,1)S(1)}, bf16[128,512]{1,0:T(8,128)(2,1)S(1)}, u32[]{:S(2)}, u32[]{:S(2)}) collective-permute-start(bf16[128,512]{1,0:T(8,128)(2,1)S(1)} %add_convert_fusion.4.refs_5_), channel_id=1, source_target_pairs={{0,8},{4,12},{8,16},{12,20},{16,24},{20,28},{1,9},{5,13},{9,17},{1... | collective-permute-start | bytes 393224 | tf_op jit(solution)/shard_map/value_halo/ppermute | solution.py:49
  83.4 4.3 %input_grad.1 = (bf16[128,8192]{1,0:T(8,128)(2,1)}, bf16[128,4096]{1,0:T(8,128)(2,1)S(1)}) custom-call(s32[2]{0:T(128)S(1)} %pad_add_fusion.me_ref, bf16[128,512]{1,0:T(8,128)(2,1)S(1)} %add_convert_fusion.5.mine_ref, bf16[128,512]{1,0:T(8,128)(2,1)S(1)} %collective-permute-done.16.theirs_ref, bf16[256,16]{1,0:T(8,128)(2,1)S(1)} %get-tuple-element.138.rank_ref, ...), custom_call_target="tpu_custom_call" | custom-call | flops 1 | bytes 1 | tf_op jit(solution)/shard_map/input_grad/pallas_call | solution.py:529
  87.7 1.8 %collective-permute-start.24 = (bf16[16,4608]{1,0:T(8,128)(2,1)S(1)}, bf16[16,4608]{1,0:T(8,128)(2,1)S(1)}, u32[]{:S(2)}, u32[]{:S(2)}) collective-permute-start(bf16[16,4608]{1,0:T(8,128)(2,1)S(1)} %add_convert_fusion), channel_id=1, source_target_pairs={{0,8},{4,12},{8,0},{12,4},{16,24},{20,28},{24,16},{28,20},{1,9},{5... | collective-permute-start | bytes 442376 | tf_op jit(solution)/shard_map/adapter_sum/ppermute | solution.py:43
  89.5 4.3 %scores_grad.1 = (bf16[128,4096]{1,0:T(8,128)(2,1)}, bf16[128,512]{1,0:T(8,128)(2,1)S(1)}, bf16[128,512]{1,0:T(8,128)(2,1)S(1)}, f32[128,512]{1,0:T(8,128)S(1)}) custom-call(bf16[4,256,1024]{2,1,0:T(8,128)(2,1)S(1)} %get-tuple-element.150.p_ref, bf16[128,4096]{1,0:T(8,128)(2,1)S(1)} %bitcast.11, bf16[128,4096]{1,0:T(8,128)(2,1)S(1)} %bitcast.13, ...), custom_call_target="tpu_custom_call" | custom-call | flops 1 | bytes 1 | tf_op jit(solution)/shard_map/scores_grad/pallas_call | solution.py:237
  100.6 4.2 %collective-permute-done.26 = bf16[128,512]{1,0:T(8,128)(2,1)S(1)} collective-permute-done((bf16[128,512]{1,0:T(8,128)(2,1)S(1)}, bf16[128,512]{1,0:T(8,128)(2,1)S(1)}, u32[]{:S(2)}, u32[]{:S(2)}) %collective-permute-start.26) | collective-permute-done | bytes 131104 | tf_op jit(solution)/shard_map/key_grad_halo/ppermute | solution.py:49
  (71 shorter events, 27.9 us)
Async XLA Ops:
  4.3 19.6 %collective-permute-start.4 = (bf16[128,4096]{1,0:T(8,128)(2,1)S(1)}, bf16[128,4096]{1,0:T(8,128)(2,1)S(1)}, u32[]{:S(2)}, u32[]{:S(2)}) collective-permute-start(bf16[128,4096]{1,0:T(8,128)(2,1)S(1)} %get-tuple-element.92), channel_id=1, source_target_pairs={{0,4},{4,0},{8,12},{12,8},{16,20},{20,16},{24,28},{28,24},{1,5},{5... | collective-permute-start | bytes 3145736 | tf_op jit(solution)/shard_map/x_core/ppermute | solution.py:43
  4.8 19.1 %collective-permute-start.1 = (bf16[256,512]{1,0:T(8,128)(2,1)S(1)}, bf16[256,512]{1,0:T(8,128)(2,1)S(1)}, u32[]{:S(2)}, u32[]{:S(2)}) collective-permute-start(bf16[256,512]{1,0:T(8,128)(2,1)S(1)} %constant_dynamic-slice_fusion), channel_id=1, source_target_pairs={{0,3},{1,0},{2,1},{3,2},{4,7},{5,4},{6,5},{7,6},{8,11},{9,8},{10,9... | collective-permute-start | bytes 786440 | tf_op jit(solution)/shard_map/weight_ring/ppermute | solution.py:55
  9.4 14.4 %collective-permute-start = (bf16[256,512]{1,0:T(8,128)(2,1)S(1)}, bf16[256,512]{1,0:T(8,128)(2,1)S(1)}, u32[]{:S(2)}, u32[]{:S(2)}) collective-permute-start(bf16[256,512]{1,0:T(8,128)(2,1)S(1)} %constant_dynamic-slice_fusion), channel_id=1, source_target_pairs={{0,1},{1,2},{2,3},{3,0},{4,5},{5,6},{6,7},{7,4},{8,9},{9,10},{10,1... | collective-permute-start | bytes 786440 | tf_op jit(solution)/shard_map/weight_ring/ppermute | solution.py:55
  11.5 7.2 %collective-permute-start.2 = (bf16[128,512]{1,0:T(8,128)(2,1)}, bf16[128,512]{1,0:T(8,128)(2,1)S(1)}, u32[]{:S(2)}, u32[]{:S(2)}) collective-permute-start(bf16[128,512]{1,0:T(8,128)(2,1)} %bitcast.16), channel_id=1, source_target_pairs={{0,8},{4,12},{8,16},{12,20},{16,24},{20,28},{1,9},{5,13},{9,17},{1... | collective-permute-start | bytes 393224 | tf_op jit(solution)/shard_map/key_halo/ppermute | solution.py:49
  23.9 10.0 %collective-permute-start.10 = (bf16[128,512]{1,0:T(8,128)(2,1)S(1)}, bf16[128,512]{1,0:T(8,128)(2,1)S(1)}, u32[]{:S(2)}, u32[]{:S(2)}) collective-permute-start(bf16[128,512]{1,0:T(8,128)(2,1)S(1)} %get-tuple-element.95), channel_id=1, source_target_pairs={{4,0},{8,4},{12,8},{16,12},{20,16},{24,20},{28,24},{5,1},{9,5},{13... | collective-permute-start | bytes 393224 | tf_op jit(solution)/shard_map/value_grad_halo/ppermute | solution.py:49
  25.2 9.3 %collective-permute-start.11 = (bf16[128,512]{1,0:T(8,128)(2,1)S(1)}, bf16[128,512]{1,0:T(8,128)(2,1)S(1)}, u32[]{:S(2)}, u32[]{:S(2)}) collective-permute-start(bf16[128,512]{1,0:T(8,128)(2,1)S(1)} %get-tuple-element.96), channel_id=1, source_target_pairs={{8,0},{12,4},{16,8},{20,12},{24,16},{28,20},{9,1},{13,5},{17,9},{2... | collective-permute-start | bytes 393224 | tf_op jit(solution)/shard_map/value_grad_halo/ppermute | solution.py:49
  26.5 11.8 %collective-permute-start.9 = (bf16[256,512]{1,0:T(8,128)(2,1)S(1)}, bf16[256,512]{1,0:T(8,128)(2,1)S(1)}, u32[]{:S(2)}, u32[]{:S(2)}) collective-permute-start(bf16[256,512]{1,0:T(8,128)(2,1)S(1)} %collective-permute-done.1.refs_4_), channel_id=1, source_target_pairs={{0,16},{4,12},{8,24},{12,4},{16,0},{20,28},{24,8},{28,20},{1,17},{... | collective-permute-start | bytes 786440 | tf_op jit(solution)/shard_map/weight_chip_1/ppermute | solution.py:43
  31.7 9.2 %collective-permute-start.8 = (bf16[256,512]{1,0:T(8,128)(2,1)S(1)}, bf16[256,512]{1,0:T(8,128)(2,1)S(1)}, u32[]{:S(2)}, u32[]{:S(2)}) collective-permute-start(bf16[256,512]{1,0:T(8,128)(2,1)S(1)} %collective-permute-done.1.refs_4_), channel_id=1, source_target_pairs={{0,8},{4,20},{8,0},{12,28},{16,24},{20,4},{24,16},{28,12},{1,9},{5... | collective-permute-start | bytes 786440 | tf_op jit(solution)/shard_map/weight_chip_0/ppermute | solution.py:43
  33.8 10.2 %collective-permute-start.7 = (bf16[256,512]{1,0:T(8,128)(2,1)S(1)}, bf16[256,512]{1,0:T(8,128)(2,1)S(1)}, u32[]{:S(2)}, u32[]{:S(2)}) collective-permute-start(bf16[256,512]{1,0:T(8,128)(2,1)S(1)} %collective-permute-done.refs_0_), channel_id=1, source_target_pairs={{0,16},{4,12},{8,24},{12,4},{16,0},{20,28},{24,8},{28,20},{1,17},{... | collective-permute-start | bytes 786440 | tf_op jit(solution)/shard_map/weight_chip_1/ppermute | solution.py:43
  33.8 11.6 %collective-permute-start.6 = (bf16[256,512]{1,0:T(8,128)(2,1)S(1)}, bf16[256,512]{1,0:T(8,128)(2,1)S(1)}, u32[]{:S(2)}, u32[]{:S(2)}) collective-permute-start(bf16[256,512]{1,0:T(8,128)(2,1)S(1)} %collective-permute-done.refs_0_), channel_id=1, source_target_pairs={{0,8},{4,20},{8,0},{12,28},{16,24},{20,4},{24,16},{28,12},{1,9},{5... | collective-permute-start | bytes 786440 | tf_op jit(solution)/shard_map/weight_chip_0/ppermute | solution.py:43
  34.4 11.1 %collective-permute-start.5 = (bf16[256,512]{1,0:T(8,128)(2,1)S(1)}, bf16[256,512]{1,0:T(8,128)(2,1)S(1)}, u32[]{:S(2)}, u32[]{:S(2)}) collective-permute-start(bf16[256,512]{1,0:T(8,128)(2,1)S(1)} %collective-permute-done.refs_0_), channel_id=1, source_target_pairs={{0,1},{1,2},{2,3},{3,0},{4,5},{5,6},{6,7},{7,4},{8,9},{9,10},{10,1... | collective-permute-start | bytes 786440 | tf_op jit(solution)/shard_map/weight_ring/ppermute | solution.py:55
  48.0 9.1 %collective-permute-start.17 = (f32[16,4608]{1,0:T(8,128)S(1)}, f32[16,4608]{1,0:T(8,128)S(1)}, u32[]{:S(2)}, u32[]{:S(2)}) collective-permute-start(f32[16,4608]{1,0:T(8,128)S(1)} %get-tuple-element.113), channel_id=1, source_target_pairs={{0,1},{1,0},{2,3},{3,2},{4,5},{5,4},{6,7},{7,6},{8,9},{9,8},{10,11... | collective-permute-start | bytes 884744 | tf_op jit(solution)/shard_map/adapter_sum/ppermute | solution.py:43
  48.1 15.6 %collective-permute-start.14 = (bf16[256,512]{1,0:T(8,128)(2,1)S(1)}, bf16[256,512]{1,0:T(8,128)(2,1)S(1)}, u32[]{:S(2)}, u32[]{:S(2)}) collective-permute-start(bf16[256,512]{1,0:T(8,128)(2,1)S(1)} %collective-permute-done.5.refs_0_.refs_8_), channel_id=1, source_target_pairs={{0,16},{4,12},{8,24},{12,4},{16,0},{20,28},{24,8},{28,20},{1,17},{... | collective-permute-start | bytes 786440 | tf_op jit(solution)/shard_map/weight_chip_1/ppermute | solution.py:43
  50.9 12.8 %collective-permute-start.13 = (bf16[256,512]{1,0:T(8,128)(2,1)S(1)}, bf16[256,512]{1,0:T(8,128)(2,1)S(1)}, u32[]{:S(2)}, u32[]{:S(2)}) collective-permute-start(bf16[256,512]{1,0:T(8,128)(2,1)S(1)} %collective-permute-done.5.refs_0_.refs_8_), channel_id=1, source_target_pairs={{0,8},{4,20},{8,0},{12,28},{16,24},{20,4},{24,16},{28,12},{1,9},{5... | collective-permute-start | bytes 786440 | tf_op jit(solution)/shard_map/weight_chip_0/ppermute | solution.py:43
  51.5 9.4 %collective-permute-start.12 = (bf16[256,512]{1,0:T(8,128)(2,1)S(1)}, bf16[256,512]{1,0:T(8,128)(2,1)S(1)}, u32[]{:S(2)}, u32[]{:S(2)}) collective-permute-start(bf16[256,512]{1,0:T(8,128)(2,1)S(1)} %collective-permute-done.6.refs_1_), channel_id=1, source_target_pairs={{0,16},{4,12},{8,24},{12,4},{16,0},{20,28},{24,8},{28,20},{1,17},{... | collective-permute-start | bytes 786440 | tf_op jit(solution)/shard_map/weight_chip_1/ppermute | solution.py:43
  52.9 10.8 %collective-permute-start.15 = (bf16[256,512]{1,0:T(8,128)(2,1)S(1)}, bf16[256,512]{1,0:T(8,128)(2,1)S(1)}, u32[]{:S(2)}, u32[]{:S(2)}) collective-permute-start(bf16[256,512]{1,0:T(8,128)(2,1)S(1)} %collective-permute-done.8.refs_5_), channel_id=1, source_target_pairs={{0,16},{4,12},{8,24},{12,4},{16,0},{20,28},{24,8},{28,20},{1,17},{... | collective-permute-start | bytes 786440 | tf_op jit(solution)/shard_map/weight_chip_1/ppermute | solution.py:43
  63.7 10.5 %collective-permute-start.19 = (bf16[16,4608]{1,0:T(8,128)(2,1)S(1)}, bf16[16,4608]{1,0:T(8,128)(2,1)S(1)}, u32[]{:S(2)}, u32[]{:S(2)}) collective-permute-start(bf16[16,4608]{1,0:T(8,128)(2,1)S(1)} %add_convert_fusion.2), channel_id=1, source_target_pairs={{0,2},{1,3},{2,0},{3,1},{4,6},{5,7},{6,4},{7,5},{8,10},{9,11},{10,... | collective-permute-start | bytes 442376 | tf_op jit(solution)/shard_map/adapter_sum/ppermute | solution.py:43
  67.6 6.6 %collective-permute-start.18 = (bf16[256,512]{1,0:T(8,128)(2,1)S(1)}, bf16[256,512]{1,0:T(8,128)(2,1)S(1)}, u32[]{:S(2)}, u32[]{:S(2)}) collective-permute-start(bf16[256,512]{1,0:T(8,128)(2,1)S(1)} %collective-permute-done.13.refs_1_.refs_9_), channel_id=1, source_target_pairs={{0,16},{4,12},{8,24},{12,4},{16,0},{20,28},{24,8},{28,20},{1,17},{... | collective-permute-start | bytes 786440 | tf_op jit(solution)/shard_map/weight_chip_1/ppermute | solution.py:43
  77.0 10.7 %collective-permute-start.23 = (bf16[16,4608]{1,0:T(8,128)(2,1)S(1)}, bf16[16,4608]{1,0:T(8,128)(2,1)S(1)}, u32[]{:S(2)}, u32[]{:S(2)}) collective-permute-start(bf16[16,4608]{1,0:T(8,128)(2,1)S(1)} %add_convert_fusion.1), channel_id=1, source_target_pairs={{0,16},{4,20},{8,24},{12,28},{16,0},{20,4},{24,8},{28,12},{1,17},{... | collective-permute-start | bytes 442376 | tf_op jit(solution)/shard_map/adapter_sum/ppermute | solution.py:43
  78.7 9.0 %collective-permute-start.22 = (bf16[128,512]{1,0:T(8,128)(2,1)S(1)}, bf16[128,512]{1,0:T(8,128)(2,1)S(1)}, u32[]{:S(2)}, u32[]{:S(2)}) collective-permute-start(bf16[128,512]{1,0:T(8,128)(2,1)S(1)} %add_convert_fusion.4.refs_5_), channel_id=1, source_target_pairs={{0,4},{4,8},{8,12},{12,16},{16,20},{20,24},{24,28},{1,5},{5,9},{9,... | collective-permute-start | bytes 393224 | tf_op jit(solution)/shard_map/value_halo/ppermute | solution.py:49
  80.5 7.2 %collective-permute-start.21 = (bf16[128,512]{1,0:T(8,128)(2,1)S(1)}, bf16[128,512]{1,0:T(8,128)(2,1)S(1)}, u32[]{:S(2)}, u32[]{:S(2)}) collective-permute-start(bf16[128,512]{1,0:T(8,128)(2,1)S(1)} %add_convert_fusion.4.refs_5_), channel_id=1, source_target_pairs={{0,8},{4,12},{8,16},{12,20},{16,24},{20,28},{1,9},{5,13},{9,17},{1... | collective-permute-start | bytes 393224 | tf_op jit(solution)/shard_map/value_halo/ppermute | solution.py:49
  87.7 6.7 %collective-permute-start.24 = (bf16[16,4608]{1,0:T(8,128)(2,1)S(1)}, bf16[16,4608]{1,0:T(8,128)(2,1)S(1)}, u32[]{:S(2)}, u32[]{:S(2)}) collective-permute-start(bf16[16,4608]{1,0:T(8,128)(2,1)S(1)} %add_convert_fusion), channel_id=1, source_target_pairs={{0,8},{4,12},{8,0},{12,4},{16,24},{20,28},{24,16},{28,20},{1,9},{5... | collective-permute-start | bytes 442376 | tf_op jit(solution)/shard_map/adapter_sum/ppermute | solution.py:43
  95.0 5.5 %collective-permute-start.25 = (bf16[128,512]{1,0:T(8,128)(2,1)S(1)}, bf16[128,512]{1,0:T(8,128)(2,1)S(1)}, u32[]{:S(2)}, u32[]{:S(2)}) collective-permute-start(bf16[128,512]{1,0:T(8,128)(2,1)S(1)} %get-tuple-element.157), channel_id=1, source_target_pairs={{4,0},{8,4},{12,8},{16,12},{20,16},{24,20},{28,24},{5,1},{9,5},{13... | collective-permute-start | bytes 393224 | tf_op jit(solution)/shard_map/key_grad_halo/ppermute | solution.py:49
  96.3 8.4 %collective-permute-start.26 = (bf16[128,512]{1,0:T(8,128)(2,1)S(1)}, bf16[128,512]{1,0:T(8,128)(2,1)S(1)}, u32[]{:S(2)}, u32[]{:S(2)}) collective-permute-start(bf16[128,512]{1,0:T(8,128)(2,1)S(1)} %get-tuple-element.158), channel_id=1, source_target_pairs={{8,0},{12,4},{16,8},{20,12},{24,16},{28,20},{9,1},{13,5},{17,9},{2... | collective-permute-start | bytes 393224 | tf_op jit(solution)/shard_map/key_grad_halo/ppermute | solution.py:49
  (14 other events, 137.7 us)

commit v3 on v2

--- a/solution.py
+++ b/solution.py
@@ -586,11 +586,13 @@
 
 
 def sum_steps(seq_count, fsdp_count):
-    steps, bit = [], 1
-    while bit < fsdp_count:
-        steps.append(("fsdp", bit))
-        bit *= 2
-    return steps + [("seq", bit) for bit in chip_bits(seq_count)[::-1]]
+    ring = [("fsdp", 1 << b) for b in range(fsdp_count.bit_length() - 1)]
+    chips = [("seq", bit) for bit in chip_bits(seq_count)[::-1]]
+    steps = []
+    while ring or chips:
+        steps += ring[:1] + chips[:1]
+        ring, chips = ring[1:], chips[1:]
+    return steps
 
 
 def sum_step(low, step, keep=False):
@@ -681,82 +683,80 @@
     pieces = Pieces(half, seq_count, fsdp_count)
     ring = ring_order(fsdp_count)
 
-    first_row = (here % 2) * half + (here // 2) * part_rows
-    arrived = {0: lax.dynamic_slice_in_dim(w, first_row, part_rows, 0)}
-    to_come = list(ring)
-    held = {}
-
-    def ring_step(count):
-        for by in to_come[:count]:
+    chips = seq_count // 2
+    direct = chips == 4
+
+    def part_of(chip):
+        first_row = (here % 2) * half + chip * part_rows
+        return lax.dynamic_slice_in_dim(w, first_row, part_rows, 0)
+
+    def ring_step(known, bys, name):
+        for by in bys:
             upward = 2 * by <= fsdp_count
             source = by - 1 if upward else (by + 1) % fsdp_count
-            arrived[by] = turn(arrived[source], "fsdp", 1 if upward else -1)
-        del to_come[:count]
-
-    def advance(bys=ring):
-        for by in list(held):
-            held[by] = spread_step(held[by]) or held[by]
-        for by in ring:
-            if by in bys and by in ready and by not in held:
-                held[by] = spread_step([arrived[by]]) or [arrived[by]]
-
-    ready = set()
-
-    ring_step(2)
+            known[by] = turn(known[source], "fsdp", 1 if upward else -1, name)
+
+    def set_out(bys):
+        for by in bys:
+            held[by] = spread_step([arrived[by]]) or [arrived[by]]
+
+    held = {}
+    arrived = {0: part_of(here // 2)}
+    across = {0: part_of(here // 2 ^ 3)} if direct else {}
+
+    ring_step(arrived, ring[:2], "weight_ring")
     arrived[0], x = after((arrived[0], x))
     key_blocks = [shift(k, "seq", by, "key_halo") for by in range(back, 0, -1)] + [k]
     x_mine, x_sent = x_halves_call(me, x, fsdp_count)
     x_theirs = swap(x_sent, "x_core")
     probs, dv_blocks = probs_call(me, packed_document_lengths, q, o, key_blocks)
-    arrived, dv_blocks, x_theirs = after((arrived, dv_blocks, x_theirs))
-    ready.update(by for by in arrived if by)
+    arrived, across, dv_blocks, x_theirs = after((arrived, across, dv_blocks, x_theirs))
 
     dv_back = [
         shift(dv_blocks[back - by], "seq", -by, "value_grad_halo") for by in range(1, back + 1)
     ]
-    advance()
-    ring_step(1)
+    if direct:
+        set_out(ring[:1])
+        ring_step(across, ring[:1], "weight_ring_across")
     acc, low = own_values_call(me, x_mine, x_theirs, down, up, w)
-    arrived, held, dv_back, acc, low = after((arrived, held, dv_back, acc, low))
-    ready.update(by for by in arrived if by)
+    held, across, dv_back, acc, low = after((held, across, dv_back, acc, low))
+
+    if direct:
+        set_out(ring[1:2])
+    ring_step(arrived, ring[2:], "weight_ring")
+    dv = dv_blocks[back]
+    for block in dv_back:
+        dv = dv + block.astype(F32)
+    dv_mine = dv.astype(BF16)
+    dv_theirs = swap(dv_mine, "value_grad_core")
+    scale = 1.0 / (tokens * seq_count * fsdp_count)
+    rank_grad, sums = adapter_grad_call(dv_mine, dv_theirs, up, low, x_mine, x_theirs, scale)
+    arrived, held, sums = after((arrived, held, sums))
 
     steps = sum_steps(seq_count, fsdp_count)
-    used = {}
-    chips = seq_count // 2
-    sums = None
-
-    def complete():
-        return {by: held[by] for by in ring if by in held and len(held[by]) == chips}
+    if direct:
+        set_out(ring[2:])
+        ring_step(across, ring[2:], "weight_ring_across")
+        held = {
+            by: held[by] + [across[by]] if by in across else spread_step(held[by]) for by in ring
+        }
+    else:
+        set_out(ring)
+    if len(steps) > 3:
+        sums = sum_step(sums, steps.pop(0))
+    held, acc, sums = after((held, acc, sums))
+    while any(len(parts) < chips for parts in held.values()):
+        held = after({by: spread_step(parts) for by, parts in held.items()})
 
     def arrays_of(parts):
         if pieces.by_parts:
             return parts
         return {by: natural_half(parts[by], pieces.order, here) for by in parts}
 
-    while sums is None or len(complete()) < len(ring):
-        done = {by: parts for by, parts in complete().items() if by not in used}
-        advance()
-        ring_step(1)
-        if sums is None:
-            dv = dv_blocks[back]
-            for block in dv_back:
-                dv = dv + block.astype(F32)
-            dv_mine = dv.astype(BF16)
-            dv_theirs = swap(dv_mine, "value_grad_core")
-            scale = 1.0 / (tokens * seq_count * fsdp_count)
-            rank_grad, sums = adapter_grad_call(
-                dv_mine, dv_theirs, up, low, x_mine, x_theirs, scale
-            )
-        if len(steps) > 2:
-            sums = sum_step(sums, steps.pop(0))
-        if done and len(done) == len(ring) - 1:
-            acc = more_values_call(me, x_mine, x_theirs, acc, arrays_of(done), pieces, False)
-            used.update(done)
-        arrived, held, acc, sums = after((arrived, held, acc, sums))
-        ready.update(by for by in arrived if by)
-    rest = {by: held[by] for by in ring if by not in used}
+    if len(steps) > 2:
+        sums = sum_step(sums, steps.pop(0))
     values, values_sent = more_values_call(
-        me, x_mine, x_theirs, acc, arrays_of(rest), pieces, True
+        me, x_mine, x_theirs, acc, arrays_of(held), pieces, True
     )
 
     values = (values + swap(values_sent, "values_core")).astype(BF16)
@@ -765,7 +765,7 @@
     while len(steps) > 1:
         sums = sum_step(sums, steps.pop(0))
     input_grad, input_grad_sent = input_grad_call(
-        me, dv_mine, dv_theirs, rank_grad, down, w, arrays_of(complete()), pieces
+        me, dv_mine, dv_theirs, rank_grad, down, w, arrays_of(held), pieces
     )
     value_blocks, sums, input_grad_sent = after((value_blocks, sums, input_grad_sent))
 

time: 106 us -> 96.8 us (0.913)
  waiting for transfers between devices: 33.1 us -> 25.8 us
  starting transfers between devices: 42.9 us -> 41.8 us
    ppermute x18 -> x16, waiting for transfers between devices: 24.7 us -> 7.05 us  [flip(): return lax.ppermute(value, axis, [(i, i ^ choose(i)) for i in range(size)])]
    ppermute x3 -> x5, waiting for transfers between devices: 0.01 us -> 10.8 us  [turn(): lax.ppermute(value, axis, [(i, (i + by) % size) for i in range(size)])]
    ppermute x18 -> x16, starting transfers between devices: 23 us -> 18.1 us  [flip(): return lax.ppermute(value, axis, [(i, i ^ choose(i)) for i in range(size)])]
    ppermute x3 -> x5, starting transfers between devices: 4.67 us -> 7.83 us  [turn(): lax.ppermute(value, axis, [(i, (i + by) % size) for i in range(size)])]
    pallas_call x2 -> x1, Pallas kernels: 2.78 us -> 2.07 us  [more_values_call(): pl.pallas_call(kernel, in_specs=[smem(), vmem()] + [hbm()] * (2 + len(arr...]
  transfers between devices with their start and end apart: 29 -> 29, of which waited for: 14 -> 9; matrix products, arithmetic and copies ran while one was open for 0% -> 0% of each run, Pallas kernels for 19% -> 22%
where the time goes in v3:
time: 96.8 us; the launch traced here: 96.4 us
  starting transfers between devices  41.8 us (43%)
  waiting for transfers between devices  25.8 us (27%)
  Pallas kernels  22.4 us (23%)
  local copies, waits for them, and re-layouts  4.39 us (5%)
  other arithmetic  1.01 us (1%)
  between operations  1 us (1%)
    ppermute x16, starting transfers between devices, flip(): return lax.ppermute(value, axis, [(i, i ^ choose(i)) for i in range(size)])  18.1 us
    ppermute x8, starting transfers between devices, shift(): lax.ppermute(value, axis, [(i, i + by) for i in range(size) if 0 <= i + b...  15.9 us
    ppermute x5, waiting for transfers between devices, turn(): lax.ppermute(value, axis, [(i, (i + by) % size) for i in range(size)])  10.8 us
    ppermute x8, waiting for transfers between devices, shift(): lax.ppermute(value, axis, [(i, i + by) for i in range(size) if 0 <= i + b...  7.95 us
    ppermute x5, starting transfers between devices, turn(): lax.ppermute(value, axis, [(i, (i + by) % size) for i in range(size)])  7.83 us
    ppermute x16, waiting for transfers between devices, flip(): return lax.ppermute(value, axis, [(i, i ^ choose(i)) for i in range(size)])  7.05 us
    pallas_call x1, Pallas kernels, scores_grad_call(): pl.pallas_call(kernel, grid=(KEY_VALUE_HEADS // HEADS_A_STEP,), in_specs=...  4.32 us
    pallas_call x1, Pallas kernels, input_grad_call(): pl.pallas_call(kernel, in_specs=[smem(), vmem(), vmem(), vmem()] + [hbm()...  4.29 us
  transfers between devices with their start and end apart: 29, of which 9 were waited for; matrix products, arithmetic and copies ran while one was open for 0% of the time, Pallas kernels for 22%

profile of v3, /device:TPU:0, one launch (start us, length us, event | category | flops | bytes accessed | tf_op | source)
XLA Modules:
  0.0 96.4 jit_solution(1339621307067151238)
XLA Ops:
  2.0 1.6 %copy-done.3 = bf16[1,128,8192]{2,1,0:T(8,128)(2,1)S(1)} copy-done((bf16[1,128,8192]{2,1,0:T(8,128)(2,1)S(1)}, bf16[1,128,8192]{2,1,0:T(8,128)(2,1)}, u32[]{:S(2)}) %copy-start.3) | copy-done | bytes 2097176
  4.9 4.7 %collective-permute-start.1 = (bf16[256,512]{1,0:T(8,128)(2,1)S(1)}, bf16[256,512]{1,0:T(8,128)(2,1)S(1)}, u32[]{:S(2)}, u32[]{:S(2)}) collective-permute-start(bf16[256,512]{1,0:T(8,128)(2,1)S(1)} %get-tuple-element.158), channel_id=1, source_target_pairs={{0,3},{1,0},{2,1},{3,2},{4,7},{5,4},{6,5},{7,6},{8,11},{9,8},{10,9... | collective-permute-start | bytes 786440 | tf_op jit(solution)/shard_map/weight_ring/ppermute | solution.py:55
  9.6 2.1 %collective-permute-start.3 = (bf16[128,512]{1,0:T(8,128)(2,1)}, bf16[128,512]{1,0:T(8,128)(2,1)S(1)}, u32[]{:S(2)}, u32[]{:S(2)}) collective-permute-start(bf16[128,512]{1,0:T(8,128)(2,1)} %bitcast.15), channel_id=1, source_target_pairs={{0,4},{4,8},{8,12},{12,16},{16,20},{20,24},{24,28},{1,5},{5,9},{9,... | collective-permute-start | bytes 393224 | tf_op jit(solution)/shard_map/key_halo/ppermute | solution.py:49
  11.6 3.4 %collective-permute-start.2 = (bf16[128,512]{1,0:T(8,128)(2,1)}, bf16[128,512]{1,0:T(8,128)(2,1)S(1)}, u32[]{:S(2)}, u32[]{:S(2)}) collective-permute-start(bf16[128,512]{1,0:T(8,128)(2,1)} %bitcast.16), channel_id=1, source_target_pairs={{0,8},{4,12},{8,16},{12,20},{16,24},{20,28},{1,9},{5,13},{9,17},{1... | collective-permute-start | bytes 393224 | tf_op jit(solution)/shard_map/key_halo/ppermute | solution.py:49
  15.0 3.8 %collective-permute-done.2.refs_0_ = bf16[128,512]{1,0:T(8,128)(2,1)S(1)} collective-permute-done((bf16[128,512]{1,0:T(8,128)(2,1)}, bf16[128,512]{1,0:T(8,128)(2,1)S(1)}, u32[]{:S(2)}, u32[]{:S(2)}) %collective-permute-start.2) | collective-permute-done | bytes 131104 | tf_op jit(solution)/shard_map/key_halo/ppermute | solution.py:49
  20.4 3.5 %probs.1 = (bf16[4,256,1024]{2,1,0:T(8,128)(2,1)S(1)}, bf16[128,512]{1,0:T(8,128)(2,1)S(1)}, bf16[128,512]{1,0:T(8,128)(2,1)S(1)}, f32[128,512]{1,0:T(8,128)S(1)}) custom-call(s32[2]{0:T(128)S(1)} %pad_add_fusion.me_ref, s32[1,8]{1,0:T(1,128)S(1)} %copy-done.8, bf16[128,4096]{1,0:T(8,128)(2,1)S(1)} %bitcast.10, bf16[128,4096]{1,0:T(8,128)(2,1)S(1)} %bitcast.12, ...), custom_call_target="tpu_custom_call" | custom-call | flops 1 | bytes 1 | tf_op jit(solution)/shard_map/probs/pallas_call | solution.py:187
  24.0 3.4 %collective-permute-start.7 = (bf16[256,512]{1,0:T(8,128)(2,1)S(1)}, bf16[256,512]{1,0:T(8,128)(2,1)S(1)}, u32[]{:S(2)}, u32[]{:S(2)}) collective-permute-start(bf16[256,512]{1,0:T(8,128)(2,1)S(1)} %collective-permute-done.refs_0_), channel_id=1, source_target_pairs={{0,16},{4,12},{8,24},{12,4},{16,0},{20,28},{24,8},{28,20},{1,17},{... | collective-permute-start | bytes 786440 | tf_op jit(solution)/shard_map/weight_chip_1/ppermute | solution.py:43
  30.3 3.4 %own_values.1 = (f32[256,512]{1,0:T(8,128)S(1)}, f32[256,16]{1,0:T(8,128)S(1)}) custom-call(s32[2]{0:T(128)S(1)} %pad_add_fusion.me_ref, bf16[128,4096]{1,0:T(8,128)(2,1)S(1)} %get-tuple-element.91.mine_hbm.x_mine_hbm, bf16[128,4096]{1,0:T(8,128)(2,1)S(1)} %collective-permute-done.4.theirs_hbm.x_theirs_hbm, bf16[16,8192]{1,0:T(8,128)(2,1)S(1)} %copy-done.4, ...), custom_call_target="tpu_custom_call" | custom-call | flops 1 | bytes 1 | tf_op jit(solution)/shard_map/own_values/pallas_call | solution.py:373
  33.7 4.5 %collective-permute-start.12 = (bf16[256,512]{1,0:T(8,128)(2,1)S(1)}, bf16[256,512]{1,0:T(8,128)(2,1)S(1)}, u32[]{:S(2)}, u32[]{:S(2)}) collective-permute-start(bf16[256,512]{1,0:T(8,128)(2,1)S(1)} %collective-permute-done.1.refs_8_), channel_id=1, source_target_pairs={{0,16},{4,12},{8,24},{12,4},{16,0},{20,28},{24,8},{28,20},{1,17},{... | collective-permute-start | bytes 786440 | tf_op jit(solution)/shard_map/weight_chip_1/ppermute | solution.py:43
  38.3 1.8 %collective-permute-start.11 = (bf16[256,512]{1,0:T(8,128)(2,1)S(1)}, bf16[256,512]{1,0:T(8,128)(2,1)S(1)}, u32[]{:S(2)}, u32[]{:S(2)}) collective-permute-start(bf16[256,512]{1,0:T(8,128)(2,1)S(1)} %collective-permute-done.1.refs_8_), channel_id=1, source_target_pairs={{0,8},{4,20},{8,0},{12,28},{16,24},{20,4},{24,16},{28,12},{1,9},{5... | collective-permute-start | bytes 786440 | tf_op jit(solution)/shard_map/weight_chip_0/ppermute | solution.py:43
  45.1 3.4 %collective-permute-done.5.refs_4_ = bf16[256,512]{1,0:T(8,128)(2,1)S(1)} collective-permute-done((bf16[256,512]{1,0:T(8,128)(2,1)S(1)}, bf16[256,512]{1,0:T(8,128)(2,1)S(1)}, u32[]{:S(2)}, u32[]{:S(2)}) %collective-permute-start.5) | collective-permute-done | bytes 262176 | tf_op jit(solution)/shard_map/weight_ring/ppermute | solution.py:55
  48.6 1.9 %collective-permute-start.16 = (bf16[256,512]{1,0:T(8,128)(2,1)S(1)}, bf16[256,512]{1,0:T(8,128)(2,1)S(1)}, u32[]{:S(2)}, u32[]{:S(2)}) collective-permute-start(bf16[256,512]{1,0:T(8,128)(2,1)S(1)} %collective-permute-done.8.refs_3_), channel_id=1, source_target_pairs={{0,1},{1,2},{2,3},{3,0},{4,5},{5,6},{6,7},{7,4},{8,9},{9,10},{10,1... | collective-permute-start | bytes 786440 | tf_op jit(solution)/shard_map/weight_ring_across/ppermute | solution.py:55
  51.6 2.1 %collective-permute-start.14 = (bf16[256,512]{1,0:T(8,128)(2,1)S(1)}, bf16[256,512]{1,0:T(8,128)(2,1)S(1)}, u32[]{:S(2)}, u32[]{:S(2)}) collective-permute-start(bf16[256,512]{1,0:T(8,128)(2,1)S(1)} %collective-permute-done.5.refs_4_), channel_id=1, source_target_pairs={{0,8},{4,20},{8,0},{12,28},{16,24},{20,4},{24,16},{28,12},{1,9},{5... | collective-permute-start | bytes 786440 | tf_op jit(solution)/shard_map/weight_chip_0/ppermute | solution.py:43
  54.3 1.8 %collective-permute-done.18 = f32[16,4608]{1,0:T(8,128)S(1)} collective-permute-done((f32[16,4608]{1,0:T(8,128)S(1)}, f32[16,4608]{1,0:T(8,128)S(1)}, u32[]{:S(2)}, u32[]{:S(2)}) %collective-permute-start.18) | collective-permute-done | bytes 294944 | tf_op jit(solution)/shard_map/adapter_sum/ppermute | solution.py:43
  56.1 7.4 %collective-permute-done.16.refs_7_ = bf16[256,512]{1,0:T(8,128)(2,1)S(1)} collective-permute-done((bf16[256,512]{1,0:T(8,128)(2,1)S(1)}, bf16[256,512]{1,0:T(8,128)(2,1)S(1)}, u32[]{:S(2)}, u32[]{:S(2)}) %collective-permute-start.16) | collective-permute-done | bytes 262176 | tf_op jit(solution)/shard_map/weight_ring_across/ppermute | solution.py:55
  64.7 2.1 %more_values.1 = (f32[128,512]{1,0:T(8,128)S(1)}, f32[128,512]{1,0:T(8,128)S(1)}) custom-call(s32[2]{0:T(128)S(1)} %pad_add_fusion.me_ref, f32[256,512]{1,0:T(8,128)S(1)} %get-tuple-element.113.acc_ref, bf16[128,4096]{1,0:T(8,128)(2,1)S(1)} %get-tuple-element.91.mine_hbm.x_mine_hbm, bf16[128,4096]{1,0:T(8,128)(2,1)S(1)} %collective-permute-done.4.theirs_hbm.x_theirs_hbm, ...), custom_call_target="tpu_custom_call" | custom-call | flops 1 | bytes 1 | tf_op jit(solution)/shard_map/more_values/pallas_call | solution.py:458
  66.8 1.9 %collective-permute-done.20 = bf16[16,4608]{1,0:T(8,128)(2,1)S(1)} collective-permute-done((bf16[16,4608]{1,0:T(8,128)(2,1)S(1)}, bf16[16,4608]{1,0:T(8,128)(2,1)S(1)}, u32[]{:S(2)}, u32[]{:S(2)}) %collective-permute-start.20) | collective-permute-done | bytes 147488 | tf_op jit(solution)/shard_map/adapter_sum/ppermute | solution.py:43
  68.9 1.6 %collective-permute-start.22 = (bf16[128,512]{1,0:T(8,128)(2,1)S(1)}, bf16[128,512]{1,0:T(8,128)(2,1)S(1)}, u32[]{:S(2)}, u32[]{:S(2)}) collective-permute-start(bf16[128,512]{1,0:T(8,128)(2,1)S(1)} %add_convert_fusion.4.refs_5_), channel_id=1, source_target_pairs={{0,4},{4,8},{8,12},{12,16},{16,20},{20,24},{24,28},{1,5},{5,9},{9,... | collective-permute-start | bytes 393224 | tf_op jit(solution)/shard_map/value_halo/ppermute | solution.py:49
  70.5 3.7 %collective-permute-start.21 = (bf16[128,512]{1,0:T(8,128)(2,1)S(1)}, bf16[128,512]{1,0:T(8,128)(2,1)S(1)}, u32[]{:S(2)}, u32[]{:S(2)}) collective-permute-start(bf16[128,512]{1,0:T(8,128)(2,1)S(1)} %add_convert_fusion.4.refs_5_), channel_id=1, source_target_pairs={{0,8},{4,12},{8,16},{12,20},{16,24},{20,28},{1,9},{5,13},{9,17},{1... | collective-permute-start | bytes 393224 | tf_op jit(solution)/shard_map/value_halo/ppermute | solution.py:49
  74.3 4.3 %input_grad.1 = (bf16[128,8192]{1,0:T(8,128)(2,1)}, bf16[128,4096]{1,0:T(8,128)(2,1)S(1)}) custom-call(s32[2]{0:T(128)S(1)} %pad_add_fusion.me_ref, bf16[128,512]{1,0:T(8,128)(2,1)S(1)} %add_convert_fusion.5.mine_ref, bf16[128,512]{1,0:T(8,128)(2,1)S(1)} %collective-permute-done.13.theirs_ref, bf16[256,16]{1,0:T(8,128)(2,1)S(1)} %get-tuple-element.132.rank_ref, ...), custom_call_target="tpu_custom_call" | custom-call | flops 1 | bytes 1 | tf_op jit(solution)/shard_map/input_grad/pallas_call | solution.py:529
  78.6 1.8 %collective-permute-start.24 = (bf16[16,4608]{1,0:T(8,128)(2,1)S(1)}, bf16[16,4608]{1,0:T(8,128)(2,1)S(1)}, u32[]{:S(2)}, u32[]{:S(2)}) collective-permute-start(bf16[16,4608]{1,0:T(8,128)(2,1)S(1)} %add_convert_fusion), channel_id=1, source_target_pairs={{0,8},{4,12},{8,0},{12,4},{16,24},{20,28},{24,16},{28,20},{1,9},{5... | collective-permute-start | bytes 442376 | tf_op jit(solution)/shard_map/adapter_sum/ppermute | solution.py:43
  80.4 4.3 %scores_grad.1 = (bf16[128,4096]{1,0:T(8,128)(2,1)}, bf16[128,512]{1,0:T(8,128)(2,1)S(1)}, bf16[128,512]{1,0:T(8,128)(2,1)S(1)}, f32[128,512]{1,0:T(8,128)S(1)}) custom-call(bf16[4,256,1024]{2,1,0:T(8,128)(2,1)S(1)} %get-tuple-element.136.p_ref, bf16[128,4096]{1,0:T(8,128)(2,1)S(1)} %bitcast.11, bf16[128,4096]{1,0:T(8,128)(2,1)S(1)} %bitcast.13, ...), custom_call_target="tpu_custom_call" | custom-call | flops 1 | bytes 1 | tf_op jit(solution)/shard_map/scores_grad/pallas_call | solution.py:237
  90.0 1.5 %put_half.1 = bf16[128,8192]{1,0:T(8,128)(2,1)} custom-call(s32[2]{0:T(128)S(1)} %pad_add_fusion.me_ref, bf16[128,4096]{1,0:T(8,128)(2,1)S(1)} %collective-permute-done.27.theirs_ref, bf16[128,8192]{1,0:T(8,128)(2,1)} %get-tuple-element.146.out_in), custom_call_target="tpu_custom_call", output_to_operand_aliasing={{}: (2, {})} | custom-call | flops 1 | bytes 1 | tf_op jit(solution)/shard_map/put_half/pallas_call | solution.py:299
  91.6 4.2 %collective-permute-done.26 = bf16[128,512]{1,0:T(8,128)(2,1)S(1)} collective-permute-done((bf16[128,512]{1,0:T(8,128)(2,1)S(1)}, bf16[128,512]{1,0:T(8,128)(2,1)S(1)}, u32[]{:S(2)}, u32[]{:S(2)}) %collective-permute-start.26) | collective-permute-done | bytes 131104 | tf_op jit(solution)/shard_map/key_grad_halo/ppermute | solution.py:49
  (70 shorter events, 21.3 us)
Async XLA Ops:
  4.4 19.6 %collective-permute-start.4 = (bf16[128,4096]{1,0:T(8,128)(2,1)S(1)}, bf16[128,4096]{1,0:T(8,128)(2,1)S(1)}, u32[]{:S(2)}, u32[]{:S(2)}) collective-permute-start(bf16[128,4096]{1,0:T(8,128)(2,1)S(1)} %get-tuple-element.85), channel_id=1, source_target_pairs={{0,4},{4,0},{8,12},{12,8},{16,20},{20,16},{24,28},{28,24},{1,5},{5... | collective-permute-start | bytes 3145736 | tf_op jit(solution)/shard_map/x_core/ppermute | solution.py:43
  4.9 19.1 %collective-permute-start.1 = (bf16[256,512]{1,0:T(8,128)(2,1)S(1)}, bf16[256,512]{1,0:T(8,128)(2,1)S(1)}, u32[]{:S(2)}, u32[]{:S(2)}) collective-permute-start(bf16[256,512]{1,0:T(8,128)(2,1)S(1)} %get-tuple-element.158), channel_id=1, source_target_pairs={{0,3},{1,0},{2,1},{3,2},{4,7},{5,4},{6,5},{7,6},{8,11},{9,8},{10,9... | collective-permute-start | bytes 786440 | tf_op jit(solution)/shard_map/weight_ring/ppermute | solution.py:55
  9.5 14.4 %collective-permute-start = (bf16[256,512]{1,0:T(8,128)(2,1)S(1)}, bf16[256,512]{1,0:T(8,128)(2,1)S(1)}, u32[]{:S(2)}, u32[]{:S(2)}) collective-permute-start(bf16[256,512]{1,0:T(8,128)(2,1)S(1)} %get-tuple-element.158), channel_id=1, source_target_pairs={{0,1},{1,2},{2,3},{3,0},{4,5},{5,6},{6,7},{7,4},{8,9},{9,10},{10,1... | collective-permute-start | bytes 786440 | tf_op jit(solution)/shard_map/weight_ring/ppermute | solution.py:55
  9.6 5.5 %collective-permute-start.3 = (bf16[128,512]{1,0:T(8,128)(2,1)}, bf16[128,512]{1,0:T(8,128)(2,1)S(1)}, u32[]{:S(2)}, u32[]{:S(2)}) collective-permute-start(bf16[128,512]{1,0:T(8,128)(2,1)} %bitcast.15), channel_id=1, source_target_pairs={{0,4},{4,8},{8,12},{12,16},{16,20},{20,24},{24,28},{1,5},{5,9},{9,... | collective-permute-start | bytes 393224 | tf_op jit(solution)/shard_map/key_halo/ppermute | solution.py:49
  11.6 7.2 %collective-permute-start.2 = (bf16[128,512]{1,0:T(8,128)(2,1)}, bf16[128,512]{1,0:T(8,128)(2,1)S(1)}, u32[]{:S(2)}, u32[]{:S(2)}) collective-permute-start(bf16[128,512]{1,0:T(8,128)(2,1)} %bitcast.16), channel_id=1, source_target_pairs={{0,8},{4,12},{8,16},{12,20},{16,24},{20,28},{1,9},{5,13},{9,17},{1... | collective-permute-start | bytes 393224 | tf_op jit(solution)/shard_map/key_halo/ppermute | solution.py:49
  24.0 16.1 %collective-permute-start.8 = (bf16[256,512]{1,0:T(8,128)(2,1)S(1)}, bf16[256,512]{1,0:T(8,128)(2,1)S(1)}, u32[]{:S(2)}, u32[]{:S(2)}) collective-permute-start(bf16[256,512]{1,0:T(8,128)(2,1)S(1)} %get-tuple-element.88), channel_id=1, source_target_pairs={{0,1},{1,2},{2,3},{3,0},{4,5},{5,6},{6,7},{7,4},{8,9},{9,10},{10,1... | collective-permute-start | bytes 786440 | tf_op jit(solution)/shard_map/weight_ring_across/ppermute | solution.py:55
  24.0 17.2 %collective-permute-start.7 = (bf16[256,512]{1,0:T(8,128)(2,1)S(1)}, bf16[256,512]{1,0:T(8,128)(2,1)S(1)}, u32[]{:S(2)}, u32[]{:S(2)}) collective-permute-start(bf16[256,512]{1,0:T(8,128)(2,1)S(1)} %collective-permute-done.refs_0_), channel_id=1, source_target_pairs={{0,16},{4,12},{8,24},{12,4},{16,0},{20,28},{24,8},{28,20},{1,17},{... | collective-permute-start | bytes 786440 | tf_op jit(solution)/shard_map/weight_chip_1/ppermute | solution.py:43
  27.4 13.8 %collective-permute-start.6 = (bf16[256,512]{1,0:T(8,128)(2,1)S(1)}, bf16[256,512]{1,0:T(8,128)(2,1)S(1)}, u32[]{:S(2)}, u32[]{:S(2)}) collective-permute-start(bf16[256,512]{1,0:T(8,128)(2,1)S(1)} %collective-permute-done.refs_0_), channel_id=1, source_target_pairs={{0,8},{4,20},{8,0},{12,28},{16,24},{20,4},{24,16},{28,12},{1,9},{5... | collective-permute-start | bytes 786440 | tf_op jit(solution)/shard_map/weight_chip_0/ppermute | solution.py:43
  27.7 6.0 %collective-permute-start.9 = (bf16[128,512]{1,0:T(8,128)(2,1)S(1)}, bf16[128,512]{1,0:T(8,128)(2,1)S(1)}, u32[]{:S(2)}, u32[]{:S(2)}) collective-permute-start(bf16[128,512]{1,0:T(8,128)(2,1)S(1)} %get-tuple-element.89), channel_id=1, source_target_pairs={{4,0},{8,4},{12,8},{16,12},{20,16},{24,20},{28,24},{5,1},{9,5},{13... | collective-permute-start | bytes 393224 | tf_op jit(solution)/shard_map/value_grad_halo/ppermute | solution.py:49
  29.0 9.3 %collective-permute-start.10 = (bf16[128,512]{1,0:T(8,128)(2,1)S(1)}, bf16[128,512]{1,0:T(8,128)(2,1)S(1)}, u32[]{:S(2)}, u32[]{:S(2)}) collective-permute-start(bf16[128,512]{1,0:T(8,128)(2,1)S(1)} %get-tuple-element.90), channel_id=1, source_target_pairs={{8,0},{12,4},{16,8},{20,12},{24,16},{28,20},{9,1},{13,5},{17,9},{2... | collective-permute-start | bytes 393224 | tf_op jit(solution)/shard_map/value_grad_halo/ppermute | solution.py:49
  33.7 11.4 %collective-permute-start.12 = (bf16[256,512]{1,0:T(8,128)(2,1)S(1)}, bf16[256,512]{1,0:T(8,128)(2,1)S(1)}, u32[]{:S(2)}, u32[]{:S(2)}) collective-permute-start(bf16[256,512]{1,0:T(8,128)(2,1)S(1)} %collective-permute-done.1.refs_8_), channel_id=1, source_target_pairs={{0,16},{4,12},{8,24},{12,4},{16,0},{20,28},{24,8},{28,20},{1,17},{... | collective-permute-start | bytes 786440 | tf_op jit(solution)/shard_map/weight_chip_1/ppermute | solution.py:43
  38.3 6.9 %collective-permute-start.11 = (bf16[256,512]{1,0:T(8,128)(2,1)S(1)}, bf16[256,512]{1,0:T(8,128)(2,1)S(1)}, u32[]{:S(2)}, u32[]{:S(2)}) collective-permute-start(bf16[256,512]{1,0:T(8,128)(2,1)S(1)} %collective-permute-done.1.refs_8_), channel_id=1, source_target_pairs={{0,8},{4,20},{8,0},{12,28},{16,24},{20,4},{24,16},{28,12},{1,9},{5... | collective-permute-start | bytes 786440 | tf_op jit(solution)/shard_map/weight_chip_0/ppermute | solution.py:43
  40.1 8.4 %collective-permute-start.5 = (bf16[256,512]{1,0:T(8,128)(2,1)S(1)}, bf16[256,512]{1,0:T(8,128)(2,1)S(1)}, u32[]{:S(2)}, u32[]{:S(2)}) collective-permute-start(bf16[256,512]{1,0:T(8,128)(2,1)S(1)} %collective-permute-done.refs_0_), channel_id=1, source_target_pairs={{0,1},{1,2},{2,3},{3,0},{4,5},{5,6},{6,7},{7,4},{8,9},{9,10},{10,1... | collective-permute-start | bytes 786440 | tf_op jit(solution)/shard_map/weight_ring/ppermute | solution.py:55
  48.5 7.6 %collective-permute-start.18 = (f32[16,4608]{1,0:T(8,128)S(1)}, f32[16,4608]{1,0:T(8,128)S(1)}, u32[]{:S(2)}, u32[]{:S(2)}) collective-permute-start(f32[16,4608]{1,0:T(8,128)S(1)} %get-tuple-element.112), channel_id=1, source_target_pairs={{0,1},{1,0},{2,3},{3,2},{4,5},{5,4},{6,7},{7,6},{8,9},{9,8},{10,11... | collective-permute-start | bytes 884744 | tf_op jit(solution)/shard_map/adapter_sum/ppermute | solution.py:43
  48.6 14.9 %collective-permute-start.16 = (bf16[256,512]{1,0:T(8,128)(2,1)S(1)}, bf16[256,512]{1,0:T(8,128)(2,1)S(1)}, u32[]{:S(2)}, u32[]{:S(2)}) collective-permute-start(bf16[256,512]{1,0:T(8,128)(2,1)S(1)} %collective-permute-done.8.refs_3_), channel_id=1, source_target_pairs={{0,1},{1,2},{2,3},{3,0},{4,5},{5,6},{6,7},{7,4},{8,9},{9,10},{10,1... | collective-permute-start | bytes 786440 | tf_op jit(solution)/shard_map/weight_ring_across/ppermute | solution.py:55
  50.5 13.0 %collective-permute-start.15 = (bf16[256,512]{1,0:T(8,128)(2,1)S(1)}, bf16[256,512]{1,0:T(8,128)(2,1)S(1)}, u32[]{:S(2)}, u32[]{:S(2)}) collective-permute-start(bf16[256,512]{1,0:T(8,128)(2,1)S(1)} %collective-permute-done.5.refs_4_), channel_id=1, source_target_pairs={{0,16},{4,12},{8,24},{12,4},{16,0},{20,28},{24,8},{28,20},{1,17},{... | collective-permute-start | bytes 786440 | tf_op jit(solution)/shard_map/weight_chip_1/ppermute | solution.py:43
  51.6 11.9 %collective-permute-start.14 = (bf16[256,512]{1,0:T(8,128)(2,1)S(1)}, bf16[256,512]{1,0:T(8,128)(2,1)S(1)}, u32[]{:S(2)}, u32[]{:S(2)}) collective-permute-start(bf16[256,512]{1,0:T(8,128)(2,1)S(1)} %collective-permute-done.5.refs_4_), channel_id=1, source_target_pairs={{0,8},{4,20},{8,0},{12,28},{16,24},{20,4},{24,16},{28,12},{1,9},{5... | collective-permute-start | bytes 786440 | tf_op jit(solution)/shard_map/weight_chip_0/ppermute | solution.py:43
  53.8 9.8 %collective-permute-start.17 = (bf16[256,512]{1,0:T(8,128)(2,1)S(1)}, bf16[256,512]{1,0:T(8,128)(2,1)S(1)}, u32[]{:S(2)}, u32[]{:S(2)}) collective-permute-start(bf16[256,512]{1,0:T(8,128)(2,1)S(1)} %collective-permute-done.11.refs_9_), channel_id=1, source_target_pairs={{0,16},{4,12},{8,24},{12,4},{16,0},{20,28},{24,8},{28,20},{1,17},{... | collective-permute-start | bytes 786440 | tf_op jit(solution)/shard_map/weight_chip_1/ppermute | solution.py:43
  68.8 9.7 %collective-permute-start.23 = (bf16[16,4608]{1,0:T(8,128)(2,1)S(1)}, bf16[16,4608]{1,0:T(8,128)(2,1)S(1)}, u32[]{:S(2)}, u32[]{:S(2)}) collective-permute-start(bf16[16,4608]{1,0:T(8,128)(2,1)S(1)} %add_convert_fusion.1), channel_id=1, source_target_pairs={{0,2},{1,3},{2,0},{3,1},{4,6},{5,7},{6,4},{7,5},{8,10},{9,11},{10,... | collective-permute-start | bytes 442376 | tf_op jit(solution)/shard_map/adapter_sum/ppermute | solution.py:43
  68.9 9.7 %collective-permute-start.22 = (bf16[128,512]{1,0:T(8,128)(2,1)S(1)}, bf16[128,512]{1,0:T(8,128)(2,1)S(1)}, u32[]{:S(2)}, u32[]{:S(2)}) collective-permute-start(bf16[128,512]{1,0:T(8,128)(2,1)S(1)} %add_convert_fusion.4.refs_5_), channel_id=1, source_target_pairs={{0,4},{4,8},{8,12},{12,16},{16,20},{20,24},{24,28},{1,5},{5,9},{9,... | collective-permute-start | bytes 393224 | tf_op jit(solution)/shard_map/value_halo/ppermute | solution.py:49
  70.5 8.1 %collective-permute-start.21 = (bf16[128,512]{1,0:T(8,128)(2,1)S(1)}, bf16[128,512]{1,0:T(8,128)(2,1)S(1)}, u32[]{:S(2)}, u32[]{:S(2)}) collective-permute-start(bf16[128,512]{1,0:T(8,128)(2,1)S(1)} %add_convert_fusion.4.refs_5_), channel_id=1, source_target_pairs={{0,8},{4,12},{8,16},{12,20},{16,24},{20,28},{1,9},{5,13},{9,17},{1... | collective-permute-start | bytes 393224 | tf_op jit(solution)/shard_map/value_halo/ppermute | solution.py:49
  78.6 6.8 %collective-permute-start.24 = (bf16[16,4608]{1,0:T(8,128)(2,1)S(1)}, bf16[16,4608]{1,0:T(8,128)(2,1)S(1)}, u32[]{:S(2)}, u32[]{:S(2)}) collective-permute-start(bf16[16,4608]{1,0:T(8,128)(2,1)S(1)} %add_convert_fusion), channel_id=1, source_target_pairs={{0,8},{4,12},{8,0},{12,4},{16,24},{20,28},{24,16},{28,20},{1,9},{5... | collective-permute-start | bytes 442376 | tf_op jit(solution)/shard_map/adapter_sum/ppermute | solution.py:43
  86.0 5.5 %collective-permute-start.25 = (bf16[128,512]{1,0:T(8,128)(2,1)S(1)}, bf16[128,512]{1,0:T(8,128)(2,1)S(1)}, u32[]{:S(2)}, u32[]{:S(2)}) collective-permute-start(bf16[128,512]{1,0:T(8,128)(2,1)S(1)} %get-tuple-element.143), channel_id=1, source_target_pairs={{4,0},{8,4},{12,8},{16,12},{20,16},{24,20},{28,24},{5,1},{9,5},{13... | collective-permute-start | bytes 393224 | tf_op jit(solution)/shard_map/key_grad_halo/ppermute | solution.py:49
  87.3 8.4 %collective-permute-start.26 = (bf16[128,512]{1,0:T(8,128)(2,1)S(1)}, bf16[128,512]{1,0:T(8,128)(2,1)S(1)}, u32[]{:S(2)}, u32[]{:S(2)}) collective-permute-start(bf16[128,512]{1,0:T(8,128)(2,1)S(1)} %get-tuple-element.144), channel_id=1, source_target_pairs={{8,0},{12,4},{16,8},{20,12},{24,16},{28,20},{9,1},{13,5},{17,9},{2... | collective-permute-start | bytes 393224 | tf_op jit(solution)/shard_map/key_grad_halo/ppermute | solution.py:49
  (14 other events, 125.2 us)

commit v4 on v3

--- a/solution.py
+++ b/solution.py
@@ -708,22 +708,24 @@
     arrived[0], x = after((arrived[0], x))
     key_blocks = [shift(k, "seq", by, "key_halo") for by in range(back, 0, -1)] + [k]
     x_mine, x_sent = x_halves_call(me, x, fsdp_count)
-    x_theirs = swap(x_sent, "x_core")
     probs, dv_blocks = probs_call(me, packed_document_lengths, q, o, key_blocks)
-    arrived, across, dv_blocks, x_theirs = after((arrived, across, dv_blocks, x_theirs))
+    arrived, across, dv_blocks, x_mine, x_sent = after(
+        (arrived, across, dv_blocks, x_mine, x_sent)
+    )
 
     dv_back = [
         shift(dv_blocks[back - by], "seq", -by, "value_grad_halo") for by in range(1, back + 1)
     ]
+    ring_step(arrived, ring[2:], "weight_ring")
     if direct:
         set_out(ring[:1])
-        ring_step(across, ring[:1], "weight_ring_across")
+    x_theirs = swap(x_sent, "x_core")
     acc, low = own_values_call(me, x_mine, x_theirs, down, up, w)
-    held, across, dv_back, acc, low = after((held, across, dv_back, acc, low))
+    held, arrived, dv_back, acc, low = after((held, arrived, dv_back, acc, low))
 
     if direct:
         set_out(ring[1:2])
-    ring_step(arrived, ring[2:], "weight_ring")
+        ring_step(across, ring[:1], "weight_ring_across")
     dv = dv_blocks[back]
     for block in dv_back:
         dv = dv + block.astype(F32)
@@ -731,7 +733,7 @@
     dv_theirs = swap(dv_mine, "value_grad_core")
     scale = 1.0 / (tokens * seq_count * fsdp_count)
     rank_grad, sums = adapter_grad_call(dv_mine, dv_theirs, up, low, x_mine, x_theirs, scale)
-    arrived, held, sums = after((arrived, held, sums))
+    across, held, sums = after((across, held, sums))
 
     steps = sum_steps(seq_count, fsdp_count)
     if direct:

time: 96.8 us -> 94.3 us (0.974)
  starting transfers between devices: 41.8 us -> 36.9 us
  waiting for transfers between devices: 25.8 us -> 28.2 us
    ppermute x16, waiting for transfers between devices: 7.05 us -> 14.9 us  [flip(): return lax.ppermute(value, axis, [(i, i ^ choose(i)) for i in range(size)])]
    ppermute x5, waiting for transfers between devices: 10.8 us -> 5.13 us  [turn(): lax.ppermute(value, axis, [(i, (i + by) % size) for i in range(size)])]
    ppermute x16, starting transfers between devices: 18.1 us -> 16 us  [flip(): return lax.ppermute(value, axis, [(i, i ^ choose(i)) for i in range(size)])]
    ppermute x8, starting transfers between devices: 15.9 us -> 14.2 us  [shift(): lax.ppermute(value, axis, [(i, i + by) for i in range(size) if 0 <= i + b...]
    ppermute x5, starting transfers between devices: 7.83 us -> 6.66 us  [turn(): lax.ppermute(value, axis, [(i, (i + by) % size) for i in range(size)])]
  transfers between devices with their start and end apart: 29 -> 29, of which waited for: 9 -> 11; matrix products, arithmetic and copies ran while one was open for 0% -> 0% of each run, Pallas kernels for 22% -> 24%
where the time goes in v4:
time: 94.3 us; the launch traced here: 93.9 us
  starting transfers between devices  36.9 us (39%)
  waiting for transfers between devices  28.2 us (30%)
  Pallas kernels  22.4 us (24%)
  local copies, waits for them, and re-layouts  4.39 us (5%)
  other arithmetic  1.02 us (1%)
  between operations  1 us (1%)
    ppermute x16, starting transfers between devices, flip(): return lax.ppermute(value, axis, [(i, i ^ choose(i)) for i in range(size)])  16 us
    ppermute x16, waiting for transfers between devices, flip(): return lax.ppermute(value, axis, [(i, i ^ choose(i)) for i in range(size)])  14.9 us
    ppermute x8, starting transfers between devices, shift(): lax.ppermute(value, axis, [(i, i + by) for i in range(size) if 0 <= i + b...  14.2 us
    ppermute x8, waiting for transfers between devices, shift(): lax.ppermute(value, axis, [(i, i + by) for i in range(size) if 0 <= i + b...  8.24 us
    ppermute x5, starting transfers between devices, turn(): lax.ppermute(value, axis, [(i, (i + by) % size) for i in range(size)])  6.66 us
    ppermute x5, waiting for transfers between devices, turn(): lax.ppermute(value, axis, [(i, (i + by) % size) for i in range(size)])  5.13 us
    pallas_call x1, Pallas kernels, scores_grad_call(): pl.pallas_call(kernel, grid=(KEY_VALUE_HEADS // HEADS_A_STEP,), in_specs=...  4.32 us
    pallas_call x1, Pallas kernels, input_grad_call(): pl.pallas_call(kernel, in_specs=[smem(), vmem(), vmem(), vmem()] + [hbm()...  4.28 us
  transfers between devices with their start and end apart: 29, of which 11 were waited for; matrix products, arithmetic and copies ran while one was open for 0% of the time, Pallas kernels for 24%

profile of v4, /device:TPU:0, one launch (start us, length us, event | category | flops | bytes accessed | tf_op | source)
XLA Modules:
  0.0 93.9 jit_solution(13835066308386437643)
XLA Ops:
  1.9 5.1 %collective-permute-start.1 = (bf16[256,512]{1,0:T(8,128)(2,1)S(1)}, bf16[256,512]{1,0:T(8,128)(2,1)S(1)}, u32[]{:S(2)}, u32[]{:S(2)}) collective-permute-start(bf16[256,512]{1,0:T(8,128)(2,1)S(1)} %get-tuple-element.162), channel_id=1, source_target_pairs={{0,3},{1,0},{2,1},{3,2},{4,7},{5,4},{6,5},{7,6},{8,11},{9,8},{10,9... | collective-permute-start | bytes 786440 | tf_op jit(solution)/shard_map/weight_ring/ppermute | solution.py:55
  8.5 3.9 %collective-permute-start.2 = (bf16[128,512]{1,0:T(8,128)(2,1)}, bf16[128,512]{1,0:T(8,128)(2,1)S(1)}, u32[]{:S(2)}, u32[]{:S(2)}) collective-permute-start(bf16[128,512]{1,0:T(8,128)(2,1)} %bitcast.16), channel_id=1, source_target_pairs={{0,8},{4,12},{8,16},{12,20},{16,24},{20,28},{1,9},{5,13},{9,17},{1... | collective-permute-start | bytes 393224 | tf_op jit(solution)/shard_map/key_halo/ppermute | solution.py:49
  12.4 1.6 %copy-done.3 = bf16[1,128,8192]{2,1,0:T(8,128)(2,1)S(1)} copy-done((bf16[1,128,8192]{2,1,0:T(8,128)(2,1)S(1)}, bf16[1,128,8192]{2,1,0:T(8,128)(2,1)}, u32[]{:S(2)}) %copy-start.3) | copy-done | bytes 2097176
  17.5 3.5 %probs.1 = (bf16[4,256,1024]{2,1,0:T(8,128)(2,1)S(1)}, bf16[128,512]{1,0:T(8,128)(2,1)S(1)}, bf16[128,512]{1,0:T(8,128)(2,1)S(1)}, f32[128,512]{1,0:T(8,128)S(1)}) custom-call(s32[2]{0:T(128)S(1)} %pad_add_fusion.me_ref, s32[1,8]{1,0:T(1,128)S(1)} %copy-done.8, bf16[128,4096]{1,0:T(8,128)(2,1)S(1)} %bitcast.10, bf16[128,4096]{1,0:T(8,128)(2,1)S(1)} %bitcast.12, ...), custom_call_target="tpu_custom_call" | custom-call | flops 1 | bytes 1 | tf_op jit(solution)/shard_map/probs/pallas_call | solution.py:187
  21.8 3.3 %collective-permute-start.6 = (bf16[256,512]{1,0:T(8,128)(2,1)S(1)}, bf16[256,512]{1,0:T(8,128)(2,1)S(1)}, u32[]{:S(2)}, u32[]{:S(2)}) collective-permute-start(bf16[256,512]{1,0:T(8,128)(2,1)S(1)} %collective-permute-done.refs_0_), channel_id=1, source_target_pairs={{0,16},{4,12},{8,24},{12,4},{16,0},{20,28},{24,8},{28,20},{1,17},{... | collective-permute-start | bytes 786440 | tf_op jit(solution)/shard_map/weight_chip_1/ppermute | solution.py:43
  27.8 3.4 %own_values.1 = (f32[256,512]{1,0:T(8,128)S(1)}, f32[256,16]{1,0:T(8,128)S(1)}) custom-call(s32[2]{0:T(128)S(1)} %pad_add_fusion.me_ref, bf16[128,4096]{1,0:T(8,128)(2,1)S(1)} %get-tuple-element.94.mine_hbm.x_mine_hbm, bf16[128,4096]{1,0:T(8,128)(2,1)S(1)} %collective-permute-done.10.theirs_hbm.x_theirs_hbm, bf16[16,8192]{1,0:T(8,128)(2,1)S(1)} %copy-done.4, ...), custom_call_target="tpu_custom_call" | custom-call | flops 1 | bytes 1 | tf_op jit(solution)/shard_map/own_values/pallas_call | solution.py:373
  31.3 1.5 %collective-permute-start.4 = (bf16[256,512]{1,0:T(8,128)(2,1)S(1)}, bf16[256,512]{1,0:T(8,128)(2,1)S(1)}, u32[]{:S(2)}, u32[]{:S(2)}) collective-permute-start(bf16[256,512]{1,0:T(8,128)(2,1)S(1)} %get-tuple-element.89), channel_id=1, source_target_pairs={{0,1},{1,2},{2,3},{3,0},{4,5},{5,6},{6,7},{7,4},{8,9},{9,10},{10,1... | collective-permute-start | bytes 786440 | tf_op jit(solution)/shard_map/weight_ring_across/ppermute | solution.py:55
  32.8 2.9 %collective-permute-done.9 = bf16[128,512]{1,0:T(8,128)(2,1)S(1)} collective-permute-done((bf16[128,512]{1,0:T(8,128)(2,1)S(1)}, bf16[128,512]{1,0:T(8,128)(2,1)S(1)}, u32[]{:S(2)}, u32[]{:S(2)}) %collective-permute-start.9) | collective-permute-done | bytes 131104 | tf_op jit(solution)/shard_map/value_grad_halo/ppermute | solution.py:49
  35.7 2.0 %collective-permute-start.12 = (bf16[256,512]{1,0:T(8,128)(2,1)S(1)}, bf16[256,512]{1,0:T(8,128)(2,1)S(1)}, u32[]{:S(2)}, u32[]{:S(2)}) collective-permute-start(bf16[256,512]{1,0:T(8,128)(2,1)S(1)} %collective-permute-done.1.refs_8_), channel_id=1, source_target_pairs={{0,16},{4,12},{8,24},{12,4},{16,0},{20,28},{24,8},{28,20},{1,17},{... | collective-permute-start | bytes 786440 | tf_op jit(solution)/shard_map/weight_chip_1/ppermute | solution.py:43
  41.0 3.5 %collective-permute-done.12.refs_10_ = bf16[256,512]{1,0:T(8,128)(2,1)S(1)} collective-permute-done((bf16[256,512]{1,0:T(8,128)(2,1)S(1)}, bf16[256,512]{1,0:T(8,128)(2,1)S(1)}, u32[]{:S(2)}, u32[]{:S(2)}) %collective-permute-start.12) | collective-permute-done | bytes 262176 | tf_op jit(solution)/shard_map/weight_chip_1/ppermute | solution.py:43
  44.5 2.9 %collective-permute-start.18 = (f32[16,4608]{1,0:T(8,128)S(1)}, f32[16,4608]{1,0:T(8,128)S(1)}, u32[]{:S(2)}, u32[]{:S(2)}) collective-permute-start(f32[16,4608]{1,0:T(8,128)S(1)} %get-tuple-element.116), channel_id=1, source_target_pairs={{0,1},{1,0},{2,3},{3,2},{4,5},{5,4},{6,7},{7,6},{8,9},{9,8},{10,11... | collective-permute-start | bytes 884744 | tf_op jit(solution)/shard_map/adapter_sum/ppermute | solution.py:43
  47.4 1.5 %collective-permute-start.15 = (bf16[256,512]{1,0:T(8,128)(2,1)S(1)}, bf16[256,512]{1,0:T(8,128)(2,1)S(1)}, u32[]{:S(2)}, u32[]{:S(2)}) collective-permute-start(bf16[256,512]{1,0:T(8,128)(2,1)S(1)} %collective-permute-done.7.refs_4_), channel_id=1, source_target_pairs={{0,16},{4,12},{8,24},{12,4},{16,0},{20,28},{24,8},{28,20},{1,17},{... | collective-permute-start | bytes 786440 | tf_op jit(solution)/shard_map/weight_chip_1/ppermute | solution.py:43
  49.0 1.7 %collective-permute-start.14 = (bf16[256,512]{1,0:T(8,128)(2,1)S(1)}, bf16[256,512]{1,0:T(8,128)(2,1)S(1)}, u32[]{:S(2)}, u32[]{:S(2)}) collective-permute-start(bf16[256,512]{1,0:T(8,128)(2,1)S(1)} %collective-permute-done.7.refs_4_), channel_id=1, source_target_pairs={{0,8},{4,20},{8,0},{12,28},{16,24},{20,4},{24,16},{28,12},{1,9},{5... | collective-permute-start | bytes 786440 | tf_op jit(solution)/shard_map/weight_chip_0/ppermute | solution.py:43
  50.7 4.1 %collective-permute-done.18 = f32[16,4608]{1,0:T(8,128)S(1)} collective-permute-done((f32[16,4608]{1,0:T(8,128)S(1)}, f32[16,4608]{1,0:T(8,128)S(1)}, u32[]{:S(2)}, u32[]{:S(2)}) %collective-permute-start.18) | collective-permute-done | bytes 294944 | tf_op jit(solution)/shard_map/adapter_sum/ppermute | solution.py:43
  54.9 1.6 %collective-permute-done.15.refs_6_ = bf16[256,512]{1,0:T(8,128)(2,1)S(1)} collective-permute-done((bf16[256,512]{1,0:T(8,128)(2,1)S(1)}, bf16[256,512]{1,0:T(8,128)(2,1)S(1)}, u32[]{:S(2)}, u32[]{:S(2)}) %collective-permute-start.15) | collective-permute-done | bytes 262176 | tf_op jit(solution)/shard_map/weight_chip_1/ppermute | solution.py:43
  57.9 4.9 %collective-permute-done.16.refs_7_ = bf16[256,512]{1,0:T(8,128)(2,1)S(1)} collective-permute-done((bf16[256,512]{1,0:T(8,128)(2,1)S(1)}, bf16[256,512]{1,0:T(8,128)(2,1)S(1)}, u32[]{:S(2)}, u32[]{:S(2)}) %collective-permute-start.16) | collective-permute-done | bytes 262176 | tf_op jit(solution)/shard_map/weight_ring_across/ppermute | solution.py:55
  63.1 2.1 %more_values.1 = (f32[128,512]{1,0:T(8,128)S(1)}, f32[128,512]{1,0:T(8,128)S(1)}) custom-call(s32[2]{0:T(128)S(1)} %pad_add_fusion.me_ref, f32[256,512]{1,0:T(8,128)S(1)} %get-tuple-element.117.acc_ref, bf16[128,4096]{1,0:T(8,128)(2,1)S(1)} %get-tuple-element.94.mine_hbm.x_mine_hbm, bf16[128,4096]{1,0:T(8,128)(2,1)S(1)} %collective-permute-done.10.theirs_hbm.x_theirs_hbm, ...), custom_call_target="tpu_custom_call" | custom-call | flops 1 | bytes 1 | tf_op jit(solution)/shard_map/more_values/pallas_call | solution.py:458
  65.3 2.8 %collective-permute-done.20 = bf16[16,4608]{1,0:T(8,128)(2,1)S(1)} collective-permute-done((bf16[16,4608]{1,0:T(8,128)(2,1)S(1)}, bf16[16,4608]{1,0:T(8,128)(2,1)S(1)}, u32[]{:S(2)}, u32[]{:S(2)}) %collective-permute-start.20) | collective-permute-done | bytes 147488 | tf_op jit(solution)/shard_map/adapter_sum/ppermute | solution.py:43
  69.6 2.4 %collective-permute-start.21 = (bf16[128,512]{1,0:T(8,128)(2,1)S(1)}, bf16[128,512]{1,0:T(8,128)(2,1)S(1)}, u32[]{:S(2)}, u32[]{:S(2)}) collective-permute-start(bf16[128,512]{1,0:T(8,128)(2,1)S(1)} %add_convert_fusion.4.refs_5_), channel_id=1, source_target_pairs={{0,8},{4,12},{8,16},{12,20},{16,24},{20,28},{1,9},{5,13},{9,17},{1... | collective-permute-start | bytes 393224 | tf_op jit(solution)/shard_map/value_halo/ppermute | solution.py:49
  72.0 4.3 %input_grad.1 = (bf16[128,8192]{1,0:T(8,128)(2,1)}, bf16[128,4096]{1,0:T(8,128)(2,1)S(1)}) custom-call(s32[2]{0:T(128)S(1)} %pad_add_fusion.me_ref, bf16[128,512]{1,0:T(8,128)(2,1)S(1)} %add_convert_fusion.5.mine_ref, bf16[128,512]{1,0:T(8,128)(2,1)S(1)} %collective-permute-done.13.theirs_ref, bf16[256,16]{1,0:T(8,128)(2,1)S(1)} %get-tuple-element.136.rank_ref, ...), custom_call_target="tpu_custom_call" | custom-call | flops 1 | bytes 1 | tf_op jit(solution)/shard_map/input_grad/pallas_call | solution.py:529
  76.4 2.2 %collective-permute-start.24 = (bf16[16,4608]{1,0:T(8,128)(2,1)S(1)}, bf16[16,4608]{1,0:T(8,128)(2,1)S(1)}, u32[]{:S(2)}, u32[]{:S(2)}) collective-permute-start(bf16[16,4608]{1,0:T(8,128)(2,1)S(1)} %add_convert_fusion), channel_id=1, source_target_pairs={{0,8},{4,12},{8,0},{12,4},{16,24},{20,28},{24,16},{28,20},{1,9},{5... | collective-permute-start | bytes 442376 | tf_op jit(solution)/shard_map/adapter_sum/ppermute | solution.py:43
  78.6 4.3 %scores_grad.1 = (bf16[128,4096]{1,0:T(8,128)(2,1)}, bf16[128,512]{1,0:T(8,128)(2,1)S(1)}, bf16[128,512]{1,0:T(8,128)(2,1)S(1)}, f32[128,512]{1,0:T(8,128)S(1)}) custom-call(bf16[4,256,1024]{2,1,0:T(8,128)(2,1)S(1)} %get-tuple-element.140.p_ref, bf16[128,4096]{1,0:T(8,128)(2,1)S(1)} %bitcast.11, bf16[128,4096]{1,0:T(8,128)(2,1)S(1)} %bitcast.13, ...), custom_call_target="tpu_custom_call" | custom-call | flops 1 | bytes 1 | tf_op jit(solution)/shard_map/scores_grad/pallas_call | solution.py:237
  87.5 1.5 %put_half.1 = bf16[128,8192]{1,0:T(8,128)(2,1)} custom-call(s32[2]{0:T(128)S(1)} %pad_add_fusion.me_ref, bf16[128,4096]{1,0:T(8,128)(2,1)S(1)} %collective-permute-done.27.theirs_ref, bf16[128,8192]{1,0:T(8,128)(2,1)} %get-tuple-element.150.out_in), custom_call_target="tpu_custom_call", output_to_operand_aliasing={{}: (2, {})} | custom-call | flops 1 | bytes 1 | tf_op jit(solution)/shard_map/put_half/pallas_call | solution.py:299
  89.1 4.2 %collective-permute-done.26 = bf16[128,512]{1,0:T(8,128)(2,1)S(1)} collective-permute-done((bf16[128,512]{1,0:T(8,128)(2,1)S(1)}, bf16[128,512]{1,0:T(8,128)(2,1)S(1)}, u32[]{:S(2)}, u32[]{:S(2)}) %collective-permute-start.26) | collective-permute-done | bytes 131104 | tf_op jit(solution)/shard_map/key_grad_halo/ppermute | solution.py:49
  (70 shorter events, 21.5 us)
Async XLA Ops:
  1.9 19.2 %collective-permute-start.1 = (bf16[256,512]{1,0:T(8,128)(2,1)S(1)}, bf16[256,512]{1,0:T(8,128)(2,1)S(1)}, u32[]{:S(2)}, u32[]{:S(2)}) collective-permute-start(bf16[256,512]{1,0:T(8,128)(2,1)S(1)} %get-tuple-element.162), channel_id=1, source_target_pairs={{0,3},{1,0},{2,1},{3,2},{4,7},{5,4},{6,5},{7,6},{8,11},{9,8},{10,9... | collective-permute-start | bytes 786440 | tf_op jit(solution)/shard_map/weight_ring/ppermute | solution.py:55
  7.0 14.1 %collective-permute-start = (bf16[256,512]{1,0:T(8,128)(2,1)S(1)}, bf16[256,512]{1,0:T(8,128)(2,1)S(1)}, u32[]{:S(2)}, u32[]{:S(2)}) collective-permute-start(bf16[256,512]{1,0:T(8,128)(2,1)S(1)} %get-tuple-element.162), channel_id=1, source_target_pairs={{0,1},{1,2},{2,3},{3,0},{4,5},{5,6},{6,7},{7,4},{8,9},{9,10},{10,1... | collective-permute-start | bytes 786440 | tf_op jit(solution)/shard_map/weight_ring/ppermute | solution.py:55
  7.0 7.8 %collective-permute-start.3 = (bf16[128,512]{1,0:T(8,128)(2,1)}, bf16[128,512]{1,0:T(8,128)(2,1)S(1)}, u32[]{:S(2)}, u32[]{:S(2)}) collective-permute-start(bf16[128,512]{1,0:T(8,128)(2,1)} %bitcast.15), channel_id=1, source_target_pairs={{0,4},{4,8},{8,12},{12,16},{16,20},{20,24},{24,28},{1,5},{5,9},{9,... | collective-permute-start | bytes 393224 | tf_op jit(solution)/shard_map/key_halo/ppermute | solution.py:49
  8.5 7.5 %collective-permute-start.2 = (bf16[128,512]{1,0:T(8,128)(2,1)}, bf16[128,512]{1,0:T(8,128)(2,1)S(1)}, u32[]{:S(2)}, u32[]{:S(2)}) collective-permute-start(bf16[128,512]{1,0:T(8,128)(2,1)} %bitcast.16), channel_id=1, source_target_pairs={{0,8},{4,12},{8,16},{12,20},{16,24},{20,28},{1,9},{5,13},{9,17},{1... | collective-permute-start | bytes 393224 | tf_op jit(solution)/shard_map/key_halo/ppermute | solution.py:49
  21.1 5.4 %collective-permute-start.10 = (bf16[128,4096]{1,0:T(8,128)(2,1)S(1)}, bf16[128,4096]{1,0:T(8,128)(2,1)S(1)}, u32[]{:S(2)}, u32[]{:S(2)}) collective-permute-start(bf16[128,4096]{1,0:T(8,128)(2,1)S(1)} %get-tuple-element.95), channel_id=1, source_target_pairs={{0,4},{4,0},{8,12},{12,8},{16,20},{20,16},{24,28},{28,24},{1,5},{5... | collective-permute-start | bytes 3145736 | tf_op jit(solution)/shard_map/x_core/ppermute | solution.py:43
  21.8 13.9 %collective-permute-start.7 = (bf16[256,512]{1,0:T(8,128)(2,1)S(1)}, bf16[256,512]{1,0:T(8,128)(2,1)S(1)}, u32[]{:S(2)}, u32[]{:S(2)}) collective-permute-start(bf16[256,512]{1,0:T(8,128)(2,1)S(1)} %collective-permute-done.refs_0_), channel_id=1, source_target_pairs={{0,1},{1,2},{2,3},{3,0},{4,5},{5,6},{6,7},{7,4},{8,9},{9,10},{10,1... | collective-permute-start | bytes 786440 | tf_op jit(solution)/shard_map/weight_ring/ppermute | solution.py:55
  21.8 13.9 %collective-permute-start.6 = (bf16[256,512]{1,0:T(8,128)(2,1)S(1)}, bf16[256,512]{1,0:T(8,128)(2,1)S(1)}, u32[]{:S(2)}, u32[]{:S(2)}) collective-permute-start(bf16[256,512]{1,0:T(8,128)(2,1)S(1)} %collective-permute-done.refs_0_), channel_id=1, source_target_pairs={{0,16},{4,12},{8,24},{12,4},{16,0},{20,28},{24,8},{28,20},{1,17},{... | collective-permute-start | bytes 786440 | tf_op jit(solution)/shard_map/weight_chip_1/ppermute | solution.py:43
  25.1 10.6 %collective-permute-start.5 = (bf16[256,512]{1,0:T(8,128)(2,1)S(1)}, bf16[256,512]{1,0:T(8,128)(2,1)S(1)}, u32[]{:S(2)}, u32[]{:S(2)}) collective-permute-start(bf16[256,512]{1,0:T(8,128)(2,1)S(1)} %collective-permute-done.refs_0_), channel_id=1, source_target_pairs={{0,8},{4,20},{8,0},{12,28},{16,24},{20,4},{24,16},{28,12},{1,9},{5... | collective-permute-start | bytes 786440 | tf_op jit(solution)/shard_map/weight_chip_0/ppermute | solution.py:43
  25.2 6.1 %collective-permute-start.8 = (bf16[128,512]{1,0:T(8,128)(2,1)S(1)}, bf16[128,512]{1,0:T(8,128)(2,1)S(1)}, u32[]{:S(2)}, u32[]{:S(2)}) collective-permute-start(bf16[128,512]{1,0:T(8,128)(2,1)S(1)} %get-tuple-element.92), channel_id=1, source_target_pairs={{4,0},{8,4},{12,8},{16,12},{20,16},{24,20},{28,24},{5,1},{9,5},{13... | collective-permute-start | bytes 393224 | tf_op jit(solution)/shard_map/value_grad_halo/ppermute | solution.py:49
  26.5 9.2 %collective-permute-start.9 = (bf16[128,512]{1,0:T(8,128)(2,1)S(1)}, bf16[128,512]{1,0:T(8,128)(2,1)S(1)}, u32[]{:S(2)}, u32[]{:S(2)}) collective-permute-start(bf16[128,512]{1,0:T(8,128)(2,1)S(1)} %get-tuple-element.93), channel_id=1, source_target_pairs={{8,0},{12,4},{16,8},{20,12},{24,16},{28,20},{9,1},{13,5},{17,9},{2... | collective-permute-start | bytes 393224 | tf_op jit(solution)/shard_map/value_grad_halo/ppermute | solution.py:49
  31.3 9.7 %collective-permute-start.4 = (bf16[256,512]{1,0:T(8,128)(2,1)S(1)}, bf16[256,512]{1,0:T(8,128)(2,1)S(1)}, u32[]{:S(2)}, u32[]{:S(2)}) collective-permute-start(bf16[256,512]{1,0:T(8,128)(2,1)S(1)} %get-tuple-element.89), channel_id=1, source_target_pairs={{0,1},{1,2},{2,3},{3,0},{4,5},{5,6},{6,7},{7,4},{8,9},{9,10},{10,1... | collective-permute-start | bytes 786440 | tf_op jit(solution)/shard_map/weight_ring_across/ppermute | solution.py:55
  35.7 8.8 %collective-permute-start.12 = (bf16[256,512]{1,0:T(8,128)(2,1)S(1)}, bf16[256,512]{1,0:T(8,128)(2,1)S(1)}, u32[]{:S(2)}, u32[]{:S(2)}) collective-permute-start(bf16[256,512]{1,0:T(8,128)(2,1)S(1)} %collective-permute-done.1.refs_8_), channel_id=1, source_target_pairs={{0,16},{4,12},{8,24},{12,4},{16,0},{20,28},{24,8},{28,20},{1,17},{... | collective-permute-start | bytes 786440 | tf_op jit(solution)/shard_map/weight_chip_1/ppermute | solution.py:43
  37.8 6.7 %collective-permute-start.11 = (bf16[256,512]{1,0:T(8,128)(2,1)S(1)}, bf16[256,512]{1,0:T(8,128)(2,1)S(1)}, u32[]{:S(2)}, u32[]{:S(2)}) collective-permute-start(bf16[256,512]{1,0:T(8,128)(2,1)S(1)} %collective-permute-done.1.refs_8_), channel_id=1, source_target_pairs={{0,8},{4,20},{8,0},{12,28},{16,24},{20,4},{24,16},{28,12},{1,9},{5... | collective-permute-start | bytes 786440 | tf_op jit(solution)/shard_map/weight_chip_0/ppermute | solution.py:43
  44.5 10.3 %collective-permute-start.18 = (f32[16,4608]{1,0:T(8,128)S(1)}, f32[16,4608]{1,0:T(8,128)S(1)}, u32[]{:S(2)}, u32[]{:S(2)}) collective-permute-start(f32[16,4608]{1,0:T(8,128)S(1)} %get-tuple-element.116), channel_id=1, source_target_pairs={{0,1},{1,0},{2,3},{3,2},{4,5},{5,4},{6,7},{7,6},{8,9},{9,8},{10,11... | collective-permute-start | bytes 884744 | tf_op jit(solution)/shard_map/adapter_sum/ppermute | solution.py:43
  47.4 9.0 %collective-permute-start.15 = (bf16[256,512]{1,0:T(8,128)(2,1)S(1)}, bf16[256,512]{1,0:T(8,128)(2,1)S(1)}, u32[]{:S(2)}, u32[]{:S(2)}) collective-permute-start(bf16[256,512]{1,0:T(8,128)(2,1)S(1)} %collective-permute-done.7.refs_4_), channel_id=1, source_target_pairs={{0,16},{4,12},{8,24},{12,4},{16,0},{20,28},{24,8},{28,20},{1,17},{... | collective-permute-start | bytes 786440 | tf_op jit(solution)/shard_map/weight_chip_1/ppermute | solution.py:43
  49.0 9.0 %collective-permute-start.14 = (bf16[256,512]{1,0:T(8,128)(2,1)S(1)}, bf16[256,512]{1,0:T(8,128)(2,1)S(1)}, u32[]{:S(2)}, u32[]{:S(2)}) collective-permute-start(bf16[256,512]{1,0:T(8,128)(2,1)S(1)} %collective-permute-done.7.refs_4_), channel_id=1, source_target_pairs={{0,8},{4,20},{8,0},{12,28},{16,24},{20,4},{24,16},{28,12},{1,9},{5... | collective-permute-start | bytes 786440 | tf_op jit(solution)/shard_map/weight_chip_0/ppermute | solution.py:43
  50.6 12.2 %collective-permute-start.16 = (bf16[256,512]{1,0:T(8,128)(2,1)S(1)}, bf16[256,512]{1,0:T(8,128)(2,1)S(1)}, u32[]{:S(2)}, u32[]{:S(2)}) collective-permute-start(bf16[256,512]{1,0:T(8,128)(2,1)S(1)} %collective-permute-done.4.refs_3_), channel_id=1, source_target_pairs={{0,1},{1,2},{2,3},{3,0},{4,5},{5,6},{6,7},{7,4},{8,9},{9,10},{10,1... | collective-permute-start | bytes 786440 | tf_op jit(solution)/shard_map/weight_ring_across/ppermute | solution.py:55
  50.6 12.2 %collective-permute-start.17 = (bf16[256,512]{1,0:T(8,128)(2,1)S(1)}, bf16[256,512]{1,0:T(8,128)(2,1)S(1)}, u32[]{:S(2)}, u32[]{:S(2)}) collective-permute-start(bf16[256,512]{1,0:T(8,128)(2,1)S(1)} %collective-permute-done.11.refs_9_), channel_id=1, source_target_pairs={{0,16},{4,12},{8,24},{12,4},{16,0},{20,28},{24,8},{28,20},{1,17},{... | collective-permute-start | bytes 786440 | tf_op jit(solution)/shard_map/weight_chip_1/ppermute | solution.py:43
  68.2 8.1 %collective-permute-start.23 = (bf16[16,4608]{1,0:T(8,128)(2,1)S(1)}, bf16[16,4608]{1,0:T(8,128)(2,1)S(1)}, u32[]{:S(2)}, u32[]{:S(2)}) collective-permute-start(bf16[16,4608]{1,0:T(8,128)(2,1)S(1)} %add_convert_fusion.1), channel_id=1, source_target_pairs={{0,2},{1,3},{2,0},{3,1},{4,6},{5,7},{6,4},{7,5},{8,10},{9,11},{10,... | collective-permute-start | bytes 442376 | tf_op jit(solution)/shard_map/adapter_sum/ppermute | solution.py:43
  68.3 8.1 %collective-permute-start.22 = (bf16[128,512]{1,0:T(8,128)(2,1)S(1)}, bf16[128,512]{1,0:T(8,128)(2,1)S(1)}, u32[]{:S(2)}, u32[]{:S(2)}) collective-permute-start(bf16[128,512]{1,0:T(8,128)(2,1)S(1)} %add_convert_fusion.4.refs_5_), channel_id=1, source_target_pairs={{0,4},{4,8},{8,12},{12,16},{16,20},{20,24},{24,28},{1,5},{5,9},{9,... | collective-permute-start | bytes 393224 | tf_op jit(solution)/shard_map/value_halo/ppermute | solution.py:49
  69.6 6.8 %collective-permute-start.21 = (bf16[128,512]{1,0:T(8,128)(2,1)S(1)}, bf16[128,512]{1,0:T(8,128)(2,1)S(1)}, u32[]{:S(2)}, u32[]{:S(2)}) collective-permute-start(bf16[128,512]{1,0:T(8,128)(2,1)S(1)} %add_convert_fusion.4.refs_5_), channel_id=1, source_target_pairs={{0,8},{4,12},{8,16},{12,20},{16,24},{20,28},{1,9},{5,13},{9,17},{1... | collective-permute-start | bytes 393224 | tf_op jit(solution)/shard_map/value_halo/ppermute | solution.py:49
  76.4 6.5 %collective-permute-start.24 = (bf16[16,4608]{1,0:T(8,128)(2,1)S(1)}, bf16[16,4608]{1,0:T(8,128)(2,1)S(1)}, u32[]{:S(2)}, u32[]{:S(2)}) collective-permute-start(bf16[16,4608]{1,0:T(8,128)(2,1)S(1)} %add_convert_fusion), channel_id=1, source_target_pairs={{0,8},{4,12},{8,0},{12,4},{16,24},{20,28},{24,16},{28,20},{1,9},{5... | collective-permute-start | bytes 442376 | tf_op jit(solution)/shard_map/adapter_sum/ppermute | solution.py:43
  83.5 5.5 %collective-permute-start.25 = (bf16[128,512]{1,0:T(8,128)(2,1)S(1)}, bf16[128,512]{1,0:T(8,128)(2,1)S(1)}, u32[]{:S(2)}, u32[]{:S(2)}) collective-permute-start(bf16[128,512]{1,0:T(8,128)(2,1)S(1)} %get-tuple-element.147), channel_id=1, source_target_pairs={{4,0},{8,4},{12,8},{16,12},{20,16},{24,20},{28,24},{5,1},{9,5},{13... | collective-permute-start | bytes 393224 | tf_op jit(solution)/shard_map/key_grad_halo/ppermute | solution.py:49
  84.8 8.4 %collective-permute-start.26 = (bf16[128,512]{1,0:T(8,128)(2,1)S(1)}, bf16[128,512]{1,0:T(8,128)(2,1)S(1)}, u32[]{:S(2)}, u32[]{:S(2)}) collective-permute-start(bf16[128,512]{1,0:T(8,128)(2,1)S(1)} %get-tuple-element.148), channel_id=1, source_target_pairs={{8,0},{12,4},{16,8},{20,12},{24,16},{28,20},{9,1},{13,5},{17,9},{2... | collective-permute-start | bytes 393224 | tf_op jit(solution)/shard_map/key_grad_halo/ppermute | solution.py:49
  (14 other events, 95.3 us)

commit v5 on v4

--- a/solution.py
+++ b/solution.py
@@ -125,31 +125,20 @@
     )
 
 
-HEADS_A_STEP = 2
-
-
-def head_specs(tokens, slots):
-    probs = pl.BlockSpec((HEADS_A_STEP, slots, GROUP * tokens), lambda step: (step, 0, 0))
-    wide = pl.BlockSpec((tokens, HEADS_A_STEP * GROUP * HEAD_FEATURES), lambda step: (0, step))
-    thin = pl.BlockSpec((tokens, HEADS_A_STEP * HEAD_FEATURES), lambda step: (0, step))
-    return probs, wide, thin
-
-
-def probs_call(me, lengths, q, o, key_blocks):
+def probs_call(me, q, o, key_blocks):
     back = len(key_blocks) - 1
-    docs = lengths.shape[1]
+    docs = me.shape[0] - 2
     tokens = q.shape[0]
     kv = key_blocks[0].shape[1]
     slots = back * tokens
 
-    def kernel(me_ref, lengths_ref, q_ref, o_ref, *refs):
+    def kernel(me_ref, q_ref, o_ref, *refs):
         key_refs = refs[: back + 1]
         p_ref = refs[back + 1]
         dv_refs = refs[back + 2 : 2 * back + 3]
         bias_ref = refs[2 * back + 3]
 
-        @pl.when(pl.program_id(0) == 0)
-        def _():
+        def fill_bias():
             here = me_ref[0]
             key = lax.broadcasted_iota(jnp.int32, (slots, tokens), 0)
             query = lax.broadcasted_iota(jnp.int32, (slots, tokens), 1)
@@ -159,12 +148,13 @@
             opening = jnp.zeros((slots, tokens), jnp.int32)
             bound = jnp.int32(0)
             for doc in range(docs):
-                bound = bound + lengths_ref[0, doc]
+                bound = bound + me_ref[2 + doc]
                 opening = jnp.where(query_place >= bound, bound, opening)
             bias_ref[...] = jnp.where(key_place >= opening, 0.0, NEG_FILL)
 
+        fill_bias()
         own = own_rows(tokens)
-        for head in range(HEADS_A_STEP):
+        for head in range(KEY_VALUE_HEADS):
             columns = slice(head * HEAD_FEATURES, (head + 1) * HEAD_FEATURES)
             key_rows = jnp.concatenate([r[:, columns] for r in key_refs], axis=0)
             scores = contract_trailing(key_rows, head_rows(q_ref, head))
@@ -183,12 +173,10 @@
                 rows = dv[block * tokens : (block + 1) * tokens]
                 dv_refs[block][:, columns] = rows.astype(dv_refs[block].dtype)
 
-    probs, wide, thin = head_specs(tokens, slots)
     out = pl.pallas_call(
         kernel,
-        grid=(KEY_VALUE_HEADS // HEADS_A_STEP,),
-        in_specs=[smem(), smem(), wide, wide] + [thin] * (back + 1),
-        out_specs=[probs] + [thin] * (back + 1),
+        in_specs=[smem()] + [vmem()] * (back + 3),
+        out_specs=[vmem()] * (back + 2),
         out_shape=[jax.ShapeDtypeStruct((KEY_VALUE_HEADS, slots, GROUP * tokens), BF16)]
         + [jax.ShapeDtypeStruct((tokens, kv), BF16)] * back
         + [jax.ShapeDtypeStruct((tokens, kv), F32)],
@@ -196,7 +184,7 @@
         compiler_params=params(),
         cost_estimate=SMALL,
         name="probs",
-    )(me, lengths, q, o, *key_blocks)
+    )(me, q, o, *key_blocks)
     return out[0], out[1:]
 
 
@@ -211,7 +199,7 @@
         dq_ref = refs[2 * back + 2]
         dk_refs = refs[2 * back + 3 :]
         own = own_rows(tokens)
-        for head in range(HEADS_A_STEP):
+        for head in range(KEY_VALUE_HEADS):
             columns = slice(head * HEAD_FEATURES, (head + 1) * HEAD_FEATURES)
             key_rows = jnp.concatenate([r[:, columns] for r in key_refs], axis=0)
             value_rows = jnp.concatenate([r[:, columns] for r in value_refs], axis=0)
@@ -233,12 +221,10 @@
                 rows = dk[block * tokens : (block + 1) * tokens]
                 dk_refs[block][:, columns] = rows.astype(dk_refs[block].dtype)
 
-    block, wide, thin = head_specs(tokens, probs.shape[1])
     out = pl.pallas_call(
         kernel,
-        grid=(KEY_VALUE_HEADS // HEADS_A_STEP,),
-        in_specs=[block, wide, wide] + [thin] * (2 * back + 2),
-        out_specs=[wide] + [thin] * (back + 1),
+        in_specs=[vmem()] * (2 * back + 5),
+        out_specs=[vmem()] * (back + 2),
         out_shape=[jax.ShapeDtypeStruct(q.shape, BF16)]
         + [jax.ShapeDtypeStruct((tokens, kv), BF16)] * back
         + [jax.ShapeDtypeStruct((tokens, kv), F32)],
@@ -253,13 +239,13 @@
     return flip(array, "seq", 1, name)
 
 
-def x_halves_call(me, x, shards):
+def x_halves_call(me, x, k, shards):
     tokens, model = x.shape
     half = model // shards // 2
 
-    def kernel(me_ref, x_hbm, mine_ref, theirs_ref, sems):
+    def kernel(me_ref, x_hbm, k_hbm, mine_ref, theirs_ref, k_ref, sems):
         core = me_ref[0] % 2
-        pairs = []
+        pairs = [(k_hbm, k_ref)]
         for which, target in ((1 - core, theirs_ref), (core, mine_ref)):
             for shard in range(shards):
                 first = pl.multiple_of(2 * shard * half + which * half, half)
@@ -271,14 +257,15 @@
 
     return pl.pallas_call(
         kernel,
-        in_specs=[smem(), hbm()],
-        out_specs=[vmem()] * 2,
-        out_shape=[jax.ShapeDtypeStruct((tokens, model // 2), BF16)] * 2,
-        scratch_shapes=[dma(2 * shards)],
+        in_specs=[smem(), hbm(), hbm()],
+        out_specs=[vmem()] * 3,
+        out_shape=[jax.ShapeDtypeStruct((tokens, model // 2), BF16)] * 2
+        + [jax.ShapeDtypeStruct(k.shape, BF16)],
+        scratch_shapes=[dma(2 * shards + 1)],
         compiler_params=params(),
         cost_estimate=SMALL,
         name="x_halves",
-    )(me, x)
+    )(me, x, k)
 
 
 def put_half_call(me, out, theirs, shards):
@@ -343,21 +330,13 @@
     half = rows // 2
     shards = model // rows
 
-    def kernel(me_ref, mine_hbm, theirs_hbm, down_hbm, up_ref, w_hbm, acc_ref, low_ref, *scratch):
-        x_ref, down_ref, w_ref, sems = scratch
+    def kernel(me_ref, mine_ref, theirs_ref, down_ref, up_ref, w_ref, acc_ref, low_ref, down_half):
         core = me_ref[0] % 2
-        pairs = []
         for shard in range(shards):
             first = pl.multiple_of(shard * rows + core * half, half)
-            pairs.append(
-                (down_hbm.at[:, pl.ds(first, half)], down_ref.at[:, pl.ds(shard * half, half)])
-            )
-        pairs.append((mine_hbm, x_ref.at[pl.ds(0, tokens)]))
-        pairs.append((theirs_hbm, x_ref.at[pl.ds(tokens, tokens)]))
-        pairs.append((w_hbm.at[pl.ds(pl.multiple_of(core * half, half), half)], w_ref))
-        for copy in copies(pairs, sems):
-            copy.wait()
-        low = contract_trailing(x_ref[...], down_ref[...])
+            down_half[:, shard * half : (shard + 1) * half] = down_ref[:, pl.ds(first, half)]
+        x_rows = jnp.concatenate([mine_ref[...], theirs_ref[...]], axis=0)
+        low = contract_trailing(x_rows, down_half[...])
         low_ref[...] = low
         adapter = jnp.dot(
             low,
@@ -365,25 +344,20 @@
             precision=lax.Precision.HIGHEST,
             preferred_element_type=F32,
         )
-        first = pl.multiple_of(me_ref[1] * half, half)
-        acc_ref[...] = ADAPTER_SCALE * adapter + jnp.dot(
-            x_ref[:, pl.ds(first, half)], w_ref[...], preferred_element_type=F32
-        )
+        columns = pl.ds(pl.multiple_of(me_ref[1] * half, half), half)
+        x_rows = jnp.concatenate([mine_ref[:, columns], theirs_ref[:, columns]], axis=0)
+        own = w_ref[pl.ds(pl.multiple_of(core * half, half), half), :]
+        acc_ref[...] = ADAPTER_SCALE * adapter + jnp.dot(x_rows, own, preferred_element_type=F32)
 
     return pl.pallas_call(
         kernel,
-        in_specs=[smem(), hbm(), hbm(), hbm(), vmem(), hbm()],
+        in_specs=[smem()] + [vmem()] * 5,
         out_specs=[vmem()] * 2,
         out_shape=[
             jax.ShapeDtypeStruct((2 * tokens, kv), F32),
             jax.ShapeDtypeStruct((2 * tokens, rank), F32),
         ],
-        scratch_shapes=[
-            pltpu.VMEM((2 * tokens, width), BF16),
-            pltpu.VMEM((rank, width), BF16),
-            pltpu.VMEM((half, kv), BF16),
-            dma(shards + 3),
-        ],
+        scratch_shapes=[pltpu.VMEM((rank, width), BF16)],
         compiler_params=params(),
         cost_estimate=SMALL,
         name="own_values",
@@ -423,48 +397,32 @@
     half, step = pieces.half, pieces.step
     bys = list(shards)
     arrays = [array for by in bys for array in shards[by]]
-    firsts, rows = heights(arrays)
-    count = len(bys)
+    firsts, _ = heights(arrays)
     kv = acc.shape[1]
 
-    def kernel(me_ref, acc_ref, mine_hbm, theirs_hbm, *refs):
-        outs = refs[len(arrays) : -3]
-        x_ref, w_ref, sems = refs[-3:]
-        pairs = []
-        for i, by in enumerate(bys):
-            columns = pl.ds(pl.multiple_of(pieces.owner(me_ref, by) * half, half), half)
-            pairs.append((mine_hbm.at[:, columns], x_ref.at[i, pl.ds(0, tokens)]))
-            pairs.append((theirs_hbm.at[:, columns], x_ref.at[i, pl.ds(tokens, tokens)]))
+    def kernel(me_ref, acc_ref, mine_ref, theirs_ref, *refs):
+        outs = refs[len(arrays) :]
+        mine, theirs = acc_ref[:tokens], acc_ref[tokens:]
         for ref, first, array in zip(refs, firsts, arrays):
-            pairs.append((ref, w_ref.at[pl.ds(first, array.shape[0])]))
-        for copy in copies(pairs, sems):
-            copy.wait()
-        total = acc_ref[...]
-        for row in range(0, rows, step):
-            i, number = row // half, (row % half) // step
-            column = pl.multiple_of(pieces.chip(me_ref, number) * step, step)
-            total = total + jnp.dot(
-                x_ref[i, :, pl.ds(column, step)],
-                w_ref[row : row + step, :],
-                preferred_element_type=F32,
-            )
+            for row in range(0, array.shape[0], step):
+                by, number = bys[(first + row) // half], (first + row) % half // step
+                column = pieces.owner(me_ref, by) * half + pieces.chip(me_ref, number) * step
+                columns = pl.ds(pl.multiple_of(column, step), step)
+                x_rows = jnp.concatenate([mine_ref[:, columns], theirs_ref[:, columns]], axis=0)
+                grown = jnp.dot(x_rows, ref[row : row + step, :], preferred_element_type=F32)
+                mine, theirs = mine + grown[:tokens], theirs + grown[tokens:]
         if last:
-            outs[0][...] = total[:tokens]
-            outs[1][...] = total[tokens:]
+            outs[0][...] = mine
+            outs[1][...] = theirs
         else:
-            outs[0][...] = total
+            outs[0][...] = jnp.concatenate([mine, theirs], axis=0)
 
     one = jax.ShapeDtypeStruct((tokens, kv), F32)
     out = pl.pallas_call(
         kernel,
-        in_specs=[smem(), vmem()] + [hbm()] * (2 + len(arrays)),
+        in_specs=[smem()] + [vmem()] * (3 + len(arrays)),
         out_specs=[vmem()] * (2 if last else 1),
         out_shape=[one, one] if last else [jax.ShapeDtypeStruct(acc.shape, F32)],
-        scratch_shapes=[
-            pltpu.VMEM((count, 2 * tokens, half), BF16),
-            pltpu.VMEM((rows, kv), BF16),
-            dma(2 * count + len(arrays)),
-        ],
         compiler_params=params(),
         cost_estimate=SMALL,
         name="more_values",
@@ -483,38 +441,24 @@
     count = 1 + len(bys)
     width = model // 2
 
-    def kernel(me_ref, mine_ref, theirs_ref, rank_ref, down_hbm, w_hbm, *refs):
-        out_hbm, send_hbm, down_ref, w_ref, term, buffer, sems, out_sems = refs[len(arrays) :]
+    def kernel(me_ref, mine_ref, theirs_ref, rank_ref, down_ref, w_ref, *refs):
+        out_hbm, send_hbm, down_half, term, buffer, out_sems = refs[len(arrays) :]
         core = me_ref[0] % 2
         starts = [pl.multiple_of(i * rows + core * half, half) for i in range(count)]
-        pairs = [
-            (down_hbm.at[:, pl.ds(starts[i], half)], down_ref.at[:, pl.ds(i * half, half)])
-            for i in range(count)
-        ]
-        pairs.append(
-            (w_hbm.at[pl.ds(pl.multiple_of(core * half, half), half)], w_ref.at[pl.ds(0, half)])
-        )
+        for i in range(count):
+            down_half[:, i * half : (i + 1) * half] = down_ref[:, pl.ds(starts[i], half)]
+        term[...] = jnp.dot(rank_ref[...], down_half[...], preferred_element_type=F32)
+        dv = jnp.concatenate([mine_ref[...], theirs_ref[...]], axis=0)
+        own = pl.ds(pl.multiple_of(me_ref[1] * half, half), half)
+        own_rows_of_w = pl.ds(pl.multiple_of(core * half, half), half)
+        buffer[:, own] = (contract_trailing(dv, w_ref[own_rows_of_w, :]) + term[:, own]).astype(BF16)
         for ref, first, array in zip(refs, firsts, arrays):
-            pairs.append((ref, w_ref.at[pl.ds(half + first, array.shape[0])]))
-        loads = copies(pairs, sems)
-        for load in loads[: count + 1]:
-            load.wait()
-        term[...] = jnp.dot(rank_ref[...], down_ref[...], preferred_element_type=F32)
-        dv = jnp.concatenate([mine_ref[...], theirs_ref[...]], axis=0)
-        own = pl.multiple_of(me_ref[1] * half, half)
-        grad = contract_trailing(dv, w_ref[0:half, :]) + term[:, pl.ds(own, half)]
-        buffer[:, pl.ds(own, half)] = grad.astype(BF16)
-        for load in loads[count + 1 :]:
-            load.wait()
-        for i, by in enumerate(bys):
-            rows_of = pl.ds(half + i * half, half)
-            grad = contract_trailing(dv, w_ref[rows_of, :])
-            for number in range(pieces.each):
+            for row in range(0, array.shape[0], step):
+                by, number = bys[(first + row) // half], (first + row) % half // step
                 column = pieces.owner(me_ref, by) * half + pieces.chip(me_ref, number) * step
-                column = pl.multiple_of(column, step)
-                part = grad[:, number * step : (number + 1) * step]
-                part = part + term[:, pl.ds(column, step)]
-                buffer[:, pl.ds(column, step)] = part.astype(BF16)
+                columns = pl.ds(pl.multiple_of(column, step), step)
+                grad = contract_trailing(dv, ref[row : row + step, :]) + term[:, columns]
+                buffer[:, columns] = grad.astype(BF16)
         pairs = [(buffer.at[pl.ds(tokens, tokens)], send_hbm)]
         for i in range(count):
             pairs.append(
@@ -528,7 +472,7 @@
 
     return pl.pallas_call(
         kernel,
-        in_specs=[smem(), vmem(), vmem(), vmem()] + [hbm()] * (2 + len(arrays)),
+        in_specs=[smem()] + [vmem()] * (5 + len(arrays)),
         out_specs=[hbm()] * 2,
         out_shape=[
             jax.ShapeDtypeStruct((tokens, model), BF16),
@@ -536,10 +480,8 @@
         ],
         scratch_shapes=[
             pltpu.VMEM((rank, width), BF16),
-            pltpu.VMEM((width, kv), BF16),
             pltpu.VMEM((2 * tokens, width), F32),
             pltpu.VMEM((2 * tokens, width), BF16),
-            dma(count + 1 + len(arrays)),
             dma(1 + count),
         ],
         compiler_params=params(),
@@ -552,33 +494,23 @@
     tokens, width = x_mine.shape
     rank, kv = up.shape
 
-    def kernel(mine_ref, theirs_ref, up_ref, low_ref, x_mine_hbm, x_theirs_hbm, *refs):
-        rank_ref, out_ref, x_ref, sems = refs
-        loads = copies(
-            [
-                (x_mine_hbm, x_ref.at[pl.ds(0, tokens)]),
-                (x_theirs_hbm, x_ref.at[pl.ds(tokens, tokens)]),
-            ],
-            sems,
-        )
+    def kernel(mine_ref, theirs_ref, up_ref, low_ref, x_mine_ref, x_theirs_ref, rank_ref, out_ref):
         dv = jnp.concatenate([mine_ref[...], theirs_ref[...]], axis=0)
         rank_low = (ADAPTER_SCALE * contract_trailing(dv, up_ref[...])).astype(BF16)
         rank_ref[...] = rank_low
         raised = contract_leading(low_ref[...], dv.astype(F32), lax.Precision.HIGHEST)
-        out_ref[:, width:] = raised * (ADAPTER_SCALE * scale)
-        for load in loads:
-            load.wait()
-        out_ref[:, :width] = contract_leading(rank_low, x_ref[...]) * scale
+        out_ref[:, width:] = (raised * (ADAPTER_SCALE * scale)).astype(BF16)
+        x_rows = jnp.concatenate([x_mine_ref[...], x_theirs_ref[...]], axis=0)
+        out_ref[:, :width] = (contract_leading(rank_low, x_rows) * scale).astype(BF16)
 
     return pl.pallas_call(
         kernel,
-        in_specs=[vmem()] * 4 + [hbm()] * 2,
+        in_specs=[vmem()] * 6,
         out_specs=[vmem()] * 2,
         out_shape=[
             jax.ShapeDtypeStruct((2 * tokens, rank), BF16),
-            jax.ShapeDtypeStruct((rank, width + kv), F32),
+            jax.ShapeDtypeStruct((rank, width + kv), BF16),
         ],
-        scratch_shapes=[pltpu.VMEM((2 * tokens, width), BF16), dma(2)],
         compiler_params=params(),
         cost_estimate=SMALL,
         name="adapter_grad",
@@ -679,7 +611,9 @@
     part_rows = half // (seq_count // 2)
     longest = tokens * seq_count // 4
     back = -(-longest // tokens)
-    me = jnp.stack([here, lax.axis_index("fsdp")]).astype(jnp.int32)
+    me = jnp.concatenate(
+        [jnp.stack([here, lax.axis_index("fsdp")]), packed_document_lengths[0]]
+    ).astype(jnp.int32)
     pieces = Pieces(half, seq_count, fsdp_count)
     ring = ring_order(fsdp_count)
 
@@ -706,9 +640,10 @@
 
     ring_step(arrived, ring[:2], "weight_ring")
     arrived[0], x = after((arrived[0], x))
-    key_blocks = [shift(k, "seq", by, "key_halo") for by in range(back, 0, -1)] + [k]
-    x_mine, x_sent = x_halves_call(me, x, fsdp_count)
-    probs, dv_blocks = probs_call(me, packed_document_lengths, q, o, key_blocks)
+    key_blocks = [shift(k, "seq", by, "key_halo") for by in range(back, 0, -1)]
+    x_mine, x_sent, k = x_halves_call(me, x, k, fsdp_count)
+    key_blocks.append(k)
+    probs, dv_blocks = probs_call(me, q, o, key_blocks)
     arrived, across, dv_blocks, x_mine, x_sent = after(
         (arrived, across, dv_blocks, x_mine, x_sent)
     )

time: 94.3 us -> 90.5 us (0.960)
  waiting for transfers between devices: 28.2 us -> 25.3 us
  Pallas kernels: 22.4 us -> 19.7 us
  starting transfers between devices: 36.9 us -> 38.7 us
    pallas_call x7, Pallas kernels: 19.5 us -> 16.8 us  [the longest x1 4.03 us: scores_grad_call(): pl.pallas_call(kernel, in_specs=[vmem()] * (2 * back + 5), out_specs=[vme...]
    ppermute x5, waiting for transfers between devices: 5.13 us -> 3.59 us  [turn(): lax.ppermute(value, axis, [(i, (i + by) % size) for i in range(size)])]
    ppermute x8, starting transfers between devices: 14.2 us -> 15.5 us  [shift(): lax.ppermute(value, axis, [(i, i + by) for i in range(size) if 0 <= i + b...]
    ppermute x16, starting transfers between devices: 16 us -> 17.3 us  [flip(): return lax.ppermute(value, axis, [(i, i ^ choose(i)) for i in range(size)])]
    unnamed x18 -> x14, local copies, waits for them, and re-layouts: 3.18 us -> 2.52 us
  transfers between devices with their start and end apart: 29 -> 29, of which waited for: 11 -> 12; matrix products, arithmetic and copies ran while one was open for 0% -> 1% of each run, Pallas kernels for 24% -> 22%
where the time goes in v5:
time: 90.5 us; the launch traced here: 90.1 us
  starting transfers between devices  38.7 us (43%)
  waiting for transfers between devices  25.3 us (28%)
  Pallas kernels  19.7 us (22%)
  local copies, waits for them, and re-layouts  3.72 us (4%)
  other arithmetic  1.67 us (2%)
  between operations  1 us (1%)
    ppermute x16, starting transfers between devices, flip(): return lax.ppermute(value, axis, [(i, i ^ choose(i)) for i in range(size)])  17.3 us
    ppermute x8, starting transfers between devices, shift(): lax.ppermute(value, axis, [(i, i + by) for i in range(size) if 0 <= i + b...  15.5 us
    ppermute x16, waiting for transfers between devices, flip(): return lax.ppermute(value, axis, [(i, i ^ choose(i)) for i in range(size)])  14.3 us
    ppermute x8, waiting for transfers between devices, shift(): lax.ppermute(value, axis, [(i, i + by) for i in range(size) if 0 <= i + b...  7.49 us
    ppermute x5, starting transfers between devices, turn(): lax.ppermute(value, axis, [(i, (i + by) % size) for i in range(size)])  5.9 us
    pallas_call x1, Pallas kernels, scores_grad_call(): pl.pallas_call(kernel, in_specs=[vmem()] * (2 * back + 5), out_specs=[vme...  4.03 us
    pallas_call x1, Pallas kernels, input_grad_call(): pl.pallas_call(kernel, in_specs=[smem()] + [vmem()] * (5 + len(arrays)),...  3.6 us
    ppermute x5, waiting for transfers between devices, turn(): lax.ppermute(value, axis, [(i, (i + by) % size) for i in range(size)])  3.59 us
  transfers between devices with their start and end apart: 29, of which 12 were waited for; matrix products, arithmetic and copies ran while one was open for 1% of the time, Pallas kernels for 22%

profile of v5, /device:TPU:0, one launch (start us, length us, event | category | flops | bytes accessed | tf_op | source)
XLA Modules:
  0.0 90.1 jit_solution(5163009815131273885)
XLA Ops:
  1.9 5.1 %collective-permute-start.1 = (bf16[256,512]{1,0:T(8,128)(2,1)S(1)}, bf16[256,512]{1,0:T(8,128)(2,1)S(1)}, u32[]{:S(2)}, u32[]{:S(2)}) collective-permute-start(bf16[256,512]{1,0:T(8,128)(2,1)S(1)} %get-tuple-element.164), channel_id=1, source_target_pairs={{0,3},{1,0},{2,1},{3,2},{4,7},{5,4},{6,5},{7,6},{8,11},{9,8},{10,9... | collective-permute-start | bytes 786440 | tf_op jit(solution)/shard_map/weight_ring/ppermute | solution.py:55
  7.0 1.5 %collective-permute-start.3 = (bf16[128,512]{1,0:T(8,128)(2,1)}, bf16[128,512]{1,0:T(8,128)(2,1)S(1)}, u32[]{:S(2)}, u32[]{:S(2)}) collective-permute-start(bf16[128,512]{1,0:T(8,128)(2,1)} %bitcast.16), channel_id=1, source_target_pairs={{0,4},{4,8},{8,12},{12,16},{16,20},{20,24},{24,28},{1,5},{5,9},{9,... | collective-permute-start | bytes 393224 | tf_op jit(solution)/shard_map/key_halo/ppermute | solution.py:49
  8.5 3.9 %collective-permute-start.2 = (bf16[128,512]{1,0:T(8,128)(2,1)}, bf16[128,512]{1,0:T(8,128)(2,1)S(1)}, u32[]{:S(2)}, u32[]{:S(2)}) collective-permute-start(bf16[128,512]{1,0:T(8,128)(2,1)} %bitcast.17), channel_id=1, source_target_pairs={{0,8},{4,12},{8,16},{12,20},{16,24},{20,28},{1,9},{5,13},{9,17},{1... | collective-permute-start | bytes 393224 | tf_op jit(solution)/shard_map/key_halo/ppermute | solution.py:49
  13.1 1.6 %copy-done.3 = bf16[1,128,8192]{2,1,0:T(8,128)(2,1)S(1)} copy-done((bf16[1,128,8192]{2,1,0:T(8,128)(2,1)S(1)}, bf16[1,128,8192]{2,1,0:T(8,128)(2,1)}, u32[]{:S(2)}) %copy-start.3) | copy-done | bytes 2097176
  16.6 2.9 %probs.1 = (bf16[4,256,1024]{2,1,0:T(8,128)(2,1)S(1)}, bf16[128,512]{1,0:T(8,128)(2,1)S(1)}, bf16[128,512]{1,0:T(8,128)(2,1)S(1)}, f32[128,512]{1,0:T(8,128)S(1)}) custom-call(s32[10]{0:T(128)S(1)} %pad_add_fusion.me_ref, bf16[128,4096]{1,0:T(8,128)(2,1)S(1)} %bitcast.11, bf16[128,4096]{1,0:T(8,128)(2,1)S(1)} %bitcast.13, ...), custom_call_target="tpu_custom_call" | custom-call | flops 1 | bytes 1 | tf_op jit(solution)/shard_map/probs/pallas_call | solution.py:176
  20.9 2.0 %collective-permute-start.6 = (bf16[256,512]{1,0:T(8,128)(2,1)S(1)}, bf16[256,512]{1,0:T(8,128)(2,1)S(1)}, u32[]{:S(2)}, u32[]{:S(2)}) collective-permute-start(bf16[256,512]{1,0:T(8,128)(2,1)S(1)} %collective-permute-done.refs_0_), channel_id=1, source_target_pairs={{0,16},{4,12},{8,24},{12,4},{16,0},{20,28},{24,8},{28,20},{1,17},{... | collective-permute-start | bytes 786440 | tf_op jit(solution)/shard_map/weight_chip_1/ppermute | solution.py:43
  26.4 3.0 %own_values.1 = (f32[256,512]{1,0:T(8,128)S(1)}, f32[256,16]{1,0:T(8,128)S(1)}) custom-call(s32[10]{0:T(128)S(1)} %pad_add_fusion.me_ref, bf16[128,4096]{1,0:T(8,128)(2,1)S(1)} %get-tuple-element.96.mine_ref.x_mine_ref, bf16[128,4096]{1,0:T(8,128)(2,1)S(1)} %collective-permute-done.10.theirs_ref.x_theirs_ref, bf16[16,8192]{1,0:T(8,128)(2,1)S(1)} %copy-done.4, ...), custom_call_target="tpu_custom_call" | custom-call | flops 1 | bytes 1 | tf_op jit(solution)/shard_map/own_values/pallas_call | solution.py:352
  30.2 3.3 %collective-permute-done.9 = bf16[128,512]{1,0:T(8,128)(2,1)S(1)} collective-permute-done((bf16[128,512]{1,0:T(8,128)(2,1)S(1)}, bf16[128,512]{1,0:T(8,128)(2,1)S(1)}, u32[]{:S(2)}, u32[]{:S(2)}) %collective-permute-start.9) | collective-permute-done | bytes 131104 | tf_op jit(solution)/shard_map/value_grad_halo/ppermute | solution.py:49
  33.5 2.0 %collective-permute-start.12 = (bf16[256,512]{1,0:T(8,128)(2,1)S(1)}, bf16[256,512]{1,0:T(8,128)(2,1)S(1)}, u32[]{:S(2)}, u32[]{:S(2)}) collective-permute-start(bf16[256,512]{1,0:T(8,128)(2,1)S(1)} %collective-permute-done.1.refs_8_), channel_id=1, source_target_pairs={{0,16},{4,12},{8,24},{12,4},{16,0},{20,28},{24,8},{28,20},{1,17},{... | collective-permute-start | bytes 786440 | tf_op jit(solution)/shard_map/weight_chip_1/ppermute | solution.py:43
  39.6 2.3 %collective-permute-done.12.refs_10_ = bf16[256,512]{1,0:T(8,128)(2,1)S(1)} collective-permute-done((bf16[256,512]{1,0:T(8,128)(2,1)S(1)}, bf16[256,512]{1,0:T(8,128)(2,1)S(1)}, u32[]{:S(2)}, u32[]{:S(2)}) %collective-permute-start.12) | collective-permute-done | bytes 262176 | tf_op jit(solution)/shard_map/weight_chip_1/ppermute | solution.py:43
  42.2 2.7 %collective-permute-start.18 = (bf16[16,4608]{1,0:T(8,128)(2,1)S(1)}, bf16[16,4608]{1,0:T(8,128)(2,1)S(1)}, u32[]{:S(2)}, u32[]{:S(2)}) collective-permute-start(bf16[16,4608]{1,0:T(8,128)(2,1)S(1)} %get-tuple-element.118), channel_id=1, source_target_pairs={{0,1},{1,0},{2,3},{3,2},{4,5},{5,4},{6,7},{7,6},{8,9},{9,8},{10,11... | collective-permute-start | bytes 442376 | tf_op jit(solution)/shard_map/adapter_sum/ppermute | solution.py:43
  44.8 1.5 %collective-permute-start.15 = (bf16[256,512]{1,0:T(8,128)(2,1)S(1)}, bf16[256,512]{1,0:T(8,128)(2,1)S(1)}, u32[]{:S(2)}, u32[]{:S(2)}) collective-permute-start(bf16[256,512]{1,0:T(8,128)(2,1)S(1)} %collective-permute-done.7.refs_4_), channel_id=1, source_target_pairs={{0,16},{4,12},{8,24},{12,4},{16,0},{20,28},{24,8},{28,20},{1,17},{... | collective-permute-start | bytes 786440 | tf_op jit(solution)/shard_map/weight_chip_1/ppermute | solution.py:43
  46.4 1.7 %collective-permute-start.14 = (bf16[256,512]{1,0:T(8,128)(2,1)S(1)}, bf16[256,512]{1,0:T(8,128)(2,1)S(1)}, u32[]{:S(2)}, u32[]{:S(2)}) collective-permute-start(bf16[256,512]{1,0:T(8,128)(2,1)S(1)} %collective-permute-done.7.refs_4_), channel_id=1, source_target_pairs={{0,8},{4,20},{8,0},{12,28},{16,24},{20,4},{24,16},{28,12},{1,9},{5... | collective-permute-start | bytes 786440 | tf_op jit(solution)/shard_map/weight_chip_0/ppermute | solution.py:43
  48.6 5.3 %collective-permute-done.15.refs_6_ = bf16[256,512]{1,0:T(8,128)(2,1)S(1)} collective-permute-done((bf16[256,512]{1,0:T(8,128)(2,1)S(1)}, bf16[256,512]{1,0:T(8,128)(2,1)S(1)}, u32[]{:S(2)}, u32[]{:S(2)}) %collective-permute-start.15) | collective-permute-done | bytes 262176 | tf_op jit(solution)/shard_map/weight_chip_1/ppermute | solution.py:43
  53.9 1.5 %collective-permute-done.14.refs_5_ = bf16[256,512]{1,0:T(8,128)(2,1)S(1)} collective-permute-done((bf16[256,512]{1,0:T(8,128)(2,1)S(1)}, bf16[256,512]{1,0:T(8,128)(2,1)S(1)}, u32[]{:S(2)}, u32[]{:S(2)}) %collective-permute-start.14) | collective-permute-done | bytes 262176 | tf_op jit(solution)/shard_map/weight_chip_0/ppermute | solution.py:43
  55.3 2.2 %collective-permute-done.16.refs_7_ = bf16[256,512]{1,0:T(8,128)(2,1)S(1)} collective-permute-done((bf16[256,512]{1,0:T(8,128)(2,1)S(1)}, bf16[256,512]{1,0:T(8,128)(2,1)S(1)}, u32[]{:S(2)}, u32[]{:S(2)}) %collective-permute-start.16) | collective-permute-done | bytes 262176 | tf_op jit(solution)/shard_map/weight_ring_across/ppermute | solution.py:55
  58.4 1.5 %more_values.1 = (f32[128,512]{1,0:T(8,128)S(1)}, f32[128,512]{1,0:T(8,128)S(1)}) custom-call(s32[10]{0:T(128)S(1)} %pad_add_fusion.me_ref, f32[256,512]{1,0:T(8,128)S(1)} %get-tuple-element.119.acc_ref, bf16[128,4096]{1,0:T(8,128)(2,1)S(1)} %get-tuple-element.96.mine_ref.x_mine_ref, bf16[128,4096]{1,0:T(8,128)(2,1)S(1)} %collective-permute-done.10.theirs_ref.x_theirs_ref, ...), custom_call_target="tpu_custom_call" | custom-call | flops 1 | bytes 1 | tf_op jit(solution)/shard_map/more_values/pallas_call | solution.py:421
  60.0 2.7 %collective-permute-done.20 = bf16[16,4608]{1,0:T(8,128)(2,1)S(1)} collective-permute-done((bf16[16,4608]{1,0:T(8,128)(2,1)S(1)}, bf16[16,4608]{1,0:T(8,128)(2,1)S(1)}, u32[]{:S(2)}, u32[]{:S(2)}) %collective-permute-start.20) | collective-permute-done | bytes 147488 | tf_op jit(solution)/shard_map/adapter_sum/ppermute | solution.py:43
  65.0 3.8 %collective-permute-start.21 = (bf16[128,512]{1,0:T(8,128)(2,1)S(1)}, bf16[128,512]{1,0:T(8,128)(2,1)S(1)}, u32[]{:S(2)}, u32[]{:S(2)}) collective-permute-start(bf16[128,512]{1,0:T(8,128)(2,1)S(1)} %add_convert_fusion.4.refs_5_), channel_id=1, source_target_pairs={{0,8},{4,12},{8,16},{12,20},{16,24},{20,28},{1,9},{5,13},{9,17},{1... | collective-permute-start | bytes 393224 | tf_op jit(solution)/shard_map/value_halo/ppermute | solution.py:49
  68.8 3.6 %input_grad.1 = (bf16[128,8192]{1,0:T(8,128)(2,1)}, bf16[128,4096]{1,0:T(8,128)(2,1)S(1)}) custom-call(s32[10]{0:T(128)S(1)} %pad_add_fusion.me_ref, bf16[128,512]{1,0:T(8,128)(2,1)S(1)} %add_convert_fusion.5.mine_ref, bf16[128,512]{1,0:T(8,128)(2,1)S(1)} %collective-permute-done.13.theirs_ref, bf16[256,16]{1,0:T(8,128)(2,1)S(1)} %get-tuple-element.138.rank_ref, ...), custom_call_target="tpu_custom_call" | custom-call | flops 1 | bytes 1 | tf_op jit(solution)/shard_map/input_grad/pallas_call | solution.py:473
  72.5 2.1 %collective-permute-start.24 = (bf16[16,4608]{1,0:T(8,128)(2,1)S(1)}, bf16[16,4608]{1,0:T(8,128)(2,1)S(1)}, u32[]{:S(2)}, u32[]{:S(2)}) collective-permute-start(bf16[16,4608]{1,0:T(8,128)(2,1)S(1)} %add_convert_fusion), channel_id=1, source_target_pairs={{0,8},{4,12},{8,0},{12,4},{16,24},{20,28},{24,16},{28,20},{1,9},{5... | collective-permute-start | bytes 442376 | tf_op jit(solution)/shard_map/adapter_sum/ppermute | solution.py:43
  74.6 4.0 %scores_grad.1 = (bf16[128,4096]{1,0:T(8,128)(2,1)}, bf16[128,512]{1,0:T(8,128)(2,1)S(1)}, bf16[128,512]{1,0:T(8,128)(2,1)S(1)}, f32[128,512]{1,0:T(8,128)S(1)}) custom-call(bf16[4,256,1024]{2,1,0:T(8,128)(2,1)S(1)} %get-tuple-element.142.p_ref, bf16[128,4096]{1,0:T(8,128)(2,1)S(1)} %bitcast.12, bf16[128,4096]{1,0:T(8,128)(2,1)S(1)} %bitcast.14, ...), custom_call_target="tpu_custom_call" | custom-call | flops 1 | bytes 1 | tf_op jit(solution)/shard_map/scores_grad/pallas_call | solution.py:224
  83.7 1.5 %put_half.1 = bf16[128,8192]{1,0:T(8,128)(2,1)} custom-call(s32[10]{0:T(128)S(1)} %pad_add_fusion.me_ref, bf16[128,4096]{1,0:T(8,128)(2,1)S(1)} %collective-permute-done.27.theirs_ref, bf16[128,8192]{1,0:T(8,128)(2,1)} %get-tuple-element.152.out_in), custom_call_target="tpu_custom_call", output_to_operand_aliasing={{}: (2, {})} | custom-call | flops 1 | bytes 1 | tf_op jit(solution)/shard_map/put_half/pallas_call | solution.py:286
  85.3 4.2 %collective-permute-done.26 = bf16[128,512]{1,0:T(8,128)(2,1)S(1)} collective-permute-done((bf16[128,512]{1,0:T(8,128)(2,1)S(1)}, bf16[128,512]{1,0:T(8,128)(2,1)S(1)}, u32[]{:S(2)}, u32[]{:S(2)}) %collective-permute-start.26) | collective-permute-done | bytes 131104 | tf_op jit(solution)/shard_map/key_grad_halo/ppermute | solution.py:49
  (66 shorter events, 23.4 us)
Async XLA Ops:
  1.9 17.6 %collective-permute-start.1 = (bf16[256,512]{1,0:T(8,128)(2,1)S(1)}, bf16[256,512]{1,0:T(8,128)(2,1)S(1)}, u32[]{:S(2)}, u32[]{:S(2)}) collective-permute-start(bf16[256,512]{1,0:T(8,128)(2,1)S(1)} %get-tuple-element.164), channel_id=1, source_target_pairs={{0,3},{1,0},{2,1},{3,2},{4,7},{5,4},{6,5},{7,6},{8,11},{9,8},{10,9... | collective-permute-start | bytes 786440 | tf_op jit(solution)/shard_map/weight_ring/ppermute | solution.py:55
  7.0 12.5 %collective-permute-start = (bf16[256,512]{1,0:T(8,128)(2,1)S(1)}, bf16[256,512]{1,0:T(8,128)(2,1)S(1)}, u32[]{:S(2)}, u32[]{:S(2)}) collective-permute-start(bf16[256,512]{1,0:T(8,128)(2,1)S(1)} %get-tuple-element.164), channel_id=1, source_target_pairs={{0,1},{1,2},{2,3},{3,0},{4,5},{5,6},{6,7},{7,4},{8,9},{9,10},{10,1... | collective-permute-start | bytes 786440 | tf_op jit(solution)/shard_map/weight_ring/ppermute | solution.py:55
  7.0 9.6 %collective-permute-start.3 = (bf16[128,512]{1,0:T(8,128)(2,1)}, bf16[128,512]{1,0:T(8,128)(2,1)S(1)}, u32[]{:S(2)}, u32[]{:S(2)}) collective-permute-start(bf16[128,512]{1,0:T(8,128)(2,1)} %bitcast.16), channel_id=1, source_target_pairs={{0,4},{4,8},{8,12},{12,16},{16,20},{20,24},{24,28},{1,5},{5,9},{9,... | collective-permute-start | bytes 393224 | tf_op jit(solution)/shard_map/key_halo/ppermute | solution.py:49
  8.5 8.1 %collective-permute-start.2 = (bf16[128,512]{1,0:T(8,128)(2,1)}, bf16[128,512]{1,0:T(8,128)(2,1)S(1)}, u32[]{:S(2)}, u32[]{:S(2)}) collective-permute-start(bf16[128,512]{1,0:T(8,128)(2,1)} %bitcast.17), channel_id=1, source_target_pairs={{0,8},{4,12},{8,16},{12,20},{16,24},{20,28},{1,9},{5,13},{9,17},{1... | collective-permute-start | bytes 393224 | tf_op jit(solution)/shard_map/key_halo/ppermute | solution.py:49
  19.5 5.5 %collective-permute-start.10 = (bf16[128,4096]{1,0:T(8,128)(2,1)S(1)}, bf16[128,4096]{1,0:T(8,128)(2,1)S(1)}, u32[]{:S(2)}, u32[]{:S(2)}) collective-permute-start(bf16[128,4096]{1,0:T(8,128)(2,1)S(1)} %get-tuple-element.97), channel_id=1, source_target_pairs={{0,4},{4,0},{8,12},{12,8},{16,20},{20,16},{24,28},{28,24},{1,5},{5... | collective-permute-start | bytes 3145736 | tf_op jit(solution)/shard_map/x_core/ppermute | solution.py:43
  20.9 12.6 %collective-permute-start.7 = (bf16[256,512]{1,0:T(8,128)(2,1)S(1)}, bf16[256,512]{1,0:T(8,128)(2,1)S(1)}, u32[]{:S(2)}, u32[]{:S(2)}) collective-permute-start(bf16[256,512]{1,0:T(8,128)(2,1)S(1)} %collective-permute-done.refs_0_), channel_id=1, source_target_pairs={{0,1},{1,2},{2,3},{3,0},{4,5},{5,6},{6,7},{7,4},{8,9},{9,10},{10,1... | collective-permute-start | bytes 786440 | tf_op jit(solution)/shard_map/weight_ring/ppermute | solution.py:55
  20.9 12.6 %collective-permute-start.6 = (bf16[256,512]{1,0:T(8,128)(2,1)S(1)}, bf16[256,512]{1,0:T(8,128)(2,1)S(1)}, u32[]{:S(2)}, u32[]{:S(2)}) collective-permute-start(bf16[256,512]{1,0:T(8,128)(2,1)S(1)} %collective-permute-done.refs_0_), channel_id=1, source_target_pairs={{0,16},{4,12},{8,24},{12,4},{16,0},{20,28},{24,8},{28,20},{1,17},{... | collective-permute-start | bytes 786440 | tf_op jit(solution)/shard_map/weight_chip_1/ppermute | solution.py:43
  22.9 10.6 %collective-permute-start.5 = (bf16[256,512]{1,0:T(8,128)(2,1)S(1)}, bf16[256,512]{1,0:T(8,128)(2,1)S(1)}, u32[]{:S(2)}, u32[]{:S(2)}) collective-permute-start(bf16[256,512]{1,0:T(8,128)(2,1)S(1)} %collective-permute-done.refs_0_), channel_id=1, source_target_pairs={{0,8},{4,20},{8,0},{12,28},{16,24},{20,4},{24,16},{28,12},{1,9},{5... | collective-permute-start | bytes 786440 | tf_op jit(solution)/shard_map/weight_chip_0/ppermute | solution.py:43
  23.7 5.7 %collective-permute-start.8 = (bf16[128,512]{1,0:T(8,128)(2,1)S(1)}, bf16[128,512]{1,0:T(8,128)(2,1)S(1)}, u32[]{:S(2)}, u32[]{:S(2)}) collective-permute-start(bf16[128,512]{1,0:T(8,128)(2,1)S(1)} %get-tuple-element.94), channel_id=1, source_target_pairs={{4,0},{8,4},{12,8},{16,12},{20,16},{24,20},{28,24},{5,1},{9,5},{13... | collective-permute-start | bytes 393224 | tf_op jit(solution)/shard_map/value_grad_halo/ppermute | solution.py:49
  25.0 8.5 %collective-permute-start.9 = (bf16[128,512]{1,0:T(8,128)(2,1)S(1)}, bf16[128,512]{1,0:T(8,128)(2,1)S(1)}, u32[]{:S(2)}, u32[]{:S(2)}) collective-permute-start(bf16[128,512]{1,0:T(8,128)(2,1)S(1)} %get-tuple-element.95), channel_id=1, source_target_pairs={{8,0},{12,4},{16,8},{20,12},{24,16},{28,20},{9,1},{13,5},{17,9},{2... | collective-permute-start | bytes 393224 | tf_op jit(solution)/shard_map/value_grad_halo/ppermute | solution.py:49
  29.4 10.2 %collective-permute-start.4 = (bf16[256,512]{1,0:T(8,128)(2,1)S(1)}, bf16[256,512]{1,0:T(8,128)(2,1)S(1)}, u32[]{:S(2)}, u32[]{:S(2)}) collective-permute-start(bf16[256,512]{1,0:T(8,128)(2,1)S(1)} %get-tuple-element.91), channel_id=1, source_target_pairs={{0,1},{1,2},{2,3},{3,0},{4,5},{5,6},{6,7},{7,4},{8,9},{9,10},{10,1... | collective-permute-start | bytes 786440 | tf_op jit(solution)/shard_map/weight_ring_across/ppermute | solution.py:55
  33.5 8.4 %collective-permute-start.12 = (bf16[256,512]{1,0:T(8,128)(2,1)S(1)}, bf16[256,512]{1,0:T(8,128)(2,1)S(1)}, u32[]{:S(2)}, u32[]{:S(2)}) collective-permute-start(bf16[256,512]{1,0:T(8,128)(2,1)S(1)} %collective-permute-done.1.refs_8_), channel_id=1, source_target_pairs={{0,16},{4,12},{8,24},{12,4},{16,0},{20,28},{24,8},{28,20},{1,17},{... | collective-permute-start | bytes 786440 | tf_op jit(solution)/shard_map/weight_chip_1/ppermute | solution.py:43
  35.6 6.6 %collective-permute-start.11 = (bf16[256,512]{1,0:T(8,128)(2,1)S(1)}, bf16[256,512]{1,0:T(8,128)(2,1)S(1)}, u32[]{:S(2)}, u32[]{:S(2)}) collective-permute-start(bf16[256,512]{1,0:T(8,128)(2,1)S(1)} %collective-permute-done.1.refs_8_), channel_id=1, source_target_pairs={{0,8},{4,20},{8,0},{12,28},{16,24},{20,4},{24,16},{28,12},{1,9},{5... | collective-permute-start | bytes 786440 | tf_op jit(solution)/shard_map/weight_chip_0/ppermute | solution.py:43
  42.2 6.4 %collective-permute-start.18 = (bf16[16,4608]{1,0:T(8,128)(2,1)S(1)}, bf16[16,4608]{1,0:T(8,128)(2,1)S(1)}, u32[]{:S(2)}, u32[]{:S(2)}) collective-permute-start(bf16[16,4608]{1,0:T(8,128)(2,1)S(1)} %get-tuple-element.118), channel_id=1, source_target_pairs={{0,1},{1,0},{2,3},{3,2},{4,5},{5,4},{6,7},{7,6},{8,9},{9,8},{10,11... | collective-permute-start | bytes 442376 | tf_op jit(solution)/shard_map/adapter_sum/ppermute | solution.py:43
  44.8 9.0 %collective-permute-start.15 = (bf16[256,512]{1,0:T(8,128)(2,1)S(1)}, bf16[256,512]{1,0:T(8,128)(2,1)S(1)}, u32[]{:S(2)}, u32[]{:S(2)}) collective-permute-start(bf16[256,512]{1,0:T(8,128)(2,1)S(1)} %collective-permute-done.7.refs_4_), channel_id=1, source_target_pairs={{0,16},{4,12},{8,24},{12,4},{16,0},{20,28},{24,8},{28,20},{1,17},{... | collective-permute-start | bytes 786440 | tf_op jit(solution)/shard_map/weight_chip_1/ppermute | solution.py:43
  46.4 9.0 %collective-permute-start.14 = (bf16[256,512]{1,0:T(8,128)(2,1)S(1)}, bf16[256,512]{1,0:T(8,128)(2,1)S(1)}, u32[]{:S(2)}, u32[]{:S(2)}) collective-permute-start(bf16[256,512]{1,0:T(8,128)(2,1)S(1)} %collective-permute-done.7.refs_4_), channel_id=1, source_target_pairs={{0,8},{4,20},{8,0},{12,28},{16,24},{20,4},{24,16},{28,12},{1,9},{5... | collective-permute-start | bytes 786440 | tf_op jit(solution)/shard_map/weight_chip_0/ppermute | solution.py:43
  48.0 9.4 %collective-permute-start.16 = (bf16[256,512]{1,0:T(8,128)(2,1)S(1)}, bf16[256,512]{1,0:T(8,128)(2,1)S(1)}, u32[]{:S(2)}, u32[]{:S(2)}) collective-permute-start(bf16[256,512]{1,0:T(8,128)(2,1)S(1)} %collective-permute-done.4.refs_3_), channel_id=1, source_target_pairs={{0,1},{1,2},{2,3},{3,0},{4,5},{5,6},{6,7},{7,4},{8,9},{9,10},{10,1... | collective-permute-start | bytes 786440 | tf_op jit(solution)/shard_map/weight_ring_across/ppermute | solution.py:55
  48.0 9.4 %collective-permute-start.17 = (bf16[256,512]{1,0:T(8,128)(2,1)S(1)}, bf16[256,512]{1,0:T(8,128)(2,1)S(1)}, u32[]{:S(2)}, u32[]{:S(2)}) collective-permute-start(bf16[256,512]{1,0:T(8,128)(2,1)S(1)} %collective-permute-done.11.refs_9_), channel_id=1, source_target_pairs={{0,16},{4,12},{8,24},{12,4},{16,0},{20,28},{24,8},{28,20},{1,17},{... | collective-permute-start | bytes 786440 | tf_op jit(solution)/shard_map/weight_chip_1/ppermute | solution.py:43
  62.7 9.7 %collective-permute-start.23 = (bf16[16,4608]{1,0:T(8,128)(2,1)S(1)}, bf16[16,4608]{1,0:T(8,128)(2,1)S(1)}, u32[]{:S(2)}, u32[]{:S(2)}) collective-permute-start(bf16[16,4608]{1,0:T(8,128)(2,1)S(1)} %add_convert_fusion.1), channel_id=1, source_target_pairs={{0,2},{1,3},{2,0},{3,1},{4,6},{5,7},{6,4},{7,5},{8,10},{9,11},{10,... | collective-permute-start | bytes 442376 | tf_op jit(solution)/shard_map/adapter_sum/ppermute | solution.py:43
  63.8 8.7 %collective-permute-start.22 = (bf16[128,512]{1,0:T(8,128)(2,1)S(1)}, bf16[128,512]{1,0:T(8,128)(2,1)S(1)}, u32[]{:S(2)}, u32[]{:S(2)}) collective-permute-start(bf16[128,512]{1,0:T(8,128)(2,1)S(1)} %add_convert_fusion.4.refs_5_), channel_id=1, source_target_pairs={{0,4},{4,8},{8,12},{12,16},{16,20},{20,24},{24,28},{1,5},{5,9},{9,... | collective-permute-start | bytes 393224 | tf_op jit(solution)/shard_map/value_halo/ppermute | solution.py:49
  65.0 7.4 %collective-permute-start.21 = (bf16[128,512]{1,0:T(8,128)(2,1)S(1)}, bf16[128,512]{1,0:T(8,128)(2,1)S(1)}, u32[]{:S(2)}, u32[]{:S(2)}) collective-permute-start(bf16[128,512]{1,0:T(8,128)(2,1)S(1)} %add_convert_fusion.4.refs_5_), channel_id=1, source_target_pairs={{0,8},{4,12},{8,16},{12,20},{16,24},{20,28},{1,9},{5,13},{9,17},{1... | collective-permute-start | bytes 393224 | tf_op jit(solution)/shard_map/value_halo/ppermute | solution.py:49
  72.5 6.6 %collective-permute-start.24 = (bf16[16,4608]{1,0:T(8,128)(2,1)S(1)}, bf16[16,4608]{1,0:T(8,128)(2,1)S(1)}, u32[]{:S(2)}, u32[]{:S(2)}) collective-permute-start(bf16[16,4608]{1,0:T(8,128)(2,1)S(1)} %add_convert_fusion), channel_id=1, source_target_pairs={{0,8},{4,12},{8,0},{12,4},{16,24},{20,28},{24,16},{28,20},{1,9},{5... | collective-permute-start | bytes 442376 | tf_op jit(solution)/shard_map/adapter_sum/ppermute | solution.py:43
  79.7 5.5 %collective-permute-start.25 = (bf16[128,512]{1,0:T(8,128)(2,1)S(1)}, bf16[128,512]{1,0:T(8,128)(2,1)S(1)}, u32[]{:S(2)}, u32[]{:S(2)}) collective-permute-start(bf16[128,512]{1,0:T(8,128)(2,1)S(1)} %get-tuple-element.149), channel_id=1, source_target_pairs={{4,0},{8,4},{12,8},{16,12},{20,16},{24,20},{28,24},{5,1},{9,5},{13... | collective-permute-start | bytes 393224 | tf_op jit(solution)/shard_map/key_grad_halo/ppermute | solution.py:49
  81.0 8.4 %collective-permute-start.26 = (bf16[128,512]{1,0:T(8,128)(2,1)S(1)}, bf16[128,512]{1,0:T(8,128)(2,1)S(1)}, u32[]{:S(2)}, u32[]{:S(2)}) collective-permute-start(bf16[128,512]{1,0:T(8,128)(2,1)S(1)} %get-tuple-element.150), channel_id=1, source_target_pairs={{8,0},{12,4},{16,8},{20,12},{24,16},{28,20},{9,1},{13,5},{17,9},{2... | collective-permute-start | bytes 393224 | tf_op jit(solution)/shard_map/key_grad_halo/ppermute | solution.py:49
  (12 other events, 83.6 us)

commit v6 on v5

--- a/solution.py
+++ b/solution.py
@@ -656,7 +656,10 @@
         set_out(ring[:1])
     x_theirs = swap(x_sent, "x_core")
     acc, low = own_values_call(me, x_mine, x_theirs, down, up, w)
-    held, arrived, dv_back, acc, low = after((held, arrived, dv_back, acc, low))
+    held, late, dv_back, acc, low = after(
+        (held, {by: arrived[by] for by in ring[2:]}, dv_back, acc, low)
+    )
+    arrived.update(late)
 
     if direct:
         set_out(ring[1:2])
@@ -697,7 +700,7 @@
     )
 
     values = (values + swap(values_sent, "values_core")).astype(BF16)
-    values, dv_mine, sums = after((values, dv_mine, sums))
+    values, dv_mine = after((values, dv_mine))
     value_blocks = [shift(values, "seq", by, "value_halo") for by in range(back, 0, -1)] + [values]
     while len(steps) > 1:
         sums = sum_step(sums, steps.pop(0))

time: 90.5 us -> 89.9 us (level)
  waiting for transfers between devices: 25.3 us -> 21.5 us
  starting transfers between devices: 38.7 us -> 41.9 us
    ppermute x16, waiting for transfers between devices: 14.3 us -> 8.26 us  [flip(): return lax.ppermute(value, axis, [(i, i ^ choose(i)) for i in range(size)])]
    ppermute x5, waiting for transfers between devices: 3.59 us -> 8.32 us  [turn(): lax.ppermute(value, axis, [(i, (i + by) % size) for i in range(size)])]
    ppermute x8, waiting for transfers between devices: 7.49 us -> 4.89 us  [shift(): lax.ppermute(value, axis, [(i, i + by) for i in range(size) if 0 <= i + b...]
    ppermute x5, starting transfers between devices: 5.9 us -> 8.1 us  [turn(): lax.ppermute(value, axis, [(i, (i + by) % size) for i in range(size)])]
    ppermute x16, starting transfers between devices: 17.3 us -> 18.8 us  [flip(): return lax.ppermute(value, axis, [(i, i ^ choose(i)) for i in range(size)])]
  transfers between devices with their start and end apart: 29 -> 29, of which waited for: 12 -> 8; matrix products, arithmetic and copies ran while one was open for 1% -> 1% of each run, Pallas kernels for 22% -> 22%
where the time goes in v6:
time: 89.9 us; the launch traced here: 89.5 us
  starting transfers between devices  41.9 us (47%)
  waiting for transfers between devices  21.5 us (24%)
  Pallas kernels  19.7 us (22%)
  local copies, waits for them, and re-layouts  3.72 us (4%)
  other arithmetic  1.68 us (2%)
  between operations  0.98 us (1%)
    ppermute x16, starting transfers between devices, flip(): return lax.ppermute(value, axis, [(i, i ^ choose(i)) for i in range(size)])  18.8 us
    ppermute x8, starting transfers between devices, shift(): lax.ppermute(value, axis, [(i, i + by) for i in range(size) if 0 <= i + b...  15.1 us
    ppermute x5, waiting for transfers between devices, turn(): lax.ppermute(value, axis, [(i, (i + by) % size) for i in range(size)])  8.32 us
    ppermute x16, waiting for transfers between devices, flip(): return lax.ppermute(value, axis, [(i, i ^ choose(i)) for i in range(size)])  8.26 us
    ppermute x5, starting transfers between devices, turn(): lax.ppermute(value, axis, [(i, (i + by) % size) for i in range(size)])  8.1 us
    ppermute x8, waiting for transfers between devices, shift(): lax.ppermute(value, axis, [(i, i + by) for i in range(size) if 0 <= i + b...  4.89 us
    pallas_call x1, Pallas kernels, scores_grad_call(): pl.pallas_call(kernel, in_specs=[vmem()] * (2 * back + 5), out_specs=[vme...  4.03 us
    pallas_call x1, Pallas kernels, input_grad_call(): pl.pallas_call(kernel, in_specs=[smem()] + [vmem()] * (5 + len(arrays)),...  3.59 us
  transfers between devices with their start and end apart: 29, of which 8 were waited for; matrix products, arithmetic and copies ran while one was open for 1% of the time, Pallas kernels for 22%

profile of v6, /device:TPU:0, one launch (start us, length us, event | category | flops | bytes accessed | tf_op | source)
XLA Modules:
  0.0 89.5 jit_solution(15775092256488413233)
XLA Ops:
  1.9 5.1 %collective-permute-start.1 = (bf16[256,512]{1,0:T(8,128)(2,1)S(1)}, bf16[256,512]{1,0:T(8,128)(2,1)S(1)}, u32[]{:S(2)}, u32[]{:S(2)}) collective-permute-start(bf16[256,512]{1,0:T(8,128)(2,1)S(1)} %get-tuple-element.160), channel_id=1, source_target_pairs={{0,3},{1,0},{2,1},{3,2},{4,7},{5,4},{6,5},{7,6},{8,11},{9,8},{10,9... | collective-permute-start | bytes 786440 | tf_op jit(solution)/shard_map/weight_ring/ppermute | solution.py:55
  7.0 1.5 %collective-permute-start.3 = (bf16[128,512]{1,0:T(8,128)(2,1)}, bf16[128,512]{1,0:T(8,128)(2,1)S(1)}, u32[]{:S(2)}, u32[]{:S(2)}) collective-permute-start(bf16[128,512]{1,0:T(8,128)(2,1)} %bitcast.16), channel_id=1, source_target_pairs={{0,4},{4,8},{8,12},{12,16},{16,20},{20,24},{24,28},{1,5},{5,9},{9,... | collective-permute-start | bytes 393224 | tf_op jit(solution)/shard_map/key_halo/ppermute | solution.py:49
  8.5 3.9 %collective-permute-start.2 = (bf16[128,512]{1,0:T(8,128)(2,1)}, bf16[128,512]{1,0:T(8,128)(2,1)S(1)}, u32[]{:S(2)}, u32[]{:S(2)}) collective-permute-start(bf16[128,512]{1,0:T(8,128)(2,1)} %bitcast.17), channel_id=1, source_target_pairs={{0,8},{4,12},{8,16},{12,20},{16,24},{20,28},{1,9},{5,13},{9,17},{1... | collective-permute-start | bytes 393224 | tf_op jit(solution)/shard_map/key_halo/ppermute | solution.py:49
  13.1 1.6 %copy-done.3 = bf16[1,128,8192]{2,1,0:T(8,128)(2,1)S(1)} copy-done((bf16[1,128,8192]{2,1,0:T(8,128)(2,1)S(1)}, bf16[1,128,8192]{2,1,0:T(8,128)(2,1)}, u32[]{:S(2)}) %copy-start.3) | copy-done | bytes 2097176
  16.6 2.9 %probs.1 = (bf16[4,256,1024]{2,1,0:T(8,128)(2,1)S(1)}, bf16[128,512]{1,0:T(8,128)(2,1)S(1)}, bf16[128,512]{1,0:T(8,128)(2,1)S(1)}, f32[128,512]{1,0:T(8,128)S(1)}) custom-call(s32[10]{0:T(128)S(1)} %pad_add_fusion.me_ref, bf16[128,4096]{1,0:T(8,128)(2,1)S(1)} %bitcast.11, bf16[128,4096]{1,0:T(8,128)(2,1)S(1)} %bitcast.13, ...), custom_call_target="tpu_custom_call" | custom-call | flops 1 | bytes 1 | tf_op jit(solution)/shard_map/probs/pallas_call | solution.py:176
  19.5 1.4 %collective-permute-start.10 = (bf16[128,4096]{1,0:T(8,128)(2,1)S(1)}, bf16[128,4096]{1,0:T(8,128)(2,1)S(1)}, u32[]{:S(2)}, u32[]{:S(2)}) collective-permute-start(bf16[128,4096]{1,0:T(8,128)(2,1)S(1)} %get-tuple-element.94), channel_id=1, source_target_pairs={{0,4},{4,0},{8,12},{12,8},{16,20},{20,16},{24,28},{28,24},{1,5},{5... | collective-permute-start | bytes 3145736 | tf_op jit(solution)/shard_map/x_core/ppermute | solution.py:43
  20.9 2.0 %collective-permute-start.6 = (bf16[256,512]{1,0:T(8,128)(2,1)S(1)}, bf16[256,512]{1,0:T(8,128)(2,1)S(1)}, u32[]{:S(2)}, u32[]{:S(2)}) collective-permute-start(bf16[256,512]{1,0:T(8,128)(2,1)S(1)} %collective-permute-done.refs_0_), channel_id=1, source_target_pairs={{0,16},{4,12},{8,24},{12,4},{16,0},{20,28},{24,8},{28,20},{1,17},{... | collective-permute-start | bytes 786440 | tf_op jit(solution)/shard_map/weight_chip_1/ppermute | solution.py:43
  26.4 3.0 %own_values.1 = (f32[256,512]{1,0:T(8,128)S(1)}, f32[256,16]{1,0:T(8,128)S(1)}) custom-call(s32[10]{0:T(128)S(1)} %pad_add_fusion.me_ref, bf16[128,4096]{1,0:T(8,128)(2,1)S(1)} %get-tuple-element.93.mine_ref.x_mine_ref, bf16[128,4096]{1,0:T(8,128)(2,1)S(1)} %collective-permute-done.10.theirs_ref.x_theirs_ref, bf16[16,8192]{1,0:T(8,128)(2,1)S(1)} %copy-done.4, ...), custom_call_target="tpu_custom_call" | custom-call | flops 1 | bytes 1 | tf_op jit(solution)/shard_map/own_values/pallas_call | solution.py:352
  29.4 4.1 %collective-permute-start.12 = (bf16[256,512]{1,0:T(8,128)(2,1)S(1)}, bf16[256,512]{1,0:T(8,128)(2,1)S(1)}, u32[]{:S(2)}, u32[]{:S(2)}) collective-permute-start(bf16[256,512]{1,0:T(8,128)(2,1)S(1)} %collective-permute-done.1.refs_8_), channel_id=1, source_target_pairs={{0,16},{4,12},{8,24},{12,4},{16,0},{20,28},{24,8},{28,20},{1,17},{... | collective-permute-start | bytes 786440 | tf_op jit(solution)/shard_map/weight_chip_1/ppermute | solution.py:43
  33.5 2.3 %collective-permute-start.11 = (bf16[256,512]{1,0:T(8,128)(2,1)S(1)}, bf16[256,512]{1,0:T(8,128)(2,1)S(1)}, u32[]{:S(2)}, u32[]{:S(2)}) collective-permute-start(bf16[256,512]{1,0:T(8,128)(2,1)S(1)} %collective-permute-done.1.refs_8_), channel_id=1, source_target_pairs={{0,8},{4,20},{8,0},{12,28},{16,24},{20,4},{24,16},{28,12},{1,9},{5... | collective-permute-start | bytes 786440 | tf_op jit(solution)/shard_map/weight_chip_0/ppermute | solution.py:43
  39.0 5.3 %collective-permute-done.4.refs_3_ = bf16[256,512]{1,0:T(8,128)(2,1)S(1)} collective-permute-done((bf16[256,512]{1,0:T(8,128)(2,1)S(1)}, bf16[256,512]{1,0:T(8,128)(2,1)S(1)}, u32[]{:S(2)}, u32[]{:S(2)}) %collective-permute-start.4) | collective-permute-done | bytes 262176 | tf_op jit(solution)/shard_map/weight_ring_across/ppermute | solution.py:55
  45.5 2.0 %collective-permute-start.14 = (bf16[256,512]{1,0:T(8,128)(2,1)S(1)}, bf16[256,512]{1,0:T(8,128)(2,1)S(1)}, u32[]{:S(2)}, u32[]{:S(2)}) collective-permute-start(bf16[256,512]{1,0:T(8,128)(2,1)S(1)} %collective-permute-done.7.refs_4_), channel_id=1, source_target_pairs={{0,8},{4,20},{8,0},{12,28},{16,24},{20,4},{24,16},{28,12},{1,9},{5... | collective-permute-start | bytes 786440 | tf_op jit(solution)/shard_map/weight_chip_0/ppermute | solution.py:43
  47.5 2.0 %collective-permute-start.16 = (bf16[256,512]{1,0:T(8,128)(2,1)S(1)}, bf16[256,512]{1,0:T(8,128)(2,1)S(1)}, u32[]{:S(2)}, u32[]{:S(2)}) collective-permute-start(bf16[256,512]{1,0:T(8,128)(2,1)S(1)} %collective-permute-done.4.refs_3_), channel_id=1, source_target_pairs={{0,1},{1,2},{2,3},{3,0},{4,5},{5,6},{6,7},{7,4},{8,9},{9,10},{10,1... | collective-permute-start | bytes 786440 | tf_op jit(solution)/shard_map/weight_ring_across/ppermute | solution.py:55
  49.8 2.9 %collective-permute-done.15.refs_6_ = bf16[256,512]{1,0:T(8,128)(2,1)S(1)} collective-permute-done((bf16[256,512]{1,0:T(8,128)(2,1)S(1)}, bf16[256,512]{1,0:T(8,128)(2,1)S(1)}, u32[]{:S(2)}, u32[]{:S(2)}) %collective-permute-start.15) | collective-permute-done | bytes 262176 | tf_op jit(solution)/shard_map/weight_chip_1/ppermute | solution.py:43
  53.8 3.0 %collective-permute-done.16.refs_7_ = bf16[256,512]{1,0:T(8,128)(2,1)S(1)} collective-permute-done((bf16[256,512]{1,0:T(8,128)(2,1)S(1)}, bf16[256,512]{1,0:T(8,128)(2,1)S(1)}, u32[]{:S(2)}, u32[]{:S(2)}) %collective-permute-start.16) | collective-permute-done | bytes 262176 | tf_op jit(solution)/shard_map/weight_ring_across/ppermute | solution.py:55
  57.6 1.5 %more_values.1 = (f32[128,512]{1,0:T(8,128)S(1)}, f32[128,512]{1,0:T(8,128)S(1)}) custom-call(s32[10]{0:T(128)S(1)} %pad_add_fusion.me_ref, f32[256,512]{1,0:T(8,128)S(1)} %get-tuple-element.116.acc_ref, bf16[128,4096]{1,0:T(8,128)(2,1)S(1)} %get-tuple-element.93.mine_ref.x_mine_ref, bf16[128,4096]{1,0:T(8,128)(2,1)S(1)} %collective-permute-done.10.theirs_ref.x_theirs_ref, ...), custom_call_target="tpu_custom_call" | custom-call | flops 1 | bytes 1 | tf_op jit(solution)/shard_map/more_values/pallas_call | solution.py:421
  59.2 2.8 %collective-permute-done.22 = bf16[16,4608]{1,0:T(8,128)(2,1)S(1)} collective-permute-done((bf16[16,4608]{1,0:T(8,128)(2,1)S(1)}, bf16[16,4608]{1,0:T(8,128)(2,1)S(1)}, u32[]{:S(2)}, u32[]{:S(2)}) %collective-permute-start.22) | collective-permute-done | bytes 147488 | tf_op jit(solution)/shard_map/adapter_sum/ppermute | solution.py:43
  64.3 3.3 %collective-permute-start.20 = (bf16[128,512]{1,0:T(8,128)(2,1)S(1)}, bf16[128,512]{1,0:T(8,128)(2,1)S(1)}, u32[]{:S(2)}, u32[]{:S(2)}) collective-permute-start(bf16[128,512]{1,0:T(8,128)(2,1)S(1)} %add_convert_fusion.4.refs_5_), channel_id=1, source_target_pairs={{0,8},{4,12},{8,16},{12,20},{16,24},{20,28},{1,9},{5,13},{9,17},{1... | collective-permute-start | bytes 393224 | tf_op jit(solution)/shard_map/value_halo/ppermute | solution.py:49
  67.7 3.6 %input_grad.1 = (bf16[128,8192]{1,0:T(8,128)(2,1)}, bf16[128,4096]{1,0:T(8,128)(2,1)S(1)}) custom-call(s32[10]{0:T(128)S(1)} %pad_add_fusion.me_ref, bf16[128,512]{1,0:T(8,128)(2,1)S(1)} %add_convert_fusion.5.mine_ref, bf16[128,512]{1,0:T(8,128)(2,1)S(1)} %collective-permute-done.13.theirs_ref, bf16[256,16]{1,0:T(8,128)(2,1)S(1)} %get-tuple-element.134.rank_ref, ...), custom_call_target="tpu_custom_call" | custom-call | flops 1 | bytes 1 | tf_op jit(solution)/shard_map/input_grad/pallas_call | solution.py:473
  71.4 2.3 %collective-permute-start.24 = (bf16[16,4608]{1,0:T(8,128)(2,1)S(1)}, bf16[16,4608]{1,0:T(8,128)(2,1)S(1)}, u32[]{:S(2)}, u32[]{:S(2)}) collective-permute-start(bf16[16,4608]{1,0:T(8,128)(2,1)S(1)} %add_convert_fusion), channel_id=1, source_target_pairs={{0,8},{4,12},{8,0},{12,4},{16,24},{20,28},{24,16},{28,20},{1,9},{5... | collective-permute-start | bytes 442376 | tf_op jit(solution)/shard_map/adapter_sum/ppermute | solution.py:43
  73.6 4.0 %scores_grad.1 = (bf16[128,4096]{1,0:T(8,128)(2,1)}, bf16[128,512]{1,0:T(8,128)(2,1)S(1)}, bf16[128,512]{1,0:T(8,128)(2,1)S(1)}, f32[128,512]{1,0:T(8,128)S(1)}) custom-call(bf16[4,256,1024]{2,1,0:T(8,128)(2,1)S(1)} %get-tuple-element.138.p_ref, bf16[128,4096]{1,0:T(8,128)(2,1)S(1)} %bitcast.12, bf16[128,4096]{1,0:T(8,128)(2,1)S(1)} %bitcast.14, ...), custom_call_target="tpu_custom_call" | custom-call | flops 1 | bytes 1 | tf_op jit(solution)/shard_map/scores_grad/pallas_call | solution.py:224
  81.0 1.4 %join_adapter.1 = (f32[16,8192]{1,0:T(8,128)}, f32[16,512]{1,0:T(8,128)}) custom-call(s32[10]{0:T(128)S(1)} %pad_add_fusion.me_ref, f32[16,4608]{1,0:T(8,128)S(1)} %convert_add_fusion.mine_ref, f32[16,4608]{1,0:T(8,128)S(1)} %collective-permute-done.28.theirs_ref), custom_call_target="tpu_custom_call" | custom-call | flops 1 | bytes 1 | tf_op jit(solution)/shard_map/join_adapter/pallas_call | solution.py:312
  82.4 1.5 %put_half.1 = bf16[128,8192]{1,0:T(8,128)(2,1)} custom-call(s32[10]{0:T(128)S(1)} %pad_add_fusion.me_ref, bf16[128,4096]{1,0:T(8,128)(2,1)S(1)} %collective-permute-done.27.theirs_ref, bf16[128,8192]{1,0:T(8,128)(2,1)} %get-tuple-element.148.out_in), custom_call_target="tpu_custom_call", output_to_operand_aliasing={{}: (2, {})} | custom-call | flops 1 | bytes 1 | tf_op jit(solution)/shard_map/put_half/pallas_call | solution.py:286
  83.9 4.8 %collective-permute-done.26 = bf16[128,512]{1,0:T(8,128)(2,1)S(1)} collective-permute-done((bf16[128,512]{1,0:T(8,128)(2,1)S(1)}, bf16[128,512]{1,0:T(8,128)(2,1)S(1)}, u32[]{:S(2)}, u32[]{:S(2)}) %collective-permute-start.26) | collective-permute-done | bytes 131104 | tf_op jit(solution)/shard_map/key_grad_halo/ppermute | solution.py:49
  (66 shorter events, 20.4 us)
Async XLA Ops:
  1.9 17.6 %collective-permute-start.1 = (bf16[256,512]{1,0:T(8,128)(2,1)S(1)}, bf16[256,512]{1,0:T(8,128)(2,1)S(1)}, u32[]{:S(2)}, u32[]{:S(2)}) collective-permute-start(bf16[256,512]{1,0:T(8,128)(2,1)S(1)} %get-tuple-element.160), channel_id=1, source_target_pairs={{0,3},{1,0},{2,1},{3,2},{4,7},{5,4},{6,5},{7,6},{8,11},{9,8},{10,9... | collective-permute-start | bytes 786440 | tf_op jit(solution)/shard_map/weight_ring/ppermute | solution.py:55
  7.0 12.5 %collective-permute-start = (bf16[256,512]{1,0:T(8,128)(2,1)S(1)}, bf16[256,512]{1,0:T(8,128)(2,1)S(1)}, u32[]{:S(2)}, u32[]{:S(2)}) collective-permute-start(bf16[256,512]{1,0:T(8,128)(2,1)S(1)} %get-tuple-element.160), channel_id=1, source_target_pairs={{0,1},{1,2},{2,3},{3,0},{4,5},{5,6},{6,7},{7,4},{8,9},{9,10},{10,1... | collective-permute-start | bytes 786440 | tf_op jit(solution)/shard_map/weight_ring/ppermute | solution.py:55
  7.0 9.6 %collective-permute-start.3 = (bf16[128,512]{1,0:T(8,128)(2,1)}, bf16[128,512]{1,0:T(8,128)(2,1)S(1)}, u32[]{:S(2)}, u32[]{:S(2)}) collective-permute-start(bf16[128,512]{1,0:T(8,128)(2,1)} %bitcast.16), channel_id=1, source_target_pairs={{0,4},{4,8},{8,12},{12,16},{16,20},{20,24},{24,28},{1,5},{5,9},{9,... | collective-permute-start | bytes 393224 | tf_op jit(solution)/shard_map/key_halo/ppermute | solution.py:49
  8.5 8.1 %collective-permute-start.2 = (bf16[128,512]{1,0:T(8,128)(2,1)}, bf16[128,512]{1,0:T(8,128)(2,1)S(1)}, u32[]{:S(2)}, u32[]{:S(2)}) collective-permute-start(bf16[128,512]{1,0:T(8,128)(2,1)} %bitcast.17), channel_id=1, source_target_pairs={{0,8},{4,12},{8,16},{12,20},{16,24},{20,28},{1,9},{5,13},{9,17},{1... | collective-permute-start | bytes 393224 | tf_op jit(solution)/shard_map/key_halo/ppermute | solution.py:49
  19.5 5.5 %collective-permute-start.10 = (bf16[128,4096]{1,0:T(8,128)(2,1)S(1)}, bf16[128,4096]{1,0:T(8,128)(2,1)S(1)}, u32[]{:S(2)}, u32[]{:S(2)}) collective-permute-start(bf16[128,4096]{1,0:T(8,128)(2,1)S(1)} %get-tuple-element.94), channel_id=1, source_target_pairs={{0,4},{4,0},{8,12},{12,8},{16,20},{20,16},{24,28},{28,24},{1,5},{5... | collective-permute-start | bytes 3145736 | tf_op jit(solution)/shard_map/x_core/ppermute | solution.py:43
  20.9 14.9 %collective-permute-start.7 = (bf16[256,512]{1,0:T(8,128)(2,1)S(1)}, bf16[256,512]{1,0:T(8,128)(2,1)S(1)}, u32[]{:S(2)}, u32[]{:S(2)}) collective-permute-start(bf16[256,512]{1,0:T(8,128)(2,1)S(1)} %collective-permute-done.refs_0_), channel_id=1, source_target_pairs={{0,1},{1,2},{2,3},{3,0},{4,5},{5,6},{6,7},{7,4},{8,9},{9,10},{10,1... | collective-permute-start | bytes 786440 | tf_op jit(solution)/shard_map/weight_ring/ppermute | solution.py:55
  20.9 16.0 %collective-permute-start.6 = (bf16[256,512]{1,0:T(8,128)(2,1)S(1)}, bf16[256,512]{1,0:T(8,128)(2,1)S(1)}, u32[]{:S(2)}, u32[]{:S(2)}) collective-permute-start(bf16[256,512]{1,0:T(8,128)(2,1)S(1)} %collective-permute-done.refs_0_), channel_id=1, source_target_pairs={{0,16},{4,12},{8,24},{12,4},{16,0},{20,28},{24,8},{28,20},{1,17},{... | collective-permute-start | bytes 786440 | tf_op jit(solution)/shard_map/weight_chip_1/ppermute | solution.py:43
  22.9 13.9 %collective-permute-start.5 = (bf16[256,512]{1,0:T(8,128)(2,1)S(1)}, bf16[256,512]{1,0:T(8,128)(2,1)S(1)}, u32[]{:S(2)}, u32[]{:S(2)}) collective-permute-start(bf16[256,512]{1,0:T(8,128)(2,1)S(1)} %collective-permute-done.refs_0_), channel_id=1, source_target_pairs={{0,8},{4,20},{8,0},{12,28},{16,24},{20,4},{24,16},{28,12},{1,9},{5... | collective-permute-start | bytes 786440 | tf_op jit(solution)/shard_map/weight_chip_0/ppermute | solution.py:43
  23.7 5.7 %collective-permute-start.8 = (bf16[128,512]{1,0:T(8,128)(2,1)S(1)}, bf16[128,512]{1,0:T(8,128)(2,1)S(1)}, u32[]{:S(2)}, u32[]{:S(2)}) collective-permute-start(bf16[128,512]{1,0:T(8,128)(2,1)S(1)} %get-tuple-element.91), channel_id=1, source_target_pairs={{4,0},{8,4},{12,8},{16,12},{20,16},{24,20},{28,24},{5,1},{9,5},{13... | collective-permute-start | bytes 393224 | tf_op jit(solution)/shard_map/value_grad_halo/ppermute | solution.py:49
  25.0 8.5 %collective-permute-start.9 = (bf16[128,512]{1,0:T(8,128)(2,1)S(1)}, bf16[128,512]{1,0:T(8,128)(2,1)S(1)}, u32[]{:S(2)}, u32[]{:S(2)}) collective-permute-start(bf16[128,512]{1,0:T(8,128)(2,1)S(1)} %get-tuple-element.92), channel_id=1, source_target_pairs={{8,0},{12,4},{16,8},{20,12},{24,16},{28,20},{9,1},{13,5},{17,9},{2... | collective-permute-start | bytes 393224 | tf_op jit(solution)/shard_map/value_grad_halo/ppermute | solution.py:49
  29.4 14.9 %collective-permute-start.12 = (bf16[256,512]{1,0:T(8,128)(2,1)S(1)}, bf16[256,512]{1,0:T(8,128)(2,1)S(1)}, u32[]{:S(2)}, u32[]{:S(2)}) collective-permute-start(bf16[256,512]{1,0:T(8,128)(2,1)S(1)} %collective-permute-done.1.refs_8_), channel_id=1, source_target_pairs={{0,16},{4,12},{8,24},{12,4},{16,0},{20,28},{24,8},{28,20},{1,17},{... | collective-permute-start | bytes 786440 | tf_op jit(solution)/shard_map/weight_chip_1/ppermute | solution.py:43
  33.5 10.8 %collective-permute-start.11 = (bf16[256,512]{1,0:T(8,128)(2,1)S(1)}, bf16[256,512]{1,0:T(8,128)(2,1)S(1)}, u32[]{:S(2)}, u32[]{:S(2)}) collective-permute-start(bf16[256,512]{1,0:T(8,128)(2,1)S(1)} %collective-permute-done.1.refs_8_), channel_id=1, source_target_pairs={{0,8},{4,20},{8,0},{12,28},{16,24},{20,4},{24,16},{28,12},{1,9},{5... | collective-permute-start | bytes 786440 | tf_op jit(solution)/shard_map/weight_chip_0/ppermute | solution.py:43
  35.8 8.5 %collective-permute-start.4 = (bf16[256,512]{1,0:T(8,128)(2,1)S(1)}, bf16[256,512]{1,0:T(8,128)(2,1)S(1)}, u32[]{:S(2)}, u32[]{:S(2)}) collective-permute-start(bf16[256,512]{1,0:T(8,128)(2,1)S(1)} %get-tuple-element.89), channel_id=1, source_target_pairs={{0,1},{1,2},{2,3},{3,0},{4,5},{5,6},{6,7},{7,4},{8,9},{9,10},{10,1... | collective-permute-start | bytes 786440 | tf_op jit(solution)/shard_map/weight_ring_across/ppermute | solution.py:55
  44.3 5.4 %collective-permute-start.18 = (bf16[16,4608]{1,0:T(8,128)(2,1)S(1)}, bf16[16,4608]{1,0:T(8,128)(2,1)S(1)}, u32[]{:S(2)}, u32[]{:S(2)}) collective-permute-start(bf16[16,4608]{1,0:T(8,128)(2,1)S(1)} %get-tuple-element.115), channel_id=1, source_target_pairs={{0,1},{1,0},{2,3},{3,2},{4,5},{5,4},{6,7},{7,6},{8,9},{9,8},{10,11... | collective-permute-start | bytes 442376 | tf_op jit(solution)/shard_map/adapter_sum/ppermute | solution.py:43
  44.7 7.9 %collective-permute-start.15 = (bf16[256,512]{1,0:T(8,128)(2,1)S(1)}, bf16[256,512]{1,0:T(8,128)(2,1)S(1)}, u32[]{:S(2)}, u32[]{:S(2)}) collective-permute-start(bf16[256,512]{1,0:T(8,128)(2,1)S(1)} %collective-permute-done.7.refs_4_), channel_id=1, source_target_pairs={{0,16},{4,12},{8,24},{12,4},{16,0},{20,28},{24,8},{28,20},{1,17},{... | collective-permute-start | bytes 786440 | tf_op jit(solution)/shard_map/weight_chip_1/ppermute | solution.py:43
  45.5 8.3 %collective-permute-start.14 = (bf16[256,512]{1,0:T(8,128)(2,1)S(1)}, bf16[256,512]{1,0:T(8,128)(2,1)S(1)}, u32[]{:S(2)}, u32[]{:S(2)}) collective-permute-start(bf16[256,512]{1,0:T(8,128)(2,1)S(1)} %collective-permute-done.7.refs_4_), channel_id=1, source_target_pairs={{0,8},{4,20},{8,0},{12,28},{16,24},{20,4},{24,16},{28,12},{1,9},{5... | collective-permute-start | bytes 786440 | tf_op jit(solution)/shard_map/weight_chip_0/ppermute | solution.py:43
  47.5 9.4 %collective-permute-start.16 = (bf16[256,512]{1,0:T(8,128)(2,1)S(1)}, bf16[256,512]{1,0:T(8,128)(2,1)S(1)}, u32[]{:S(2)}, u32[]{:S(2)}) collective-permute-start(bf16[256,512]{1,0:T(8,128)(2,1)S(1)} %collective-permute-done.4.refs_3_), channel_id=1, source_target_pairs={{0,1},{1,2},{2,3},{3,0},{4,5},{5,6},{6,7},{7,4},{8,9},{9,10},{10,1... | collective-permute-start | bytes 786440 | tf_op jit(solution)/shard_map/weight_ring_across/ppermute | solution.py:55
  49.4 7.4 %collective-permute-start.17 = (bf16[256,512]{1,0:T(8,128)(2,1)S(1)}, bf16[256,512]{1,0:T(8,128)(2,1)S(1)}, u32[]{:S(2)}, u32[]{:S(2)}) collective-permute-start(bf16[256,512]{1,0:T(8,128)(2,1)S(1)} %collective-permute-done.11.refs_9_), channel_id=1, source_target_pairs={{0,16},{4,12},{8,24},{12,4},{16,0},{20,28},{24,8},{28,20},{1,17},{... | collective-permute-start | bytes 786440 | tf_op jit(solution)/shard_map/weight_chip_1/ppermute | solution.py:43
  62.0 9.3 %collective-permute-start.23 = (bf16[16,4608]{1,0:T(8,128)(2,1)S(1)}, bf16[16,4608]{1,0:T(8,128)(2,1)S(1)}, u32[]{:S(2)}, u32[]{:S(2)}) collective-permute-start(bf16[16,4608]{1,0:T(8,128)(2,1)S(1)} %add_convert_fusion.1), channel_id=1, source_target_pairs={{0,2},{1,3},{2,0},{3,1},{4,6},{5,7},{6,4},{7,5},{8,10},{9,11},{10,... | collective-permute-start | bytes 442376 | tf_op jit(solution)/shard_map/adapter_sum/ppermute | solution.py:43
  63.0 8.3 %collective-permute-start.21 = (bf16[128,512]{1,0:T(8,128)(2,1)S(1)}, bf16[128,512]{1,0:T(8,128)(2,1)S(1)}, u32[]{:S(2)}, u32[]{:S(2)}) collective-permute-start(bf16[128,512]{1,0:T(8,128)(2,1)S(1)} %add_convert_fusion.4.refs_5_), channel_id=1, source_target_pairs={{0,4},{4,8},{8,12},{12,16},{16,20},{20,24},{24,28},{1,5},{5,9},{9,... | collective-permute-start | bytes 393224 | tf_op jit(solution)/shard_map/value_halo/ppermute | solution.py:49
  64.3 7.0 %collective-permute-start.20 = (bf16[128,512]{1,0:T(8,128)(2,1)S(1)}, bf16[128,512]{1,0:T(8,128)(2,1)S(1)}, u32[]{:S(2)}, u32[]{:S(2)}) collective-permute-start(bf16[128,512]{1,0:T(8,128)(2,1)S(1)} %add_convert_fusion.4.refs_5_), channel_id=1, source_target_pairs={{0,8},{4,12},{8,16},{12,20},{16,24},{20,28},{1,9},{5,13},{9,17},{1... | collective-permute-start | bytes 393224 | tf_op jit(solution)/shard_map/value_halo/ppermute | solution.py:49
  71.4 6.3 %collective-permute-start.24 = (bf16[16,4608]{1,0:T(8,128)(2,1)S(1)}, bf16[16,4608]{1,0:T(8,128)(2,1)S(1)}, u32[]{:S(2)}, u32[]{:S(2)}) collective-permute-start(bf16[16,4608]{1,0:T(8,128)(2,1)S(1)} %add_convert_fusion), channel_id=1, source_target_pairs={{0,8},{4,12},{8,0},{12,4},{16,24},{20,28},{24,16},{28,20},{1,9},{5... | collective-permute-start | bytes 442376 | tf_op jit(solution)/shard_map/adapter_sum/ppermute | solution.py:43
  78.4 5.6 %collective-permute-start.25 = (bf16[128,512]{1,0:T(8,128)(2,1)S(1)}, bf16[128,512]{1,0:T(8,128)(2,1)S(1)}, u32[]{:S(2)}, u32[]{:S(2)}) collective-permute-start(bf16[128,512]{1,0:T(8,128)(2,1)S(1)} %get-tuple-element.145), channel_id=1, source_target_pairs={{4,0},{8,4},{12,8},{16,12},{20,16},{24,20},{28,24},{5,1},{9,5},{13... | collective-permute-start | bytes 393224 | tf_op jit(solution)/shard_map/key_grad_halo/ppermute | solution.py:49
  79.7 9.1 %collective-permute-start.26 = (bf16[128,512]{1,0:T(8,128)(2,1)S(1)}, bf16[128,512]{1,0:T(8,128)(2,1)S(1)}, u32[]{:S(2)}, u32[]{:S(2)}) collective-permute-start(bf16[128,512]{1,0:T(8,128)(2,1)S(1)} %get-tuple-element.146), channel_id=1, source_target_pairs={{8,0},{12,4},{16,8},{20,12},{24,16},{28,20},{9,1},{13,5},{17,9},{2... | collective-permute-start | bytes 393224 | tf_op jit(solution)/shard_map/key_grad_halo/ppermute | solution.py:49
  (12 other events, 84.4 us)
